TPU v7x, 32 devices: a whole 2x2x4 slice. The times are simulated.
32 devices in a mesh: dp: 16 (over z, y, x), mp: 2 (over core).
Axes of the slice: x: 2, y: 2, z: 4, core: 2. Of those that a mesh axis runs over, the one named last changes fastest.
Arguments:
- tokens: bfloat16 [16384, 768], P('dp'), may hold values from -6 to 6
- masked: int32 [16384], P('dp'), may hold values 0 or 1
- lengths: int32 [128], P('dp'), may hold values from 66 to 128, as said below
- mask_vector: bfloat16 [768], replicated, may hold values from -6 to 6
- w_query: bfloat16 [768, 768], P('dp', 'mp'), may hold values from -0.21875 to 0.21875
- b_query: bfloat16 [768], P('mp'), may hold values from -3 to 3
- w_key: bfloat16 [768, 768], P('dp', 'mp'), may hold values from -0.21875 to 0.21875
- w_value: bfloat16 [768, 768], P('dp', 'mp'), may hold values from -0.21875 to 0.21875
- b_value: bfloat16 [768], P('mp'), may hold values from -3 to 3
- w_out: bfloat16 [768, 768], P('mp', 'dp'), may hold values from -1.25 to 1.25
- b_out: bfloat16 [768], replicated, may hold values from -3 to 3
- gain_one: bfloat16 [768], replicated, may hold values from 0.099609375 to 1.8984375
- shift_one: bfloat16 [768], replicated, may hold values from -2 to 2
- w_up: bfloat16 [768, 3072], P('dp', 'mp'), may hold values from -0.21875 to 0.21875
- b_up: bfloat16 [3072], P('mp'), may hold values from -3 to 3
- w_down: bfloat16 [3072, 768], P('mp', 'dp'), may hold values from -0.109375 to 0.109375
- b_down: bfloat16 [768], replicated, may hold values from -3 to 3
- gain_two: bfloat16 [768], replicated, may hold values from 0.099609375 to 1.8984375
- shift_two: bfloat16 [768], replicated, may hold values from -2 to 2
- grad_out: bfloat16 [16384, 768], P('dp'), may hold values from -6 to 6
Outputs:
- out: bfloat16 [16384, 768], P('dp')
- d_tokens: float32 [16384, 768], P('dp')
- d_mask_vector: float32 [768], replicated
- d_w_query: float32 [768, 768], P('dp', 'mp')
- d_b_query: float32 [768], P('mp')
- d_w_key: float32 [768, 768], P('dp', 'mp')
- d_w_value: float32 [768, 768], P('dp', 'mp')
- d_b_value: float32 [768], P('mp')
- d_w_out: float32 [768, 768], P('mp', 'dp')
- d_b_out: float32 [768], replicated
- d_gain_one: float32 [768], replicated
- d_shift_one: float32 [768], replicated
- d_w_up: float32 [768, 3072], P('dp', 'mp')
- d_b_up: float32 [3072], P('mp')
- d_w_down: float32 [3072, 768], P('mp', 'dp')
- d_b_down: float32 [768], replicated
- d_gain_two: float32 [768], replicated
- d_shift_two: float32 [768], replicated
Inputs may be any that keep to these rules, and one draw needn't show every extreme that they name: `lengths`: the first chain of each aligned block of 8 chains uses all 128 slots; the others lose up to 62 slots, small losses more often than large ones.
All inputs are finite; a program needn't handle non-finite values. No bound on the sum of `masked` on one device may be relied on, other than what follows from the above.
Results may differ from a plain program's by a relative error of at most 0.018.
Values may be sent and summed in bfloat16 or wider, within the bound.
No kernel may reach another device: no remote copies, remote signals or barrier semaphores. Data moves between devices by JAX's collectives and lax.ppermute only.
A program may use at most 128 MiB of HBM per device.

v0:
```python
import functools

import jax
import jax.numpy as jnp
from jax import lax
from jax.experimental import pallas as pl
from jax.experimental.pallas import tpu as pltpu
from jax.sharding import PartitionSpec as P

HEAD = 64
NORM_EPS = 1e-05
F32 = jnp.float32
B16 = jnp.bfloat16
MIB = 1 << 20

BLOCKS = 16
NEAR = (0, 12)
MID = (4, 8)


def swap(values, bit):
    return lax.ppermute(values, "dp", [(i, i ^ bit) for i in range(BLOCKS)])


def tie(*values):
    return lax.optimization_barrier(values)


def after(value, *earlier):
    return tie(value, *earlier)[0]


def pair_swap(partial):
    return lax.ppermute(partial, "mp", [(0, 1), (1, 0)])


def as_pieces(full):
    rows = full.shape[0] // BLOCKS
    blocks = full.reshape(BLOCKS, rows, full.shape[1])
    return [
        jnp.stack([blocks[offset + bits[0]], blocks[offset + bits[1]]])
        for offset in range(4)
        for bits in (NEAR, MID)
    ]


SMEM_SPEC = pl.BlockSpec(memory_space=pltpu.SMEM)
VMEM_SPEC = pl.BlockSpec(memory_space=pltpu.VMEM)
CHUNK = 256
UNROLL = 8
LIGHT = pl.CostEstimate(flops=1, bytes_accessed=1, transcendentals=0)


def call(body, name, shapes, operands, scratch=(), limit=16):
    return pl.pallas_call(
        body,
        in_specs=[
            SMEM_SPEC if member.dtype == jnp.int32 and member.ndim == 1 else VMEM_SPEC
            for member in operands
        ],
        out_specs=[VMEM_SPEC] * len(shapes),
        out_shape=[jax.ShapeDtypeStruct(shape, dtype) for shape, dtype in shapes],
        scratch_shapes=[pltpu.VMEM(shape, dtype) for shape, dtype in scratch],
        compiler_params=pltpu.CompilerParams(vmem_limit_bytes=limit * MIB),
        cost_estimate=LIGHT,
        name=name,
    )(*operands)


def chunks(count):
    return [slice(start, start + CHUNK) for start in range(0, count, CHUNK)]


def loop(count, step, size=CHUNK):
    def body(index, carry):
        step(pl.ds(pl.multiple_of(index * size, size), size))
        return carry

    lax.fori_loop(0, count // size, body, 0)


PAIRS = [(q + bits[k], 2 * q + m, k) for q in range(4) for m, bits in enumerate((NEAR, MID)) for k in range(2)]


def fill(me, pieces, full_ref):
    rows = pieces[0].shape[1]
    for offset, piece, index in PAIRS:
        block = me ^ offset
        full_ref[pl.ds(pl.multiple_of(block * rows, rows), rows), :] = pieces[piece][index]


def dot(left, right):
    return jnp.dot(left, right, preferred_element_type=F32)


def dot_t(left, right):
    return lax.dot_general(left, right, (((1,), (1,)), ((), ())), preferred_element_type=F32)


def t_dot(left, right):
    return lax.dot_general(left, right, (((0,), (0,)), ((), ())), preferred_element_type=F32)


def row_mean(values):
    return jnp.mean(values, axis=-1, keepdims=True)


def normalize(values):
    centred = values - row_mean(values)
    inverse = lax.rsqrt(row_mean(centred * centred) + NORM_EPS)
    return centred * inverse, inverse


def col_sum(values):
    return jnp.sum(values, axis=0, keepdims=True)


def norm_back(scaled, normed, inverse):
    return inverse * (scaled - row_mean(scaled) - normed * row_mean(scaled * normed))


def two_heads(slots):
    row = lax.broadcasted_iota(jnp.int32, (2 * slots, 2 * HEAD), 0) // slots
    lane = lax.broadcasted_iota(jnp.int32, (2 * slots, 2 * HEAD), 1) // HEAD
    return (row == lane).astype(F32).astype(B16)


def doubled(values, mask):
    return jnp.concatenate([values, values], axis=0) * mask


def attend_body(slots, me_ref, len_ref, in_ref, bias_ref, *rest):
    pieces, (w_ref, qkv_ref, prob_ref, att_ref, part_ref) = rest[:-5], rest[-5:]
    count, width = att_ref.shape
    fill(me_ref[0], pieces, w_ref)

    def project(rows):
        qkv_ref[rows] = (dot(in_ref[rows], w_ref[:, : 3 * width]) + bias_ref[...]).astype(B16)

    loop(count, project)
    mask = two_heads(slots)
    key_slot = lax.broadcasted_iota(jnp.int32, (slots, slots), 1)

    def chain_step(chain, carry):
        valid = key_slot < len_ref[chain]
        rows = pl.ds(pl.multiple_of(chain * slots, slots), slots)
        for pair in range(width // (2 * HEAD)):
            lanes = 2 * HEAD * pair
            query = qkv_ref[rows, lanes : lanes + 2 * HEAD]
            key = qkv_ref[rows, width + lanes : width + lanes + 2 * HEAD]
            value = qkv_ref[rows, 2 * width + lanes : 2 * width + lanes + 2 * HEAD]
            scores = dot_t(query * (HEAD**-0.5), doubled(key, mask))
            probs = []
            for head in range(2):
                part = jnp.where(valid, scores[:, head * slots : (head + 1) * slots], -1e30)
                terms = jnp.exp(part - jnp.max(part, axis=-1, keepdims=True))
                probs.append((terms / jnp.sum(terms, axis=-1, keepdims=True)).astype(B16))
            prob = jnp.concatenate(probs, axis=1)
            prob_ref[rows, 2 * slots * pair : 2 * slots * (pair + 1)] = prob
            att_ref[rows, lanes : lanes + 2 * HEAD] = dot(prob, doubled(value, mask)).astype(B16)
        return carry

    lax.fori_loop(0, count // slots, chain_step, 0, unroll=UNROLL)

    def bring_out(rows):
        part_ref[rows] = dot_t(att_ref[rows], w_ref[:, 3 * width :]).astype(B16)

    loop(count, bring_out)


def attend(me, lengths, in_low, bias, pieces):
    count, width = in_low.shape
    heads = bias.shape[1] // 3
    slots = count // lengths.shape[0]
    shapes = [
        ((width, 4 * heads), B16),
        ((count, 3 * heads), B16),
        ((count, heads // HEAD * slots), B16),
        ((count, heads), B16),
        ((count, width), B16),
    ]
    body = functools.partial(attend_body, slots)
    return call(body, "attend", shapes, [me, lengths, in_low, bias, *pieces])


def up_body(me_ref, in_ref, own_ref, other_ref, vec_ref, bias_ref, *rest):
    pieces, (w_ref, normed_ref, inverse_ref, low_ref, act_ref, slope_ref) = rest[:-6], rest[-6:]
    fill(me_ref[0], pieces, w_ref)
    vectors = vec_ref[...]

    def step(rows):
        attn = own_ref[rows].astype(F32) + other_ref[rows].astype(F32) + vectors[0:1]
        normed, inverse = normalize(in_ref[rows].astype(F32) + attn)
        normed_ref[rows] = normed
        inverse_ref[rows] = jnp.broadcast_to(inverse, (CHUNK, inverse_ref.shape[1]))
        low_ref[rows] = (normed * vectors[1:2] + vectors[2:3]).astype(B16)
        pre = dot(low_ref[rows], w_ref[...]) + bias_ref[...]
        cdf = 0.5 + 0.5 * lax.erf(pre * (2.0**-0.5))
        act_ref[rows] = (pre * cdf).astype(B16)
        density = jnp.exp(pre * pre * -0.5) * 0.3989422804014327
        slope_ref[rows] = (cdf + pre * density).astype(B16)

    loop(in_ref.shape[0], step)


def up(me, in_low, own, other, vectors, bias, pieces):
    count, width = in_low.shape
    units = bias.shape[1]
    shapes = [
        ((width, units), B16),
        ((count, width), F32),
        ((count, 128), F32),
        ((count, width), B16),
        ((count, units), B16),
        ((count, units), B16),
    ]
    return call(up_body, "up", shapes, [me, in_low, own, other, vectors, bias, *pieces])


def down_body(me_ref, act_ref, *rest):
    pieces, (w_ref, part_ref) = rest[:-2], rest[-2:]
    fill(me_ref[0], pieces, w_ref)
    for rows in chunks(part_ref.shape[0]):
        part_ref[rows] = dot_t(act_ref[rows], w_ref[...]).astype(B16)


def down_rest_body(act_ref, w_ref, part_ref):
    half = part_ref.shape[0]
    for rows in chunks(half):
        part_ref[rows] = dot_t(act_ref[half + rows.start : half + rows.stop], w_ref[...]).astype(B16)


def down(me, act, pieces):
    count, units = act.shape
    width = BLOCKS * pieces[0].shape[1]
    half = ((count // 2, width), B16)
    w_down_t, first = call(down_body, "down", [((width, units), B16), half], [me, act, *pieces])
    (second,) = call(down_rest_body, "down_rest", [half], [act, w_down_t])
    return w_down_t, first, second


def second_norm_body(start, normed_ref, own_ref, other_ref, grad_ref, vec_ref, out_ref, dz_ref, low_ref, sum_ref):
    vectors = vec_ref[...]
    sum_ref[...] = jnp.zeros_like(sum_ref)
    for rows in chunks(own_ref.shape[0]):
        there = slice(start + rows.start, start + rows.stop)
        hidden = normed_ref[there] * vectors[0:1] + vectors[1:2]
        ffn = own_ref[rows].astype(F32) + other_ref[rows].astype(F32) + vectors[2:3]
        normed, inverse = normalize(hidden + ffn)
        out_ref[rows] = (normed * vectors[3:4] + vectors[4:5]).astype(B16)
        grad = grad_ref[there].astype(F32)
        dz = norm_back(grad * vectors[3:4], normed, inverse)
        dz_ref[rows] = dz
        low_ref[rows] = dz.astype(B16)
        sum_ref[0:1] += col_sum(grad * normed)
        sum_ref[1:2] += col_sum(grad)
        sum_ref[2:3] += col_sum(dz)


def second_norm(start, normed, own, other, grad, vectors):
    shape = own.shape
    shapes = [(shape, B16), (shape, F32), (shape, B16), ((8, shape[1]), F32)]
    body = functools.partial(second_norm_body, start)
    return call(body, "second_norm", shapes, [normed, own, other, grad, vectors])


def rows_in(halves, rows):
    size = halves[0].shape[0]
    half = halves[rows.start // size]
    return half[rows.start % size : rows.start % size + rows.stop - rows.start]


ORDER = (
    (3, 15, 1, 13),
    (7, 11, 6, 10),
    (5, 9),
    (2, 14),
    (0, 12, 4, 8),
)


def weight_grad(me, lefts, rights, groups=ORDER, vector=None, turned=None):
    count = rights[0].shape[0]
    width = lefts[-1][0].shape[1] if turned is None else turned.shape[0]
    tile = 384 if all(right.shape[1] % 384 == 0 for right in rights) else 128
    total = sum(right.shape[1] for right in rights)
    rows = width // BLOCKS
    n = len(rights)
    flat = [half for left in lefts for half in left] if turned is None else [turned]
    wide = [] if vector is None else [vector]
    keep = turned is None and len(groups) < len(ORDER)
    wanted = [offset for offsets in groups for offset in offsets]

    def body(me_ref, *refs):
        left_refs, right_refs = list(refs[: len(flat)]), refs[len(flat) : len(flat) + n]
        outs = refs[len(flat) + n + len(wide) :]
        placed_ref = outs[-1]
        if wide:
            outs[0][0:2, :, total:] = refs[len(flat) + n][...]
            outs[0][2:4, :, total:] = jnp.zeros((2, rows, 128), B16)
        at = 0
        for index, right_ref in enumerate(right_refs):
            turned_ref = left_refs[0] if turned is not None else outs[-2]
            if turned is None:
                start = 0
                for _ in lefts[index]:
                    half_ref = left_refs.pop(0)
                    turned_ref[:, start : start + half_ref.shape[0]] = half_ref[...].T
                    start += half_ref.shape[0]
            for k, offset in enumerate(wanted):
                place = pl.multiple_of((me_ref[0] ^ offset) * rows, rows)
                placed_ref[k * rows : (k + 1) * rows] = turned_ref[pl.ds(place, rows), :]

            def step(cols, right_ref=right_ref, at=at):
                product = dot(placed_ref[...], right_ref[:, cols]).astype(B16)
                there = pl.ds(pl.multiple_of(at + cols.start, 128), tile)
                first = 0
                for out_ref, offsets in zip(outs, groups):
                    for k in range(len(offsets)):
                        out_ref[k, :, there] = product[first : first + rows]
                        first += rows

            loop(right_ref.shape[1], step, tile)
            at += right_ref.shape[1]

    shapes = [((len(offsets), rows, total), B16) for offsets in groups]
    shapes[0] = ((len(groups[0]), rows, total + 128 * len(wide)), B16)
    held = ((width, count), B16)
    shapes += [held] * keep
    scratch = [held] * (turned is None and not keep) + [((len(wanted) * rows, count), B16)]
    return call(body, "weight_grad", shapes, [me, *flat, *rights, *wide], scratch)


def hidden_back_body(low_a_ref, low_b_ref, slope_ref, down_ref, up_ref, pre_ref, part_ref, sum_ref):
    sum_ref[...] = jnp.zeros_like(sum_ref)
    half = low_a_ref.shape[0]
    for start, low_ref in ((0, low_a_ref), (half, low_b_ref)):

        def step(here, start=start, low_ref=low_ref):
            rows = pl.ds(pl.multiple_of(start + here.start, CHUNK), CHUNK)
            d_pre = dot(low_ref[here], down_ref[...]) * slope_ref[rows].astype(F32)
            sum_ref[0:1] += col_sum(d_pre)
            pre_ref[rows] = d_pre.astype(B16)
            part_ref[rows] = dot_t(pre_ref[rows], up_ref[...]).astype(B16)

        loop(half, step)


def hidden_back(lows, slope, w_down_t, w_up):
    count, units = slope.shape
    shapes = [((count, units), B16), ((count, w_up.shape[0]), B16), ((8, units), F32)]
    return call(hidden_back_body, "hidden_back", shapes, [*lows, slope, w_down_t, w_up])


def attend_back_body(slots, dz_a_ref, dz_b_ref, own_ref, other_ref, normed_ref, inverse_ref, gain_ref,
                     flag_ref, qkv_ref, prob_ref, w_ref, dz_one_ref, low_ref, d_qkv_ref, part_ref, sum_ref,
                     sum_qkv_ref, d_att_ref):
    count, width = d_att_ref.shape
    sum_ref[...] = jnp.zeros_like(sum_ref)
    sum_qkv_ref[...] = jnp.zeros_like(sum_qkv_ref)
    half = dz_a_ref.shape[0]
    for start, dz_ref in ((0, dz_a_ref), (half, dz_b_ref)):

        def step(here, start=start, dz_ref=dz_ref):
            rows = pl.ds(pl.multiple_of(start + here.start, CHUNK), CHUNK)
            normed = normed_ref[rows]
            d_hidden = dz_ref[here] + (own_ref[rows].astype(F32) + other_ref[rows].astype(F32))
            dz_one = norm_back(d_hidden * gain_ref[...], normed, inverse_ref[rows, 0:1])
            dz_one_ref[rows] = dz_one
            low_ref[rows] = dz_one.astype(B16)
            sum_ref[0:1] += col_sum(d_hidden * normed)
            sum_ref[1:2] += col_sum(d_hidden)
            sum_ref[2:3] += col_sum(dz_one)
            sum_ref[3:4] += col_sum(dz_one * flag_ref[rows, 0:1])
            d_att_ref[rows] = dot(low_ref[rows], w_ref[:, 3 * width :]).astype(B16)

        loop(half, step)
    mask = two_heads(slots)

    def chain_step(chain, carry):
        rows = pl.ds(pl.multiple_of(chain * slots, slots), slots)
        for pair in range(width // (2 * HEAD)):
            lanes = 2 * HEAD * pair
            query = qkv_ref[rows, lanes : lanes + 2 * HEAD]
            key = qkv_ref[rows, width + lanes : width + lanes + 2 * HEAD]
            value = qkv_ref[rows, 2 * width + lanes : 2 * width + lanes + 2 * HEAD]
            d_att = d_att_ref[rows, lanes : lanes + 2 * HEAD]
            prob = prob_ref[rows, 2 * slots * pair : 2 * slots * (pair + 1)]
            d_prob = dot_t(d_att, doubled(value, mask))
            weights = prob.astype(F32)
            products = weights * d_prob
            lows = []
            for head in range(2):
                half = slice(head * slots, (head + 1) * slots)
                total = jnp.sum(products[:, half], axis=-1, keepdims=True)
                lows.append((products[:, half] - weights[:, half] * total).astype(B16))
            low = jnp.concatenate(lows, axis=1)
            d_query = dot(low, doubled(key, mask)) * (HEAD**-0.5)
            tall = jnp.concatenate(lows, axis=0)
            d_key = t_dot(tall, doubled(query, mask)) * (HEAD**-0.5)
            tall = jnp.concatenate([prob[:, :slots], prob[:, slots:]], axis=0)
            d_value = t_dot(tall, doubled(d_att, mask))
            d_qkv_ref[rows, lanes : lanes + 2 * HEAD] = d_query.astype(B16)
            d_qkv_ref[rows, width + lanes : width + lanes + 2 * HEAD] = d_key.astype(B16)
            d_qkv_ref[rows, 2 * width + lanes : 2 * width + lanes + 2 * HEAD] = d_value.astype(B16)
        return carry

    lax.fori_loop(0, count // slots, chain_step, 0)

    def bring_back(rows):
        sum_qkv_ref[0:1] += col_sum(d_qkv_ref[rows].astype(F32))
        part = dot_t(d_qkv_ref[rows], w_ref[:, : 3 * width]).astype(B16)
        part_ref[rows] = part
        sum_ref[4:5] += col_sum(part.astype(F32) * flag_ref[rows, 0:1])

    loop(count, bring_back)


def attend_back(chain_count, dz_two, own, other, normed, inverse, gain, flag, qkv, prob, w_a):
    shape = normed.shape
    heads = qkv.shape[1] // 3
    shapes = [
        (shape, F32),
        (shape, B16),
        (qkv.shape, B16),
        (shape, B16),
        ((8, shape[1]), F32),
        ((8, 3 * heads), F32),
    ]
    operands = [*dz_two, own, other, normed, inverse, gain, flag, qkv, prob, w_a]
    body = functools.partial(attend_back_body, shape[0] // chain_count)
    return call(body, "attend_back", shapes, operands, [((shape[0], heads), B16)])


def join_body(one_ref, other_ref, two_a_ref, two_b_ref, up_ref, qkv_ref, out_ref):
    width = one_ref.shape[1]
    heads = qkv_ref.shape[1] // 3
    rows = out_ref.shape[1]
    out_ref[...] = jnp.zeros_like(out_ref)

    def put(start, values):
        for k in range(values.shape[1] // 128):
            place = (start + 128 * k) // 128
            chunk = values[:, 128 * k : 128 * (k + 1)]
            out_ref[place // rows, place % rows : place % rows + 1] = chunk

    put(0, one_ref[3:4] + (one_ref[4:5] + other_ref[4:5]))
    for k in range(3):
        put((1 + k) * width, one_ref[k : k + 1])
        put((4 + k) * width, two_a_ref[k : k + 1] + two_b_ref[k : k + 1])
    put(7 * width, qkv_ref[0:1, :heads])
    put(7 * width + heads, qkv_ref[0:1, 2 * heads :])
    put(7 * width + 2 * heads, up_ref[0:1])


def join(rows, sums_one, sums_other, sums_two, sums_up, sums_qkv):
    width = sums_one.shape[1]
    length = 7 * width + 2 * sums_qkv.shape[1] // 3 + sums_up.shape[1]
    assert length <= 2 * rows * 128
    operands = [sums_one, sums_other, *sums_two, sums_up, sums_qkv]
    return call(join_body, "join", [((2, rows, 128), F32)], operands, limit=4)[0]


def last_body(dz_ref, own_ref, other_ref, flag_ref, out_a_ref, out_b_ref, tokens_ref, out_ref):
    for rows in chunks(dz_ref.shape[0]):
        total = dz_ref[rows] + (own_ref[rows].astype(F32) + other_ref[rows].astype(F32))
        tokens_ref[rows] = jnp.where(flag_ref[rows, 0:1] > 0.0, 0.0, total)
        out_ref[rows] = rows_in((out_a_ref, out_b_ref), rows)


def last(dz_one, own, other, flag, results):
    shapes = [(dz_one.shape, F32), (dz_one.shape, B16)]
    return call(last_body, "last", shapes, [dz_one, own, other, flag, *results])


def add_late_body(x_ref, y_ref, from_x_ref, from_y_ref, out_x_ref, out_y_ref):
    out_x_ref[...] = (x_ref[...].astype(F32) + from_y_ref[:2].astype(F32)).astype(B16)
    out_y_ref[...] = (y_ref[...].astype(F32) + from_x_ref[:2].astype(F32)).astype(B16)


def add_own_body(own_ref, from_x_ref, from_y_ref, late_x_ref, late_y_ref, near_ref, mid_ref):
    near_ref[...] = (
        own_ref[:2].astype(F32) + from_x_ref[2:].astype(F32) + late_y_ref[...].astype(F32)
    )
    mid_ref[...] = (
        own_ref[2:].astype(F32) + late_x_ref[...].astype(F32) + from_y_ref[2:].astype(F32)
    ).astype(B16)


def add_mid_body(near_ref, mid_ref, own_ref, far_ref):
    own_ref[...] = near_ref[0] + mid_ref[0].astype(F32)
    far_ref[...] = (near_ref[1] + mid_ref[1].astype(F32)).astype(B16)


def late_vector_body(x_ref, y_ref, from_x_ref, from_y_ref, v_ref, out_x_ref, out_y_ref, vector_ref):
    cols = x_ref.shape[2]
    out_x_ref[...] = (x_ref[...].astype(F32) + from_y_ref[:2].astype(F32)).astype(B16)
    out_y_ref[:, :, :cols] = (y_ref[...].astype(F32) + from_x_ref[:2, :, :cols].astype(F32)).astype(B16)
    vector = (v_ref[...].astype(F32) + from_x_ref[:2, :, cols:].astype(F32)).astype(B16)
    out_y_ref[:, :, cols:] = vector
    vector_ref[...] = vector


def own_vector_body(own_ref, from_x_ref, from_y_ref, late_x_ref, late_y_ref, v_ref, near_ref, mid_ref, vector_ref):
    cols = own_ref.shape[2]
    near_ref[...] = (
        own_ref[:2].astype(F32)
        + from_x_ref[2:, :, :cols].astype(F32)
        + late_y_ref[:, :, :cols].astype(F32)
    )
    mid_ref[:, :, :cols] = (
        own_ref[2:].astype(F32) + late_x_ref[...].astype(F32) + from_y_ref[2:].astype(F32)
    ).astype(B16)
    vector = (v_ref[...].astype(F32) + late_y_ref[:, :, cols:].astype(F32)).astype(B16)
    mid_ref[:, :, cols:] = vector
    vector_ref[...] = vector


def mid_vector_body(near_ref, mid_ref, v_ref, own_ref, far_ref, vector_ref):
    cols = own_ref.shape[1]
    own_ref[...] = near_ref[0] + mid_ref[0, :, :cols].astype(F32)
    far_ref[:, :cols] = (near_ref[1] + mid_ref[1, :, :cols].astype(F32)).astype(B16)
    vector = (v_ref[...].astype(F32) + mid_ref[:, :, cols:].astype(F32)).astype(B16)
    for k in range(2):
        far_ref[:, cols + 128 * k : cols + 128 * (k + 1)] = vector[k]
    vector_ref[...] = vector


def far_vector_body(own_ref, far_ref, v_ref, *outs):
    rows, cols = own_ref.shape
    part = cols // 4
    for k in range(4):
        lanes = slice(k * part, (k + 1) * part)
        outs[k][...] = own_ref[:, lanes] + far_ref[:, lanes].astype(F32)
    place = 0
    joined = [
        v_ref[k].astype(F32) + far_ref[:, cols + 128 * k : cols + 128 * (k + 1)].astype(F32) for k in range(2)
    ]
    for out_ref in outs[4:]:
        for k in range(out_ref.shape[0]):
            out_ref[k : k + 1] = joined[place // rows][place % rows : place % rows + 1]
            place += 1


def late_vector(late_x, late_y, from_x, from_y, vector):
    rows, cols = late_x.shape[1:]
    shapes = [(late_x.shape, B16), ((2, rows, cols + 128), B16), (vector.shape, B16)]
    operands = [late_x, late_y, from_x, from_y, vector]
    return call(late_vector_body, "late_vector", shapes, operands, limit=8)


def own_vector(own, from_x, from_y, late_x, late_y, vector):
    rows, cols = own.shape[1:]
    shapes = [((2, rows, cols), F32), ((2, rows, cols + 128), B16), (vector.shape, B16)]
    operands = [own, from_x, from_y, late_x, late_y, vector]
    return call(own_vector_body, "own_vector", shapes, operands, limit=8)


def mid_vector(near, mid, vector):
    rows, cols = near.shape[1:]
    shapes = [((rows, cols), F32), ((rows, cols + 256), B16), (vector.shape, B16)]
    return call(mid_vector_body, "mid_vector", shapes, [near, mid, vector], limit=8)


def far_vector(own, far, vector, sizes):
    rows, cols = own.shape
    shapes = [((rows, cols // 4), F32)] * 4 + [((size // 128, 128), F32) for size in sizes]
    outs = call(far_vector_body, "far_vector", shapes, [own, far, vector], limit=8)
    return outs[:4], [member.reshape(-1) for member in outs[4:]]


def add_late(late_x, late_y, from_x, from_y):
    shape = (late_x.shape, B16)
    return call(add_late_body, "add_late", [shape, shape], [late_x, late_y, from_x, from_y], limit=8)


def add_own(own, from_x, from_y, late_x, late_y):
    shapes = [(late_x.shape, F32), (late_x.shape, B16)]
    return call(add_own_body, "add_own", shapes, [own, from_x, from_y, late_x, late_y], limit=8)


def add_mid(near, mid):
    shapes = [(near.shape[1:], F32), (near.shape[1:], B16)]
    return call(add_mid_body, "add_mid", shapes, [near, mid], limit=8)


def per_device(dp_size, tokens, masked, lengths, mask_vector, w_query, b_query, w_key, w_value,
               b_value, w_out, b_out, gain_one, shift_one, w_up, b_up, w_down, b_down, gain_two,
               shift_two, grad_out):
    head_cols = w_query.shape[1]
    width = tokens.shape[1]
    fast = dp_size == BLOCKS and w_query.shape[0] % 16 == 0
    me = lax.axis_index("dp").astype(jnp.int32).reshape(1)
    if not fast:
        me = jnp.zeros_like(me)

    (b_query, b_value, b_out, gain_one, shift_one, b_up, b_down, gain_two, shift_two) = (
        member.astype(F32)
        for member in (b_query, b_value, b_out, gain_one, shift_one, b_up, b_down, gain_two, shift_two)
    )
    is_masked = (masked == 1)[:, None]
    flag = jnp.broadcast_to(is_masked, (masked.shape[0], 128)).astype(F32)
    in_low = jnp.where(is_masked, mask_vector[None, :], tokens)
    bias_qkv = jnp.concatenate([b_query, jnp.zeros_like(b_query), b_value])[None, :]
    vectors_one = jnp.stack([b_out, gain_one, shift_one])
    vectors_two = jnp.stack([gain_one, shift_one, b_down, gain_two, shift_two])
    b_up, gain_one = b_up[None, :], gain_one[None, :]

    a = jnp.concatenate([w_query, w_key, w_value, w_out.T], axis=1)
    c = w_up
    d = w_down.T
    if fast:
        az = swap(a, 12)
        az, me, flag, in_low, bias_qkv, vectors_one, vectors_two, b_up, gain_one = tie(
            az, me, flag, in_low, bias_qkv, vectors_one, vectors_two, b_up, gain_one
        )
        an = jnp.stack([a, az])
        anx, any_, am = swap(an, 1), swap(an, 2), swap(an, 4)
        anx, any_, am, an, c = tie(anx, any_, am, an, c)
        amx, amy, cz = swap(am, 1), swap(am, 2), swap(c, 12)
        amx, amy, cz, anx, c, d = tie(amx, amy, cz, anx, c, d)
        cn = jnp.stack([c, cz])
        amd, and_, cm = swap(amy, 1), swap(anx, 2), swap(cn, 4)
        cnx, cny, dz = swap(cn, 1), swap(cn, 2), swap(after(d, cm), 12)
        amd, and_, cm, cnx, cny = tie(amd, and_, cm, cnx, cny)
        dn = jnp.stack([d, dz])
        pieces_a = [an, am, anx, amx, any_, amy, and_, amd]
        cmx, cnd, dm = swap(cm, 1), swap(cnx, 2), swap(dn, 4)
        dnx, dny = swap(dn, 1), swap(dn, 2)
    else:
        a, c, d = (lax.all_gather(piece, "dp", axis=0, tiled=True) for piece in (a, c, d))
        pieces_a, pieces_c, pieces_d = as_pieces(a), as_pieces(c), as_pieces(d)
    w_a, qkv, prob, attended, part = attend(me, lengths, in_low, bias_qkv, pieces_a)
    if fast:
        cmx, cnd, dm, dnx, dny, cm, part = tie(cmx, cnd, dm, dnx, dny, cm, part)
        cmy, dnd, cmd = swap(cm, 2), swap(dny, 1), swap(cnd, 4)
    other = pair_swap(part)
    if fast:
        cmy, dnd, cmd, dm, other, part = tie(cmy, dnd, cmd, dm, other, part)
        pieces_c = [cn, cm, cnx, cmx, cny, cmy, cnd, cmd]
        dmx, dmy, dmd = swap(dm, 1), swap(dm, 2), swap(dnd, 4)
    w_u, normed_one, inverse_one, hidden_low, act_low, slope = up(
        me, in_low, part, other, vectors_one, b_up, pieces_c
    )
    if fast:
        dmx, dmy, dmd, act_low = tie(dmx, dmy, dmd, act_low)
        pieces_d = [dn, dm, dnx, dmx, dny, dmy, dnd, dmd]
    w_d, *parts = down(me, act_low, pieces_d)
    halves = [
        second_norm(index * part.shape[0], normed_one, part, pair_swap(part), grad_out, vectors_two)
        for index, part in enumerate(parts)
    ]
    results, dz_two, dz_two_low, sums_two = zip(*halves)
    dx, dy, turned = weight_grad(me, [dz_two_low], [act_low], ORDER[:2])
    if fast:
        dx, dy, turned, dz_two_low = tie(dx, dy, turned, dz_two_low)
        dxr, dyr = swap(dx, 1), swap(dy, 2)
    dxl, dyl, do = weight_grad(me, None, [act_low], ORDER[2:], turned=turned)
    d_pre_low, part, sums_up = hidden_back(dz_two_low, slope, w_d, w_u)
    cx, cy, cxl, cyl, co = weight_grad(me, [[hidden_low]], [d_pre_low])
    if fast:
        dxr, dyr, part, cx, cy, dxl, dyl, do = tie(dxr, dyr, part, cx, cy, dxl, dyl, do)
        cxr, cyr = swap(cx, 1), swap(cy, 2)
        dxl, dyl = add_late(dxl, dyl, dxr, dyr)
        dxlr, dylr = swap(dxl, 1), swap(dyl, 2)
    other = pair_swap(part)
    dz_one, dz_one_low, d_qkv, part, sums_one, sums_qkv = attend_back(
        lengths.shape[0], dz_two, part, other, normed_one, inverse_one, gain_one, flag, qkv, prob, w_a
    )
    if fast:
        cxr, cyr, dxlr, dylr, part, d_qkv, dz_one_low = tie(cxr, cyr, dxlr, dylr, part, d_qkv, dz_one_low)
        cxl, cyl = add_late(cxl, cyl, cxr, cyr)
        cxlr, cylr = swap(cxl, 1), swap(cyl, 2)
        d_near, d_mid = add_own(do, dxr, dyr, dxlr, dylr)
        d_midr = swap(d_mid, 4)
    sums_other = pair_swap(sums_one)
    joined = join(width // BLOCKS, sums_one, sums_other, sums_two, sums_up, sums_qkv)
    vector = joined.astype(B16) if fast else None
    ax, ay, axl, ayl, ao = weight_grad(me, [[in_low], [dz_one_low]], [d_qkv, attended], vector=vector)
    if fast:
        cxlr, cylr, d_midr, ax, ay, part = tie(cxlr, cylr, d_midr, ax, ay, part)
        axr, ayr = swap(ax, 1), swap(ay, 2)
        c_near, c_mid = add_own(co, cxr, cyr, cxlr, cylr)
        d_near, d_far = add_mid(d_near, d_midr)
        c_midr, d_farr = swap(c_mid, 4), swap(d_far, 12)
    other = pair_swap(part)
    d_tokens, result = last(dz_one, part, other, flag, results)
    sizes = [width] * 7 + [head_cols] * 2 + [w_up.shape[1]]
    if fast:
        axr, ayr, c_midr, d_farr, d_tokens, result = tie(axr, ayr, c_midr, d_farr, d_tokens, result)
        axl, ayl, vector = late_vector(axl, ayl, axr, ayr, vector)
        axlr, aylr = swap(axl, 1), swap(ayl, 2)
        c_near, c_far = add_mid(c_near, c_midr)
        c_farr = swap(c_far, 12)
        axlr, aylr, c_farr = tie(axlr, aylr, c_farr)
        a_near, a_mid, vector = own_vector(ao, axr, ayr, axlr, aylr, vector)
        a_midr = swap(a_mid, 4)
        d_w_down_t = d_near + d_farr.astype(F32)
        a_midr, d_w_down_t = tie(a_midr, d_w_down_t)
        a_near, a_far, vector = mid_vector(a_near, a_midr, vector)
        a_farr = swap(a_far, 12)
        d_w_up = c_near + c_farr.astype(F32)
        d_wa, summed = far_vector(a_near, a_farr, vector, sizes)
    else:
        full = []
        for parts in ((ax, ay, axl, ayl, ao), (cx, cy, cxl, cyl, co), (dx, dy, dxl, dyl, do)):
            blocks = [None] * BLOCKS
            for member, offsets in zip(parts, ORDER):
                for k, offset in enumerate(offsets):
                    blocks[offset] = member[k]
            full.append(jnp.concatenate(blocks).astype(F32))
        joined = lax.psum(joined, "dp")
        d_wa, d_w_up, d_w_down_t = (
            lax.psum_scatter(member, "dp", scatter_dimension=0, tiled=True) for member in full
        )
        d_wa = [d_wa[:, k * head_cols : (k + 1) * head_cols] for k in range(4)]
        joined = joined.reshape(-1)
        summed = []
        start = 0
        for size in sizes:
            summed.append(joined[start : start + size])
            start += size
    return (
        result,
        d_tokens,
        summed[0],
        d_wa[0],
        summed[7],
        d_wa[1],
        d_wa[2],
        summed[8],
        d_wa[3].T,
        summed[3],
        summed[1],
        summed[2],
        d_w_up,
        summed[9],
        d_w_down_t.T,
        summed[6],
        summed[4],
        summed[5],
    )


def solution(mesh):
    rows, flat, both = P("dp", None), P(), P("dp", "mp")
    return jax.shard_map(
        functools.partial(per_device, mesh.shape["dp"]),
        mesh=mesh,
        in_specs=(rows, P("dp"), P("dp"), flat, both, P("mp"), both, both, P("mp"), P("mp", "dp"),
                  flat, flat, flat, both, P("mp"), P("mp", "dp"), flat, flat, flat, rows),
        out_specs=(rows, rows, flat, both, P("mp"), both, both, P("mp"), P("mp", "dp"), flat, flat,
                   flat, both, P("mp"), P("mp", "dp"), flat, flat, flat),
        check_vma=False,
    )
```

profile of v0, /device:TPU:0, one launch (start us, length us, event | category | flops | bytes accessed | tf_op | source)
XLA Modules:
  0.0 186.8 jit_solution(16980043654322439414)
XLA Ops:
  1.5 5.1 %collective-permute-start = (bf16[48,1536]{1,0:T(8,128)(2,1)S(1)}, bf16[48,1536]{1,0:T(8,128)(2,1)S(1)}, u32[]{:S(2)}, u32[]{:S(2)}) collective-permute-start(bf16[48,1536]{1,0:T(8,128)(2,1)S(1)} %get-tuple-element.347), channel_id=1, source_target_pairs={{0,24},{2,26},{4,28},{6,30},{8,16},{10,18},{12,20},{14,22},{16,8},... | collective-permute-start | bytes 442376 | tf_op jit(solution)/shard_map/ppermute | solution.py:22
  11.0 2.7 %collective-permute-start.3 = (bf16[2,48,1536]{2,1,0:T(8,128)(2,1)S(1)}, bf16[2,48,1536]{2,1,0:T(8,128)(2,1)S(1)}, u32[]{:S(2)}, u32[]{:S(2)}) collective-permute-start(bf16[2,48,1536]{2,1,0:T(8,128)(2,1)S(1)} %pad_maximum_fusion.rest_0_), channel_id=1, source_target_pairs={{0,8},{2,10},{4,12},{6,14},{8,0},{10,2},{12,4},{14,6},{16,24},{18,... | collective-permute-start | bytes 884744 | tf_op jit(solution)/shard_map/ppermute | solution.py:22
  16.7 3.3 %collective-permute-done.3.rest_1_ = bf16[2,48,1536]{2,1,0:T(8,128)(2,1)S(1)} collective-permute-done((bf16[2,48,1536]{2,1,0:T(8,128)(2,1)S(1)}, bf16[2,48,1536]{2,1,0:T(8,128)(2,1)S(1)}, u32[]{:S(2)}, u32[]{:S(2)}) %collective-permute-start.3) | collective-permute-done | bytes 294944 | tf_op jit(solution)/shard_map/ppermute | solution.py:22
  26.4 6.1 %collective-permute-done.6 = bf16[48,1536]{1,0:T(8,128)(2,1)S(1)} collective-permute-done((bf16[48,1536]{1,0:T(8,128)(2,1)S(1)}, bf16[48,1536]{1,0:T(8,128)(2,1)S(1)}, u32[]{:S(2)}, u32[]{:S(2)}) %collective-permute-start.6) | collective-permute-done | bytes 147488 | tf_op jit(solution)/shard_map/ppermute | solution.py:22
  36.7 4.2 %collective-permute-done.9.rest_1_ = bf16[2,48,1536]{2,1,0:T(8,128)(2,1)S(1)} collective-permute-done((bf16[2,48,1536]{2,1,0:T(8,128)(2,1)S(1)}, bf16[2,48,1536]{2,1,0:T(8,128)(2,1)S(1)}, u32[]{:S(2)}, u32[]{:S(2)}) %collective-permute-start.9) | collective-permute-done | bytes 294944 | tf_op jit(solution)/shard_map/ppermute | solution.py:22
  41.8 6.0 %collective-permute-done.7.rest_7_ = bf16[2,48,1536]{2,1,0:T(8,128)(2,1)S(1)} collective-permute-done((bf16[2,48,1536]{2,1,0:T(8,128)(2,1)S(1)}, bf16[2,48,1536]{2,1,0:T(8,128)(2,1)S(1)}, u32[]{:S(2)}, u32[]{:S(2)}) %collective-permute-start.7) | collective-permute-done | bytes 294944 | tf_op jit(solution)/shard_map/ppermute | solution.py:22
  54.0 8.0 %attend.1 = (bf16[768,1536]{1,0:T(8,128)(2,1)S(1)}, bf16[1024,1152]{1,0:T(8,128)(2,1)S(1)}, bf16[1024,768]{1,0:T(8,128)(2,1)S(1)}, bf16[1024,384]{1,0:T(8,128)(2,1)S(1)}, bf16[1024,768]{1,0:T(8,128)(2,1)S(1)}) custom-call(s32[1]{0:T(128)} %bitcast.1.me_ref, s32[8]{0:T(128)S(1)} %copy-done.1, bf16[1024,768]{1,0:T(8,128)(2,1)S(1)} %broadcast_select_fusion.in_ref.refs_0_, ...), custom_call_target="tpu_custom_call" | custom-call | flops 1 | bytes 1 | tf_op jit(solution)/shard_map/attend/pallas_call | solution.py:55
  63.8 7.7 %collective-permute-done.18.rest_5_ = bf16[2,48,1536]{2,1,0:T(8,128)(2,1)S(1)} collective-permute-done((bf16[2,48,1536]{2,1,0:T(8,128)(2,1)S(1)}, bf16[2,48,1536]{2,1,0:T(8,128)(2,1)S(1)}, u32[]{:S(2)}, u32[]{:S(2)}) %collective-permute-start.18) | collective-permute-done | bytes 294944 | tf_op jit(solution)/shard_map/ppermute | solution.py:22
  75.3 6.3 %up.1 = (bf16[768,1536]{1,0:T(8,128)(2,1)S(1)}, f32[1024,768]{1,0:T(8,128)S(1)}, f32[1024,128]{1,0:T(8,128)S(1)}, bf16[1024,768]{1,0:T(8,128)(2,1)S(1)}, bf16[10...) custom-call(s32[1]{0:T(128)} %bitcast.1.me_ref, bf16[1024,768]{1,0:T(8,128)(2,1)S(1)} %broadcast_select_fusion.in_ref.refs_0_, ...), custom_call_target="tpu_custom_call" | custom-call | flops 1 | bytes 1 | tf_op jit(solution)/shard_map/up/pallas_call | solution.py:55
  88.9 2.9 %weight_grad.4 = (bf16[4,48,1536]{2,1,0:T(8,128)(2,1)S(1)}, bf16[4,48,1536]{2,1,0:T(8,128)(2,1)S(1)}, bf16[768,1024]{1,0:T(8,128)(2,1)S(1)}) custom-call(s32[1]{0:T(128)} %bitcast.1.me_ref, bf16[512,768]{1,0:T(8,128)(2,1)S(1)} %get-tuple-element.233.refs_0_.low_a_ref, bf16[512,768]{1,0:T(8,128)(2,1)S(1)} %get-tuple-element.234.refs_1_.low_b_ref, ...), custom_call_target="tpu_custom_call" | custom-call | flops 1 | bytes 1 | tf_op jit(solution)/shard_map/weight_grad/pallas_call | solution.py:55
  93.5 2.6 %weight_grad.6 = (bf16[2,48,1536]{2,1,0:T(8,128)(2,1)S(1)}, bf16[2,48,1536]{2,1,0:T(8,128)(2,1)S(1)}, bf16[4,48,1536]{2,1,0:T(8,128)(2,1)S(1)}) custom-call(s32[1]{0:T(128)} %bitcast.1.me_ref, bf16[768,1024]{1,0:T(8,128)(2,1)S(1)} %get-tuple-element.245.refs_0_, bf16[1024,1536]{1,0:T(8,128)(2,1)S(1)} %get-tuple-element.220.act_ref.refs_2_.refs_1_), custom_call_target="tpu_custom_call" | custom-call | flops 1 | bytes 1 | tf_op jit(solution)/shard_map/weight_grad/pallas_call | solution.py:55
  96.1 6.1 %hidden_back.1 = (bf16[1024,1536]{1,0:T(8,128)(2,1)S(1)}, bf16[1024,768]{1,0:T(8,128)(2,1)S(1)}, f32[8,1536]{1,0:T(8,128)S(1)}) custom-call(bf16[512,768]{1,0:T(8,128)(2,1)S(1)} %get-tuple-element.233.refs_0_.low_a_ref, bf16[512,768]{1,0:T(8,128)(2,1)S(1)} %get-tuple-element.234.refs_1_.low_b_ref, bf16[1024,1536]{1,0:T(8,128)(2,1)S(1)} %get-tuple-element.235.slope_ref, ...), custom_call_target="tpu_custom_call" | custom-call | flops 1 | bytes 1 | tf_op jit(solution)/shard_map/hidden_back/pallas_call | solution.py:55
  102.1 4.5 %weight_grad.5 = (bf16[4,48,1536]{2,1,0:T(8,128)(2,1)S(1)}, bf16[4,48,1536]{2,1,0:T(8,128)(2,1)S(1)}, bf16[2,48,1536]{2,1,0:T(8,128)(2,1)S(1)}, bf16[2,48,1536]{2,1,0:T(8,128)(2,1)S(1)}, bf16[4,48,1536]{2,1,0:T(8,128)(2,1)S(1)}) custom-call(s32[1]{0:T(128)} %bitcast.1.me_ref, bf16[1024,768]{1,0:T(8,128)(2,1)S(1)} %get-tuple-element.215.refs_0_, ...), custom_call_target="tpu_custom_call" | custom-call | flops 1 | bytes 1 | tf_op jit(solution)/shard_map/weight_grad/pallas_call | solution.py:55
  112.7 15.5 %attend_back.1 = (f32[1024,768]{1,0:T(8,128)S(1)}, bf16[1024,768]{1,0:T(8,128)(2,1)S(1)}, bf16[1024,1152]{1,0:T(8,128)(2,1)S(1)}, bf16[1024,768]{1,0:T(8,128)(2,...) custom-call(f32[512,768]{1,0:T(8,128)S(1)} %get-tuple-element.257.dz_a_ref, ...), custom_call_target="tpu_custom_call" | custom-call | flops 1 | bytes 1 | tf_op jit(solution)/shard_map/attend_back/pallas_call | solution.py:55
  128.2 2.3 %collective-permute-done.31.late_x_ref = bf16[2,48,1536]{2,1,0:T(8,128)(2,1)S(1)} collective-permute-done((bf16[2,48,1536]{2,1,0:T(8,128)(2,1)S(1)}, bf16[2,48,1536]{2,1,0:T(8,128)(2,1)S(1)}, u32[]{:S(2)}, u32[]{:S(2)}) %collective-permute-start.31) | collective-permute-done | bytes 294944 | tf_op jit(solution)/shard_map/ppermute | solution.py:22
  135.7 5.4 %weight_grad.7 = (bf16[4,48,1664]{2,1,0:T(8,128)(2,1)S(1)}, bf16[4,48,1536]{2,1,0:T(8,128)(2,1)S(1)}, bf16[2,48,1536]{2,1,0:T(8,128)(2,1)S(1)}, bf16[2,48,1536]{2,1,0:T(8,128)(2,1)S(1)}, bf16[4,48,1536]{2,1,0:T(8,128)(2,1)S(1)}) custom-call(s32[1]{0:T(128)} %bitcast.1.me_ref, bf16[1024,768]{1,0:T(8,128)(2,1)S(1)} %broadcast_select_fusion.in_ref.refs_0_, ...), custom_call_target="tpu_custom_call" | custom-call | flops 1 | bytes 1 | tf_op jit(solution)/shard_map/weight_grad/pallas_call | solution.py:55
  145.4 3.4 %collective-permute-start.41 = (bf16[48,1536]{1,0:T(8,128)(2,1)S(1)}, bf16[48,1536]{1,0:T(8,128)(2,1)S(1)}, u32[]{:S(2)}, u32[]{:S(2)}) collective-permute-start(bf16[48,1536]{1,0:T(8,128)(2,1)S(1)} %get-tuple-element.296), channel_id=1, source_target_pairs={{0,24},{2,26},{4,28},{6,30},{8,16},{10,18},{12,20},{14,22},{16,8},... | collective-permute-start | bytes 442376 | tf_op jit(solution)/shard_map/ppermute | solution.py:22
  148.8 2.8 %last.1 = (f32[1024,768]{1,0:T(8,128)}, bf16[1024,768]{1,0:T(8,128)(2,1)}) custom-call(f32[1024,768]{1,0:T(8,128)S(1)} %get-tuple-element.297.dz_ref, bf16[1024,768]{1,0:T(8,128)(2,1)S(1)} %get-tuple-element.298.own_ref, bf16[1024,768]{1,0:T(8,128)(2,1)S(1)} %collective-permute-done.42.other_ref, f32[1024,128]{1,0:T(8,128)S(1)} %broadcast_in_dim.36.flag_ref, ...), custom_call_target="tpu_custom_call" | custom-call | flops 1 | bytes 1 | tf_op jit(solution)/shard_map/last/pallas_call | solution.py:55
  151.6 7.0 %collective-permute-done.41 = bf16[48,1536]{1,0:T(8,128)(2,1)S(1)} collective-permute-done((bf16[48,1536]{1,0:T(8,128)(2,1)S(1)}, bf16[48,1536]{1,0:T(8,128)(2,1)S(1)}, u32[]{:S(2)}, u32[]{:S(2)}) %collective-permute-start.41) | collective-permute-done | bytes 147488 | tf_op jit(solution)/shard_map/ppermute | solution.py:22
  161.0 3.4 %collective-permute-start.45 = (bf16[48,1536]{1,0:T(8,128)(2,1)S(1)}, bf16[48,1536]{1,0:T(8,128)(2,1)S(1)}, u32[]{:S(2)}, u32[]{:S(2)}) collective-permute-start(bf16[48,1536]{1,0:T(8,128)(2,1)S(1)} %get-tuple-element.314), channel_id=1, source_target_pairs={{0,24},{2,26},{4,28},{6,30},{8,16},{10,18},{12,20},{14,22},{16,8},... | collective-permute-start | bytes 442376 | tf_op jit(solution)/shard_map/ppermute | solution.py:22
  164.5 3.6 %collective-permute-done.45 = bf16[48,1536]{1,0:T(8,128)(2,1)S(1)} collective-permute-done((bf16[48,1536]{1,0:T(8,128)(2,1)S(1)}, bf16[48,1536]{1,0:T(8,128)(2,1)S(1)}, u32[]{:S(2)}, u32[]{:S(2)}) %collective-permute-start.45) | collective-permute-done | bytes 147488 | tf_op jit(solution)/shard_map/ppermute | solution.py:22
  168.4 2.9 %collective-permute-start.46 = (bf16[2,48,1664]{2,1,0:T(8,128)(2,1)S(1)}, bf16[2,48,1664]{2,1,0:T(8,128)(2,1)S(1)}, u32[]{:S(2)}, u32[]{:S(2)}) collective-permute-start(bf16[2,48,1664]{2,1,0:T(8,128)(2,1)S(1)} %get-tuple-element.319), channel_id=1, source_target_pairs={{0,8},{2,10},{4,12},{6,14},{8,0},{10,2},{12,4},{14,6},{16,24},{18,... | collective-permute-start | bytes 958472 | tf_op jit(solution)/shard_map/ppermute | solution.py:22
  172.0 6.5 %collective-permute-done.46.mid_ref = bf16[2,48,1664]{2,1,0:T(8,128)(2,1)S(1)} collective-permute-done((bf16[2,48,1664]{2,1,0:T(8,128)(2,1)S(1)}, bf16[2,48,1664]{2,1,0:T(8,128)(2,1)S(1)}, u32[]{:S(2)}, u32[]{:S(2)}) %collective-permute-start.46) | collective-permute-done | bytes 319520 | tf_op jit(solution)/shard_map/ppermute | solution.py:22
  181.3 4.6 %collective-permute-done.47.far_ref = bf16[48,1792]{1,0:T(8,128)(2,1)S(1)} collective-permute-done((bf16[48,1792]{1,0:T(8,128)(2,1)S(1)}, bf16[48,1792]{1,0:T(8,128)(2,1)S(1)}, u32[]{:S(2)}, u32[]{:S(2)}) %collective-permute-start.47) | collective-permute-done | bytes 172064 | tf_op jit(solution)/shard_map/ppermute | solution.py:22
  (142 shorter events, 62.5 us)
Async XLA Ops:
  22.7 9.8 %collective-permute-start.5 = (bf16[2,48,1536]{2,1,0:T(8,128)(2,1)S(1)}, bf16[2,48,1536]{2,1,0:T(8,128)(2,1)S(1)}, u32[]{:S(2)}, u32[]{:S(2)}) collective-permute-start(bf16[2,48,1536]{2,1,0:T(8,128)(2,1)S(1)} %collective-permute-done.3.rest_1_), channel_id=1, source_target_pairs={{0,4},{2,6},{4,0},{6,2},{8,12},{10,14},{12,8},{14,10},{16,20},{18,... | collective-permute-start | bytes 884744 | tf_op jit(solution)/shard_map/ppermute | solution.py:22
  23.2 9.3 %collective-permute-start.4 = (bf16[2,48,1536]{2,1,0:T(8,128)(2,1)S(1)}, bf16[2,48,1536]{2,1,0:T(8,128)(2,1)S(1)}, u32[]{:S(2)}, u32[]{:S(2)}) collective-permute-start(bf16[2,48,1536]{2,1,0:T(8,128)(2,1)S(1)} %collective-permute-done.3.rest_1_), channel_id=1, source_target_pairs={{0,2},{2,0},{4,6},{6,4},{8,10},{10,8},{12,14},{14,12},{16,18},{18,... | collective-permute-start | bytes 884744 | tf_op jit(solution)/shard_map/ppermute | solution.py:22
  34.8 13.0 %collective-permute-start.7 = (bf16[2,48,1536]{2,1,0:T(8,128)(2,1)S(1)}, bf16[2,48,1536]{2,1,0:T(8,128)(2,1)S(1)}, u32[]{:S(2)}, u32[]{:S(2)}) collective-permute-start(bf16[2,48,1536]{2,1,0:T(8,128)(2,1)S(1)} %collective-permute-done.5.rest_5_), channel_id=1, source_target_pairs={{0,2},{2,0},{4,6},{6,4},{8,10},{10,8},{12,14},{14,12},{16,18},{18,... | collective-permute-start | bytes 884744 | tf_op jit(solution)/shard_map/ppermute | solution.py:22
  36.3 11.5 %collective-permute-start.8 = (bf16[2,48,1536]{2,1,0:T(8,128)(2,1)S(1)}, bf16[2,48,1536]{2,1,0:T(8,128)(2,1)S(1)}, u32[]{:S(2)}, u32[]{:S(2)}) collective-permute-start(bf16[2,48,1536]{2,1,0:T(8,128)(2,1)S(1)} %collective-permute-done.1.rest_2_), channel_id=1, source_target_pairs={{0,4},{2,6},{4,0},{6,2},{8,12},{10,14},{12,8},{14,10},{16,20},{18,... | collective-permute-start | bytes 884744 | tf_op jit(solution)/shard_map/ppermute | solution.py:22
  47.8 14.2 %collective-permute-start.12 = (bf16[2,48,1536]{2,1,0:T(8,128)(2,1)S(1)}, bf16[2,48,1536]{2,1,0:T(8,128)(2,1)S(1)}, u32[]{:S(2)}, u32[]{:S(2)}) collective-permute-start(bf16[2,48,1536]{2,1,0:T(8,128)(2,1)S(1)} %collective-permute-done.9.rest_1_), channel_id=1, source_target_pairs={{0,2},{2,0},{4,6},{6,4},{8,10},{10,8},{12,14},{14,12},{16,18},{18,... | collective-permute-start | bytes 884744 | tf_op jit(solution)/shard_map/ppermute | solution.py:22
  48.3 13.7 %collective-permute-start.13 = (bf16[2,48,1536]{2,1,0:T(8,128)(2,1)S(1)}, bf16[2,48,1536]{2,1,0:T(8,128)(2,1)S(1)}, u32[]{:S(2)}, u32[]{:S(2)}) collective-permute-start(bf16[2,48,1536]{2,1,0:T(8,128)(2,1)S(1)} %collective-permute-done.10.rest_2_), channel_id=1, source_target_pairs={{0,4},{2,6},{4,0},{6,2},{8,12},{10,14},{12,8},{14,10},{16,20},{18,... | collective-permute-start | bytes 884744 | tf_op jit(solution)/shard_map/ppermute | solution.py:22
  49.5 12.5 %collective-permute-start.17 = (bf16[2,48,1536]{2,1,0:T(8,128)(2,1)S(1)}, bf16[2,48,1536]{2,1,0:T(8,128)(2,1)S(1)}, u32[]{:S(2)}, u32[]{:S(2)}) collective-permute-start(bf16[2,48,1536]{2,1,0:T(8,128)(2,1)S(1)} %pad_maximum_fusion.2.rest_0_), channel_id=1, source_target_pairs={{0,4},{2,6},{4,0},{6,2},{8,12},{10,14},{12,8},{14,10},{16,20},{18,... | collective-permute-start | bytes 884744 | tf_op jit(solution)/shard_map/ppermute | solution.py:22
  50.4 11.6 %collective-permute-start.16 = (bf16[2,48,1536]{2,1,0:T(8,128)(2,1)S(1)}, bf16[2,48,1536]{2,1,0:T(8,128)(2,1)S(1)}, u32[]{:S(2)}, u32[]{:S(2)}) collective-permute-start(bf16[2,48,1536]{2,1,0:T(8,128)(2,1)S(1)} %pad_maximum_fusion.2.rest_0_), channel_id=1, source_target_pairs={{0,2},{2,0},{4,6},{6,4},{8,10},{10,8},{12,14},{14,12},{16,18},{18,... | collective-permute-start | bytes 884744 | tf_op jit(solution)/shard_map/ppermute | solution.py:22
  51.9 10.1 %collective-permute-start.15 = (bf16[2,48,1536]{2,1,0:T(8,128)(2,1)S(1)}, bf16[2,48,1536]{2,1,0:T(8,128)(2,1)S(1)}, u32[]{:S(2)}, u32[]{:S(2)}) collective-permute-start(bf16[2,48,1536]{2,1,0:T(8,128)(2,1)S(1)} %pad_maximum_fusion.2.rest_0_), channel_id=1, source_target_pairs={{0,8},{2,10},{4,12},{6,14},{8,0},{10,2},{12,4},{14,6},{16,24},{18,... | collective-permute-start | bytes 884744 | tf_op jit(solution)/shard_map/ppermute | solution.py:22
  62.0 9.8 %collective-permute-start.21 = (bf16[1024,768]{1,0:T(8,128)(2,1)S(1)}, bf16[1024,768]{1,0:T(8,128)(2,1)S(1)}, u32[]{:S(2)}, u32[]{:S(2)}) collective-permute-start(bf16[1024,768]{1,0:T(8,128)(2,1)S(1)} %get-tuple-element.207.own_ref), channel_id=1, source_target_pairs={{0,1},{1,0},{2,3},{3,2},{4,5},{5,4},{6,7},{7,6},{8,9},{9,8},{10,11... | collective-permute-start | bytes 4718600 | tf_op jit(solution)/shard_map/ppermute | solution.py:34
  62.1 9.4 %collective-permute-start.18 = (bf16[2,48,1536]{2,1,0:T(8,128)(2,1)S(1)}, bf16[2,48,1536]{2,1,0:T(8,128)(2,1)S(1)}, u32[]{:S(2)}, u32[]{:S(2)}) collective-permute-start(bf16[2,48,1536]{2,1,0:T(8,128)(2,1)S(1)} %collective-permute-done.9.rest_1_), channel_id=1, source_target_pairs={{0,4},{2,6},{4,0},{6,2},{8,12},{10,14},{12,8},{14,10},{16,20},{18,... | collective-permute-start | bytes 884744 | tf_op jit(solution)/shard_map/ppermute | solution.py:22
  71.8 9.8 %collective-permute-start.24 = (bf16[2,48,1536]{2,1,0:T(8,128)(2,1)S(1)}, bf16[2,48,1536]{2,1,0:T(8,128)(2,1)S(1)}, u32[]{:S(2)}, u32[]{:S(2)}) collective-permute-start(bf16[2,48,1536]{2,1,0:T(8,128)(2,1)S(1)} %collective-permute-done.19.rest_6_), channel_id=1, source_target_pairs={{0,8},{2,10},{4,12},{6,14},{8,0},{10,2},{12,4},{14,6},{16,24},{18,... | collective-permute-start | bytes 884744 | tf_op jit(solution)/shard_map/ppermute | solution.py:22
  91.8 15.6 %collective-permute-start.27 = (bf16[4,48,1536]{2,1,0:T(8,128)(2,1)S(1)}, bf16[4,48,1536]{2,1,0:T(8,128)(2,1)S(1)}, u32[]{:S(2)}, u32[]{:S(2)}) collective-permute-start(bf16[4,48,1536]{2,1,0:T(8,128)(2,1)S(1)} %get-tuple-element.240), channel_id=1, source_target_pairs={{0,2},{2,0},{4,6},{6,4},{8,10},{10,8},{12,14},{14,12},{16,18},{18,... | collective-permute-start | bytes 1769480 | tf_op jit(solution)/shard_map/ppermute | solution.py:22
  93.2 15.3 %collective-permute-start.28 = (bf16[4,48,1536]{2,1,0:T(8,128)(2,1)S(1)}, bf16[4,48,1536]{2,1,0:T(8,128)(2,1)S(1)}, u32[]{:S(2)}, u32[]{:S(2)}) collective-permute-start(bf16[4,48,1536]{2,1,0:T(8,128)(2,1)S(1)} %get-tuple-element.241), channel_id=1, source_target_pairs={{0,4},{2,6},{4,0},{6,2},{8,12},{10,14},{12,8},{14,10},{16,20},{18,... | collective-permute-start | bytes 1769480 | tf_op jit(solution)/shard_map/ppermute | solution.py:22
  108.5 22.5 %collective-permute-start.29 = (bf16[4,48,1536]{2,1,0:T(8,128)(2,1)S(1)}, bf16[4,48,1536]{2,1,0:T(8,128)(2,1)S(1)}, u32[]{:S(2)}, u32[]{:S(2)}) collective-permute-start(bf16[4,48,1536]{2,1,0:T(8,128)(2,1)S(1)} %get-tuple-element.249), channel_id=1, source_target_pairs={{0,2},{2,0},{4,6},{6,4},{8,10},{10,8},{12,14},{14,12},{16,18},{18,... | collective-permute-start | bytes 1769480 | tf_op jit(solution)/shard_map/ppermute | solution.py:22
  109.2 21.8 %collective-permute-start.30 = (bf16[4,48,1536]{2,1,0:T(8,128)(2,1)S(1)}, bf16[4,48,1536]{2,1,0:T(8,128)(2,1)S(1)}, u32[]{:S(2)}, u32[]{:S(2)}) collective-permute-start(bf16[4,48,1536]{2,1,0:T(8,128)(2,1)S(1)} %get-tuple-element.250), channel_id=1, source_target_pairs={{0,4},{2,6},{4,0},{6,2},{8,12},{10,14},{12,8},{14,10},{16,20},{18,... | collective-permute-start | bytes 1769480 | tf_op jit(solution)/shard_map/ppermute | solution.py:22
  109.6 20.9 %collective-permute-start.31 = (bf16[2,48,1536]{2,1,0:T(8,128)(2,1)S(1)}, bf16[2,48,1536]{2,1,0:T(8,128)(2,1)S(1)}, u32[]{:S(2)}, u32[]{:S(2)}) collective-permute-start(bf16[2,48,1536]{2,1,0:T(8,128)(2,1)S(1)} %get-tuple-element.255), channel_id=1, source_target_pairs={{0,2},{2,0},{4,6},{6,4},{8,10},{10,8},{12,14},{14,12},{16,18},{18,... | collective-permute-start | bytes 884744 | tf_op jit(solution)/shard_map/ppermute | solution.py:22
  111.0 19.9 %collective-permute-start.32 = (bf16[2,48,1536]{2,1,0:T(8,128)(2,1)S(1)}, bf16[2,48,1536]{2,1,0:T(8,128)(2,1)S(1)}, u32[]{:S(2)}, u32[]{:S(2)}) collective-permute-start(bf16[2,48,1536]{2,1,0:T(8,128)(2,1)S(1)} %get-tuple-element.256), channel_id=1, source_target_pairs={{0,4},{2,6},{4,0},{6,2},{8,12},{10,14},{12,8},{14,10},{16,20},{18,... | collective-permute-start | bytes 884744 | tf_op jit(solution)/shard_map/ppermute | solution.py:22
  131.1 10.0 %collective-permute-start.34 = (bf16[2,48,1536]{2,1,0:T(8,128)(2,1)S(1)}, bf16[2,48,1536]{2,1,0:T(8,128)(2,1)S(1)}, u32[]{:S(2)}, u32[]{:S(2)}) collective-permute-start(bf16[2,48,1536]{2,1,0:T(8,128)(2,1)S(1)} %get-tuple-element.271), channel_id=1, source_target_pairs={{0,2},{2,0},{4,6},{6,4},{8,10},{10,8},{12,14},{14,12},{16,18},{18,... | collective-permute-start | bytes 884744 | tf_op jit(solution)/shard_map/ppermute | solution.py:22
  141.4 17.3 %collective-permute-start.38 = (bf16[4,48,1664]{2,1,0:T(8,128)(2,1)S(1)}, bf16[4,48,1664]{2,1,0:T(8,128)(2,1)S(1)}, u32[]{:S(2)}, u32[]{:S(2)}) collective-permute-start(bf16[4,48,1664]{2,1,0:T(8,128)(2,1)S(1)} %get-tuple-element.288), channel_id=1, source_target_pairs={{0,2},{2,0},{4,6},{6,4},{8,10},{10,8},{12,14},{14,12},{16,18},{18,... | collective-permute-start | bytes 1916936 | tf_op jit(solution)/shard_map/ppermute | solution.py:22
  142.4 16.3 %collective-permute-start.39 = (bf16[4,48,1536]{2,1,0:T(8,128)(2,1)S(1)}, bf16[4,48,1536]{2,1,0:T(8,128)(2,1)S(1)}, u32[]{:S(2)}, u32[]{:S(2)}) collective-permute-start(bf16[4,48,1536]{2,1,0:T(8,128)(2,1)S(1)} %get-tuple-element.289), channel_id=1, source_target_pairs={{0,4},{2,6},{4,0},{6,2},{8,12},{10,14},{12,8},{14,10},{16,20},{18,... | collective-permute-start | bytes 1769480 | tf_op jit(solution)/shard_map/ppermute | solution.py:22
  144.4 14.3 %collective-permute-start.40 = (bf16[2,48,1536]{2,1,0:T(8,128)(2,1)S(1)}, bf16[2,48,1536]{2,1,0:T(8,128)(2,1)S(1)}, u32[]{:S(2)}, u32[]{:S(2)}) collective-permute-start(bf16[2,48,1536]{2,1,0:T(8,128)(2,1)S(1)} %get-tuple-element.293), channel_id=1, source_target_pairs={{0,8},{2,10},{4,12},{6,14},{8,0},{10,2},{12,4},{14,6},{16,24},{18,... | collective-permute-start | bytes 884744 | tf_op jit(solution)/shard_map/ppermute | solution.py:22
  145.4 13.3 %collective-permute-start.41 = (bf16[48,1536]{1,0:T(8,128)(2,1)S(1)}, bf16[48,1536]{1,0:T(8,128)(2,1)S(1)}, u32[]{:S(2)}, u32[]{:S(2)}) collective-permute-start(bf16[48,1536]{1,0:T(8,128)(2,1)S(1)} %get-tuple-element.296), channel_id=1, source_target_pairs={{0,24},{2,26},{4,28},{6,30},{8,16},{10,18},{12,20},{14,22},{16,8},... | collective-permute-start | bytes 442376 | tf_op jit(solution)/shard_map/ppermute | solution.py:22
  168.4 10.1 %collective-permute-start.46 = (bf16[2,48,1664]{2,1,0:T(8,128)(2,1)S(1)}, bf16[2,48,1664]{2,1,0:T(8,128)(2,1)S(1)}, u32[]{:S(2)}, u32[]{:S(2)}) collective-permute-start(bf16[2,48,1664]{2,1,0:T(8,128)(2,1)S(1)} %get-tuple-element.319), channel_id=1, source_target_pairs={{0,8},{2,10},{4,12},{6,14},{8,0},{10,2},{12,4},{14,6},{16,24},{18,... | collective-permute-start | bytes 958472 | tf_op jit(solution)/shard_map/ppermute | solution.py:22
  (35 other events, 281.7 us)
where the time goes:
time: 187 us
  Pallas kernels  62.4 us (33%)
  waiting for transfers between devices  58.9 us (31%)
  starting transfers between devices  57.6 us (31%)
  other arithmetic  6.19 us (3%)
    pallas_call x24, Pallas kernels, call(): pl.pallas_call(body, in_specs=[SMEM_SPEC if member.dtype == jnp.int32 and...  62.4 us
    ppermute x42, waiting for transfers between devices, swap(): return lax.ppermute(values, 'dp', [(i, i ^ bit) for i in range(BLOCKS)])  57.4 us
    ppermute x42, starting transfers between devices, swap(): return lax.ppermute(values, 'dp', [(i, i ^ bit) for i in range(BLOCKS)])  56.7 us
  transfers between devices with their start and end apart: 48, of which 20 were waited for; matrix products, arithmetic and copies ran while one was open for 3% of the time, Pallas kernels for 29%

commit v1 on v0

--- a/solution.py
+++ b/solution.py
@@ -71,12 +71,12 @@
     return [slice(start, start + CHUNK) for start in range(0, count, CHUNK)]
 
 
-def loop(count, step, size=CHUNK):
+def loop(count, step, size=CHUNK, unroll=1):
     def body(index, carry):
         step(pl.ds(pl.multiple_of(index * size, size), size))
         return carry
 
-    lax.fori_loop(0, count // size, body, 0)
+    lax.fori_loop(0, count // size, body, 0, unroll=unroll)
 
 
 PAIRS = [(q + bits[k], 2 * q + m, k) for q in range(4) for m, bits in enumerate((NEAR, MID)) for k in range(2)]
@@ -137,7 +137,7 @@
     def project(rows):
         qkv_ref[rows] = (dot(in_ref[rows], w_ref[:, : 3 * width]) + bias_ref[...]).astype(B16)
 
-    loop(count, project)
+    loop(count, project, unroll=4)
     mask = two_heads(slots)
     key_slot = lax.broadcasted_iota(jnp.int32, (slots, slots), 1)
 
@@ -165,7 +165,7 @@
     def bring_out(rows):
         part_ref[rows] = dot_t(att_ref[rows], w_ref[:, 3 * width :]).astype(B16)
 
-    loop(count, bring_out)
+    loop(count, bring_out, unroll=4)
 
 
 def attend(me, lengths, in_low, bias, pieces):
@@ -320,7 +320,7 @@
                         out_ref[k, :, there] = product[first : first + rows]
                         first += rows
 
-            loop(right_ref.shape[1], step, tile)
+            loop(right_ref.shape[1], step, tile, unroll=4 if wide or keep else 1)
             at += right_ref.shape[1]
 
     shapes = [((len(offsets), rows, total), B16) for offsets in groups]

time: 187 us -> 184 us (0.984)
  Pallas kernels: 62.4 us -> 59.3 us
    pallas_call x24, Pallas kernels: 62.4 us -> 59.3 us  [call(): pl.pallas_call(body, in_specs=[SMEM_SPEC if member.dtype == jnp.int32 and...]
  transfers between devices with their start and end apart: 48 -> 48, of which waited for: 20 -> 22; matrix products, arithmetic and copies ran while one was open for 3% -> 3% of each run, Pallas kernels for 29% -> 29%
where the time goes in v1:
time: 184 us
  Pallas kernels  59.3 us (32%)
  waiting for transfers between devices  59.1 us (32%)
  starting transfers between devices  57.7 us (31%)
  other arithmetic  6.19 us (3%)
    pallas_call x24, Pallas kernels, call(): pl.pallas_call(body, in_specs=[SMEM_SPEC if member.dtype == jnp.int32 and...  59.3 us
    ppermute x42, waiting for transfers between devices, swap(): return lax.ppermute(values, 'dp', [(i, i ^ bit) for i in range(BLOCKS)])  57.6 us
    ppermute x42, starting transfers between devices, swap(): return lax.ppermute(values, 'dp', [(i, i ^ bit) for i in range(BLOCKS)])  57 us
  transfers between devices with their start and end apart: 48, of which 22 were waited for; matrix products, arithmetic and copies ran while one was open for 3% of the time, Pallas kernels for 29%

profile of v1, /device:TPU:0, one launch (start us, length us, event | category | flops | bytes accessed | tf_op | source)
XLA Modules:
  0.0 184.0 jit_solution(14390730715365997647)
XLA Ops:
  1.5 5.1 %collective-permute-start = (bf16[48,1536]{1,0:T(8,128)(2,1)S(1)}, bf16[48,1536]{1,0:T(8,128)(2,1)S(1)}, u32[]{:S(2)}, u32[]{:S(2)}) collective-permute-start(bf16[48,1536]{1,0:T(8,128)(2,1)S(1)} %get-tuple-element.347), channel_id=1, source_target_pairs={{0,24},{2,26},{4,28},{6,30},{8,16},{10,18},{12,20},{14,22},{16,8},... | collective-permute-start | bytes 442376 | tf_op jit(solution)/shard_map/ppermute | solution.py:22
  11.0 2.7 %collective-permute-start.3 = (bf16[2,48,1536]{2,1,0:T(8,128)(2,1)S(1)}, bf16[2,48,1536]{2,1,0:T(8,128)(2,1)S(1)}, u32[]{:S(2)}, u32[]{:S(2)}) collective-permute-start(bf16[2,48,1536]{2,1,0:T(8,128)(2,1)S(1)} %pad_maximum_fusion.rest_0_), channel_id=1, source_target_pairs={{0,8},{2,10},{4,12},{6,14},{8,0},{10,2},{12,4},{14,6},{16,24},{18,... | collective-permute-start | bytes 884744 | tf_op jit(solution)/shard_map/ppermute | solution.py:22
  16.7 3.3 %collective-permute-done.3.rest_1_ = bf16[2,48,1536]{2,1,0:T(8,128)(2,1)S(1)} collective-permute-done((bf16[2,48,1536]{2,1,0:T(8,128)(2,1)S(1)}, bf16[2,48,1536]{2,1,0:T(8,128)(2,1)S(1)}, u32[]{:S(2)}, u32[]{:S(2)}) %collective-permute-start.3) | collective-permute-done | bytes 294944 | tf_op jit(solution)/shard_map/ppermute | solution.py:22
  26.4 6.1 %collective-permute-done.6 = bf16[48,1536]{1,0:T(8,128)(2,1)S(1)} collective-permute-done((bf16[48,1536]{1,0:T(8,128)(2,1)S(1)}, bf16[48,1536]{1,0:T(8,128)(2,1)S(1)}, u32[]{:S(2)}, u32[]{:S(2)}) %collective-permute-start.6) | collective-permute-done | bytes 147488 | tf_op jit(solution)/shard_map/ppermute | solution.py:22
  36.7 4.2 %collective-permute-done.9.rest_1_ = bf16[2,48,1536]{2,1,0:T(8,128)(2,1)S(1)} collective-permute-done((bf16[2,48,1536]{2,1,0:T(8,128)(2,1)S(1)}, bf16[2,48,1536]{2,1,0:T(8,128)(2,1)S(1)}, u32[]{:S(2)}, u32[]{:S(2)}) %collective-permute-start.9) | collective-permute-done | bytes 294944 | tf_op jit(solution)/shard_map/ppermute | solution.py:22
  41.8 6.0 %collective-permute-done.7.rest_7_ = bf16[2,48,1536]{2,1,0:T(8,128)(2,1)S(1)} collective-permute-done((bf16[2,48,1536]{2,1,0:T(8,128)(2,1)S(1)}, bf16[2,48,1536]{2,1,0:T(8,128)(2,1)S(1)}, u32[]{:S(2)}, u32[]{:S(2)}) %collective-permute-start.7) | collective-permute-done | bytes 294944 | tf_op jit(solution)/shard_map/ppermute | solution.py:22
  54.0 5.7 %attend.1 = (bf16[768,1536]{1,0:T(8,128)(2,1)S(1)}, bf16[1024,1152]{1,0:T(8,128)(2,1)S(1)}, bf16[1024,768]{1,0:T(8,128)(2,1)S(1)}, bf16[1024,384]{1,0:T(8,128)(2,1)S(1)}, bf16[1024,768]{1,0:T(8,128)(2,1)S(1)}) custom-call(s32[1]{0:T(128)} %bitcast.1.me_ref, s32[8]{0:T(128)S(1)} %copy-done.1, bf16[1024,768]{1,0:T(8,128)(2,1)S(1)} %broadcast_select_fusion.in_ref.refs_0_, ...), custom_call_target="tpu_custom_call" | custom-call | flops 1 | bytes 1 | tf_op jit(solution)/shard_map/attend/pallas_call | solution.py:55
  62.1 7.1 %collective-permute-done.18.rest_5_ = bf16[2,48,1536]{2,1,0:T(8,128)(2,1)S(1)} collective-permute-done((bf16[2,48,1536]{2,1,0:T(8,128)(2,1)S(1)}, bf16[2,48,1536]{2,1,0:T(8,128)(2,1)S(1)}, u32[]{:S(2)}, u32[]{:S(2)}) %collective-permute-start.18) | collective-permute-done | bytes 294944 | tf_op jit(solution)/shard_map/ppermute | solution.py:22
  73.6 6.5 %up.1 = (bf16[768,1536]{1,0:T(8,128)(2,1)S(1)}, f32[1024,768]{1,0:T(8,128)S(1)}, f32[1024,128]{1,0:T(8,128)S(1)}, bf16[1024,768]{1,0:T(8,128)(2,1)S(1)}, bf16[10...) custom-call(s32[1]{0:T(128)} %bitcast.1.me_ref, bf16[1024,768]{1,0:T(8,128)(2,1)S(1)} %broadcast_select_fusion.in_ref.refs_0_, ...), custom_call_target="tpu_custom_call" | custom-call | flops 1 | bytes 1 | tf_op jit(solution)/shard_map/up/pallas_call | solution.py:55
  87.4 2.3 %weight_grad.4 = (bf16[4,48,1536]{2,1,0:T(8,128)(2,1)S(1)}, bf16[4,48,1536]{2,1,0:T(8,128)(2,1)S(1)}, bf16[768,1024]{1,0:T(8,128)(2,1)S(1)}) custom-call(s32[1]{0:T(128)} %bitcast.1.me_ref, bf16[512,768]{1,0:T(8,128)(2,1)S(1)} %get-tuple-element.233.refs_0_.low_a_ref, bf16[512,768]{1,0:T(8,128)(2,1)S(1)} %get-tuple-element.234.refs_1_.low_b_ref, ...), custom_call_target="tpu_custom_call" | custom-call | flops 1 | bytes 1 | tf_op jit(solution)/shard_map/weight_grad/pallas_call | solution.py:55
  91.1 2.4 %weight_grad.6 = (bf16[2,48,1536]{2,1,0:T(8,128)(2,1)S(1)}, bf16[2,48,1536]{2,1,0:T(8,128)(2,1)S(1)}, bf16[4,48,1536]{2,1,0:T(8,128)(2,1)S(1)}) custom-call(s32[1]{0:T(128)} %bitcast.1.me_ref, bf16[768,1024]{1,0:T(8,128)(2,1)S(1)} %get-tuple-element.245.refs_0_, bf16[1024,1536]{1,0:T(8,128)(2,1)S(1)} %get-tuple-element.220.act_ref.refs_2_.refs_1_), custom_call_target="tpu_custom_call" | custom-call | flops 1 | bytes 1 | tf_op jit(solution)/shard_map/weight_grad/pallas_call | solution.py:55
  93.4 6.1 %hidden_back.1 = (bf16[1024,1536]{1,0:T(8,128)(2,1)S(1)}, bf16[1024,768]{1,0:T(8,128)(2,1)S(1)}, f32[8,1536]{1,0:T(8,128)S(1)}) custom-call(bf16[512,768]{1,0:T(8,128)(2,1)S(1)} %get-tuple-element.233.refs_0_.low_a_ref, bf16[512,768]{1,0:T(8,128)(2,1)S(1)} %get-tuple-element.234.refs_1_.low_b_ref, bf16[1024,1536]{1,0:T(8,128)(2,1)S(1)} %get-tuple-element.235.slope_ref, ...), custom_call_target="tpu_custom_call" | custom-call | flops 1 | bytes 1 | tf_op jit(solution)/shard_map/hidden_back/pallas_call | solution.py:55
  99.5 4.7 %weight_grad.5 = (bf16[4,48,1536]{2,1,0:T(8,128)(2,1)S(1)}, bf16[4,48,1536]{2,1,0:T(8,128)(2,1)S(1)}, bf16[2,48,1536]{2,1,0:T(8,128)(2,1)S(1)}, bf16[2,48,1536]{2,1,0:T(8,128)(2,1)S(1)}, bf16[4,48,1536]{2,1,0:T(8,128)(2,1)S(1)}) custom-call(s32[1]{0:T(128)} %bitcast.1.me_ref, bf16[1024,768]{1,0:T(8,128)(2,1)S(1)} %get-tuple-element.215.refs_0_, ...), custom_call_target="tpu_custom_call" | custom-call | flops 1 | bytes 1 | tf_op jit(solution)/shard_map/weight_grad/pallas_call | solution.py:55
  110.3 15.4 %attend_back.1 = (f32[1024,768]{1,0:T(8,128)S(1)}, bf16[1024,768]{1,0:T(8,128)(2,1)S(1)}, bf16[1024,1152]{1,0:T(8,128)(2,1)S(1)}, bf16[1024,768]{1,0:T(8,128)(2,...) custom-call(f32[512,768]{1,0:T(8,128)S(1)} %get-tuple-element.257.dz_a_ref, ...), custom_call_target="tpu_custom_call" | custom-call | flops 1 | bytes 1 | tf_op jit(solution)/shard_map/attend_back/pallas_call | solution.py:55
  125.8 2.3 %collective-permute-done.31.late_x_ref = bf16[2,48,1536]{2,1,0:T(8,128)(2,1)S(1)} collective-permute-done((bf16[2,48,1536]{2,1,0:T(8,128)(2,1)S(1)}, bf16[2,48,1536]{2,1,0:T(8,128)(2,1)S(1)}, u32[]{:S(2)}, u32[]{:S(2)}) %collective-permute-start.31) | collective-permute-done | bytes 294944 | tf_op jit(solution)/shard_map/ppermute | solution.py:22
  132.8 5.1 %weight_grad.7 = (bf16[4,48,1664]{2,1,0:T(8,128)(2,1)S(1)}, bf16[4,48,1536]{2,1,0:T(8,128)(2,1)S(1)}, bf16[2,48,1536]{2,1,0:T(8,128)(2,1)S(1)}, bf16[2,48,1536]{2,1,0:T(8,128)(2,1)S(1)}, bf16[4,48,1536]{2,1,0:T(8,128)(2,1)S(1)}) custom-call(s32[1]{0:T(128)} %bitcast.1.me_ref, bf16[1024,768]{1,0:T(8,128)(2,1)S(1)} %broadcast_select_fusion.in_ref.refs_0_, ...), custom_call_target="tpu_custom_call" | custom-call | flops 1 | bytes 1 | tf_op jit(solution)/shard_map/weight_grad/pallas_call | solution.py:55
  142.6 3.5 %collective-permute-start.41 = (bf16[48,1536]{1,0:T(8,128)(2,1)S(1)}, bf16[48,1536]{1,0:T(8,128)(2,1)S(1)}, u32[]{:S(2)}, u32[]{:S(2)}) collective-permute-start(bf16[48,1536]{1,0:T(8,128)(2,1)S(1)} %get-tuple-element.296), channel_id=1, source_target_pairs={{0,24},{2,26},{4,28},{6,30},{8,16},{10,18},{12,20},{14,22},{16,8},... | collective-permute-start | bytes 442376 | tf_op jit(solution)/shard_map/ppermute | solution.py:22
  146.1 2.8 %last.1 = (f32[1024,768]{1,0:T(8,128)}, bf16[1024,768]{1,0:T(8,128)(2,1)}) custom-call(f32[1024,768]{1,0:T(8,128)S(1)} %get-tuple-element.297.dz_ref, bf16[1024,768]{1,0:T(8,128)(2,1)S(1)} %get-tuple-element.298.own_ref, bf16[1024,768]{1,0:T(8,128)(2,1)S(1)} %collective-permute-done.42.other_ref, f32[1024,128]{1,0:T(8,128)S(1)} %broadcast_in_dim.36.flag_ref, ...), custom_call_target="tpu_custom_call" | custom-call | flops 1 | bytes 1 | tf_op jit(solution)/shard_map/last/pallas_call | solution.py:55
  148.9 7.0 %collective-permute-done.41 = bf16[48,1536]{1,0:T(8,128)(2,1)S(1)} collective-permute-done((bf16[48,1536]{1,0:T(8,128)(2,1)S(1)}, bf16[48,1536]{1,0:T(8,128)(2,1)S(1)}, u32[]{:S(2)}, u32[]{:S(2)}) %collective-permute-start.41) | collective-permute-done | bytes 147488 | tf_op jit(solution)/shard_map/ppermute | solution.py:22
  158.2 3.5 %collective-permute-start.45 = (bf16[48,1536]{1,0:T(8,128)(2,1)S(1)}, bf16[48,1536]{1,0:T(8,128)(2,1)S(1)}, u32[]{:S(2)}, u32[]{:S(2)}) collective-permute-start(bf16[48,1536]{1,0:T(8,128)(2,1)S(1)} %get-tuple-element.314), channel_id=1, source_target_pairs={{0,24},{2,26},{4,28},{6,30},{8,16},{10,18},{12,20},{14,22},{16,8},... | collective-permute-start | bytes 442376 | tf_op jit(solution)/shard_map/ppermute | solution.py:22
  161.6 3.6 %collective-permute-done.45 = bf16[48,1536]{1,0:T(8,128)(2,1)S(1)} collective-permute-done((bf16[48,1536]{1,0:T(8,128)(2,1)S(1)}, bf16[48,1536]{1,0:T(8,128)(2,1)S(1)}, u32[]{:S(2)}, u32[]{:S(2)}) %collective-permute-start.45) | collective-permute-done | bytes 147488 | tf_op jit(solution)/shard_map/ppermute | solution.py:22
  165.7 2.8 %collective-permute-start.46 = (bf16[2,48,1664]{2,1,0:T(8,128)(2,1)S(1)}, bf16[2,48,1664]{2,1,0:T(8,128)(2,1)S(1)}, u32[]{:S(2)}, u32[]{:S(2)}) collective-permute-start(bf16[2,48,1664]{2,1,0:T(8,128)(2,1)S(1)} %get-tuple-element.319), channel_id=1, source_target_pairs={{0,8},{2,10},{4,12},{6,14},{8,0},{10,2},{12,4},{14,6},{16,24},{18,... | collective-permute-start | bytes 958472 | tf_op jit(solution)/shard_map/ppermute | solution.py:22
  169.3 6.4 %collective-permute-done.46.mid_ref = bf16[2,48,1664]{2,1,0:T(8,128)(2,1)S(1)} collective-permute-done((bf16[2,48,1664]{2,1,0:T(8,128)(2,1)S(1)}, bf16[2,48,1664]{2,1,0:T(8,128)(2,1)S(1)}, u32[]{:S(2)}, u32[]{:S(2)}) %collective-permute-start.46) | collective-permute-done | bytes 319520 | tf_op jit(solution)/shard_map/ppermute | solution.py:22
  178.5 4.6 %collective-permute-done.47.far_ref = bf16[48,1792]{1,0:T(8,128)(2,1)S(1)} collective-permute-done((bf16[48,1792]{1,0:T(8,128)(2,1)S(1)}, bf16[48,1792]{1,0:T(8,128)(2,1)S(1)}, u32[]{:S(2)}, u32[]{:S(2)}) %collective-permute-start.47) | collective-permute-done | bytes 172064 | tf_op jit(solution)/shard_map/ppermute | solution.py:22
  (142 shorter events, 63.5 us)
Async XLA Ops:
  1.5 9.2 %collective-permute-start = (bf16[48,1536]{1,0:T(8,128)(2,1)S(1)}, bf16[48,1536]{1,0:T(8,128)(2,1)S(1)}, u32[]{:S(2)}, u32[]{:S(2)}) collective-permute-start(bf16[48,1536]{1,0:T(8,128)(2,1)S(1)} %get-tuple-element.347), channel_id=1, source_target_pairs={{0,24},{2,26},{4,28},{6,30},{8,16},{10,18},{12,20},{14,22},{16,8},... | collective-permute-start | bytes 442376 | tf_op jit(solution)/shard_map/ppermute | solution.py:22
  22.7 9.8 %collective-permute-start.5 = (bf16[2,48,1536]{2,1,0:T(8,128)(2,1)S(1)}, bf16[2,48,1536]{2,1,0:T(8,128)(2,1)S(1)}, u32[]{:S(2)}, u32[]{:S(2)}) collective-permute-start(bf16[2,48,1536]{2,1,0:T(8,128)(2,1)S(1)} %collective-permute-done.3.rest_1_), channel_id=1, source_target_pairs={{0,4},{2,6},{4,0},{6,2},{8,12},{10,14},{12,8},{14,10},{16,20},{18,... | collective-permute-start | bytes 884744 | tf_op jit(solution)/shard_map/ppermute | solution.py:22
  23.2 9.3 %collective-permute-start.4 = (bf16[2,48,1536]{2,1,0:T(8,128)(2,1)S(1)}, bf16[2,48,1536]{2,1,0:T(8,128)(2,1)S(1)}, u32[]{:S(2)}, u32[]{:S(2)}) collective-permute-start(bf16[2,48,1536]{2,1,0:T(8,128)(2,1)S(1)} %collective-permute-done.3.rest_1_), channel_id=1, source_target_pairs={{0,2},{2,0},{4,6},{6,4},{8,10},{10,8},{12,14},{14,12},{16,18},{18,... | collective-permute-start | bytes 884744 | tf_op jit(solution)/shard_map/ppermute | solution.py:22
  34.8 13.0 %collective-permute-start.7 = (bf16[2,48,1536]{2,1,0:T(8,128)(2,1)S(1)}, bf16[2,48,1536]{2,1,0:T(8,128)(2,1)S(1)}, u32[]{:S(2)}, u32[]{:S(2)}) collective-permute-start(bf16[2,48,1536]{2,1,0:T(8,128)(2,1)S(1)} %collective-permute-done.5.rest_5_), channel_id=1, source_target_pairs={{0,2},{2,0},{4,6},{6,4},{8,10},{10,8},{12,14},{14,12},{16,18},{18,... | collective-permute-start | bytes 884744 | tf_op jit(solution)/shard_map/ppermute | solution.py:22
  36.3 11.5 %collective-permute-start.8 = (bf16[2,48,1536]{2,1,0:T(8,128)(2,1)S(1)}, bf16[2,48,1536]{2,1,0:T(8,128)(2,1)S(1)}, u32[]{:S(2)}, u32[]{:S(2)}) collective-permute-start(bf16[2,48,1536]{2,1,0:T(8,128)(2,1)S(1)} %collective-permute-done.1.rest_2_), channel_id=1, source_target_pairs={{0,4},{2,6},{4,0},{6,2},{8,12},{10,14},{12,8},{14,10},{16,20},{18,... | collective-permute-start | bytes 884744 | tf_op jit(solution)/shard_map/ppermute | solution.py:22
  47.8 11.9 %collective-permute-start.12 = (bf16[2,48,1536]{2,1,0:T(8,128)(2,1)S(1)}, bf16[2,48,1536]{2,1,0:T(8,128)(2,1)S(1)}, u32[]{:S(2)}, u32[]{:S(2)}) collective-permute-start(bf16[2,48,1536]{2,1,0:T(8,128)(2,1)S(1)} %collective-permute-done.9.rest_1_), channel_id=1, source_target_pairs={{0,2},{2,0},{4,6},{6,4},{8,10},{10,8},{12,14},{14,12},{16,18},{18,... | collective-permute-start | bytes 884744 | tf_op jit(solution)/shard_map/ppermute | solution.py:22
  48.3 11.4 %collective-permute-start.13 = (bf16[2,48,1536]{2,1,0:T(8,128)(2,1)S(1)}, bf16[2,48,1536]{2,1,0:T(8,128)(2,1)S(1)}, u32[]{:S(2)}, u32[]{:S(2)}) collective-permute-start(bf16[2,48,1536]{2,1,0:T(8,128)(2,1)S(1)} %collective-permute-done.10.rest_2_), channel_id=1, source_target_pairs={{0,4},{2,6},{4,0},{6,2},{8,12},{10,14},{12,8},{14,10},{16,20},{18,... | collective-permute-start | bytes 884744 | tf_op jit(solution)/shard_map/ppermute | solution.py:22
  49.5 10.2 %collective-permute-start.17 = (bf16[2,48,1536]{2,1,0:T(8,128)(2,1)S(1)}, bf16[2,48,1536]{2,1,0:T(8,128)(2,1)S(1)}, u32[]{:S(2)}, u32[]{:S(2)}) collective-permute-start(bf16[2,48,1536]{2,1,0:T(8,128)(2,1)S(1)} %pad_maximum_fusion.2.rest_0_), channel_id=1, source_target_pairs={{0,4},{2,6},{4,0},{6,2},{8,12},{10,14},{12,8},{14,10},{16,20},{18,... | collective-permute-start | bytes 884744 | tf_op jit(solution)/shard_map/ppermute | solution.py:22
  50.4 9.3 %collective-permute-start.16 = (bf16[2,48,1536]{2,1,0:T(8,128)(2,1)S(1)}, bf16[2,48,1536]{2,1,0:T(8,128)(2,1)S(1)}, u32[]{:S(2)}, u32[]{:S(2)}) collective-permute-start(bf16[2,48,1536]{2,1,0:T(8,128)(2,1)S(1)} %pad_maximum_fusion.2.rest_0_), channel_id=1, source_target_pairs={{0,2},{2,0},{4,6},{6,4},{8,10},{10,8},{12,14},{14,12},{16,18},{18,... | collective-permute-start | bytes 884744 | tf_op jit(solution)/shard_map/ppermute | solution.py:22
  59.7 9.8 %collective-permute-start.21 = (bf16[1024,768]{1,0:T(8,128)(2,1)S(1)}, bf16[1024,768]{1,0:T(8,128)(2,1)S(1)}, u32[]{:S(2)}, u32[]{:S(2)}) collective-permute-start(bf16[1024,768]{1,0:T(8,128)(2,1)S(1)} %get-tuple-element.207.own_ref), channel_id=1, source_target_pairs={{0,1},{1,0},{2,3},{3,2},{4,5},{5,4},{6,7},{7,6},{8,9},{9,8},{10,11... | collective-permute-start | bytes 4718600 | tf_op jit(solution)/shard_map/ppermute | solution.py:34
  59.8 9.4 %collective-permute-start.18 = (bf16[2,48,1536]{2,1,0:T(8,128)(2,1)S(1)}, bf16[2,48,1536]{2,1,0:T(8,128)(2,1)S(1)}, u32[]{:S(2)}, u32[]{:S(2)}) collective-permute-start(bf16[2,48,1536]{2,1,0:T(8,128)(2,1)S(1)} %collective-permute-done.9.rest_1_), channel_id=1, source_target_pairs={{0,4},{2,6},{4,0},{6,2},{8,12},{10,14},{12,8},{14,10},{16,20},{18,... | collective-permute-start | bytes 884744 | tf_op jit(solution)/shard_map/ppermute | solution.py:22
  69.5 10.6 %collective-permute-start.24 = (bf16[2,48,1536]{2,1,0:T(8,128)(2,1)S(1)}, bf16[2,48,1536]{2,1,0:T(8,128)(2,1)S(1)}, u32[]{:S(2)}, u32[]{:S(2)}) collective-permute-start(bf16[2,48,1536]{2,1,0:T(8,128)(2,1)S(1)} %collective-permute-done.19.rest_6_), channel_id=1, source_target_pairs={{0,8},{2,10},{4,12},{6,14},{8,0},{10,2},{12,4},{14,6},{16,24},{18,... | collective-permute-start | bytes 884744 | tf_op jit(solution)/shard_map/ppermute | solution.py:22
  89.7 15.6 %collective-permute-start.27 = (bf16[4,48,1536]{2,1,0:T(8,128)(2,1)S(1)}, bf16[4,48,1536]{2,1,0:T(8,128)(2,1)S(1)}, u32[]{:S(2)}, u32[]{:S(2)}) collective-permute-start(bf16[4,48,1536]{2,1,0:T(8,128)(2,1)S(1)} %get-tuple-element.240), channel_id=1, source_target_pairs={{0,2},{2,0},{4,6},{6,4},{8,10},{10,8},{12,14},{14,12},{16,18},{18,... | collective-permute-start | bytes 1769480 | tf_op jit(solution)/shard_map/ppermute | solution.py:22
  90.8 15.3 %collective-permute-start.28 = (bf16[4,48,1536]{2,1,0:T(8,128)(2,1)S(1)}, bf16[4,48,1536]{2,1,0:T(8,128)(2,1)S(1)}, u32[]{:S(2)}, u32[]{:S(2)}) collective-permute-start(bf16[4,48,1536]{2,1,0:T(8,128)(2,1)S(1)} %get-tuple-element.241), channel_id=1, source_target_pairs={{0,4},{2,6},{4,0},{6,2},{8,12},{10,14},{12,8},{14,10},{16,20},{18,... | collective-permute-start | bytes 1769480 | tf_op jit(solution)/shard_map/ppermute | solution.py:22
  106.0 22.8 %collective-permute-start.29 = (bf16[4,48,1536]{2,1,0:T(8,128)(2,1)S(1)}, bf16[4,48,1536]{2,1,0:T(8,128)(2,1)S(1)}, u32[]{:S(2)}, u32[]{:S(2)}) collective-permute-start(bf16[4,48,1536]{2,1,0:T(8,128)(2,1)S(1)} %get-tuple-element.249), channel_id=1, source_target_pairs={{0,2},{2,0},{4,6},{6,4},{8,10},{10,8},{12,14},{14,12},{16,18},{18,... | collective-permute-start | bytes 1769480 | tf_op jit(solution)/shard_map/ppermute | solution.py:22
  107.0 21.8 %collective-permute-start.30 = (bf16[4,48,1536]{2,1,0:T(8,128)(2,1)S(1)}, bf16[4,48,1536]{2,1,0:T(8,128)(2,1)S(1)}, u32[]{:S(2)}, u32[]{:S(2)}) collective-permute-start(bf16[4,48,1536]{2,1,0:T(8,128)(2,1)S(1)} %get-tuple-element.250), channel_id=1, source_target_pairs={{0,4},{2,6},{4,0},{6,2},{8,12},{10,14},{12,8},{14,10},{16,20},{18,... | collective-permute-start | bytes 1769480 | tf_op jit(solution)/shard_map/ppermute | solution.py:22
  107.5 20.6 %collective-permute-start.31 = (bf16[2,48,1536]{2,1,0:T(8,128)(2,1)S(1)}, bf16[2,48,1536]{2,1,0:T(8,128)(2,1)S(1)}, u32[]{:S(2)}, u32[]{:S(2)}) collective-permute-start(bf16[2,48,1536]{2,1,0:T(8,128)(2,1)S(1)} %get-tuple-element.255), channel_id=1, source_target_pairs={{0,2},{2,0},{4,6},{6,4},{8,10},{10,8},{12,14},{14,12},{16,18},{18,... | collective-permute-start | bytes 884744 | tf_op jit(solution)/shard_map/ppermute | solution.py:22
  108.6 20.2 %collective-permute-start.32 = (bf16[2,48,1536]{2,1,0:T(8,128)(2,1)S(1)}, bf16[2,48,1536]{2,1,0:T(8,128)(2,1)S(1)}, u32[]{:S(2)}, u32[]{:S(2)}) collective-permute-start(bf16[2,48,1536]{2,1,0:T(8,128)(2,1)S(1)} %get-tuple-element.256), channel_id=1, source_target_pairs={{0,4},{2,6},{4,0},{6,2},{8,12},{10,14},{12,8},{14,10},{16,20},{18,... | collective-permute-start | bytes 884744 | tf_op jit(solution)/shard_map/ppermute | solution.py:22
  138.4 17.6 %collective-permute-start.38 = (bf16[4,48,1664]{2,1,0:T(8,128)(2,1)S(1)}, bf16[4,48,1664]{2,1,0:T(8,128)(2,1)S(1)}, u32[]{:S(2)}, u32[]{:S(2)}) collective-permute-start(bf16[4,48,1664]{2,1,0:T(8,128)(2,1)S(1)} %get-tuple-element.288), channel_id=1, source_target_pairs={{0,2},{2,0},{4,6},{6,4},{8,10},{10,8},{12,14},{14,12},{16,18},{18,... | collective-permute-start | bytes 1916936 | tf_op jit(solution)/shard_map/ppermute | solution.py:22
  139.4 16.6 %collective-permute-start.39 = (bf16[4,48,1536]{2,1,0:T(8,128)(2,1)S(1)}, bf16[4,48,1536]{2,1,0:T(8,128)(2,1)S(1)}, u32[]{:S(2)}, u32[]{:S(2)}) collective-permute-start(bf16[4,48,1536]{2,1,0:T(8,128)(2,1)S(1)} %get-tuple-element.289), channel_id=1, source_target_pairs={{0,4},{2,6},{4,0},{6,2},{8,12},{10,14},{12,8},{14,10},{16,20},{18,... | collective-permute-start | bytes 1769480 | tf_op jit(solution)/shard_map/ppermute | solution.py:22
  141.4 14.6 %collective-permute-start.40 = (bf16[2,48,1536]{2,1,0:T(8,128)(2,1)S(1)}, bf16[2,48,1536]{2,1,0:T(8,128)(2,1)S(1)}, u32[]{:S(2)}, u32[]{:S(2)}) collective-permute-start(bf16[2,48,1536]{2,1,0:T(8,128)(2,1)S(1)} %get-tuple-element.293), channel_id=1, source_target_pairs={{0,8},{2,10},{4,12},{6,14},{8,0},{10,2},{12,4},{14,6},{16,24},{18,... | collective-permute-start | bytes 884744 | tf_op jit(solution)/shard_map/ppermute | solution.py:22
  142.6 13.3 %collective-permute-start.41 = (bf16[48,1536]{1,0:T(8,128)(2,1)S(1)}, bf16[48,1536]{1,0:T(8,128)(2,1)S(1)}, u32[]{:S(2)}, u32[]{:S(2)}) collective-permute-start(bf16[48,1536]{1,0:T(8,128)(2,1)S(1)} %get-tuple-element.296), channel_id=1, source_target_pairs={{0,24},{2,26},{4,28},{6,30},{8,16},{10,18},{12,20},{14,22},{16,8},... | collective-permute-start | bytes 442376 | tf_op jit(solution)/shard_map/ppermute | solution.py:22
  156.1 9.4 %collective-permute-start.44 = (bf16[2,48,1664]{2,1,0:T(8,128)(2,1)S(1)}, bf16[2,48,1664]{2,1,0:T(8,128)(2,1)S(1)}, u32[]{:S(2)}, u32[]{:S(2)}) collective-permute-start(bf16[2,48,1664]{2,1,0:T(8,128)(2,1)S(1)} %get-tuple-element.311), channel_id=1, source_target_pairs={{0,4},{2,6},{4,0},{6,2},{8,12},{10,14},{12,8},{14,10},{16,20},{18,... | collective-permute-start | bytes 958472 | tf_op jit(solution)/shard_map/ppermute | solution.py:22
  165.7 10.0 %collective-permute-start.46 = (bf16[2,48,1664]{2,1,0:T(8,128)(2,1)S(1)}, bf16[2,48,1664]{2,1,0:T(8,128)(2,1)S(1)}, u32[]{:S(2)}, u32[]{:S(2)}) collective-permute-start(bf16[2,48,1664]{2,1,0:T(8,128)(2,1)S(1)} %get-tuple-element.319), channel_id=1, source_target_pairs={{0,8},{2,10},{4,12},{6,14},{8,0},{10,2},{12,4},{14,6},{16,24},{18,... | collective-permute-start | bytes 958472 | tf_op jit(solution)/shard_map/ppermute | solution.py:22
  (35 other events, 279.1 us)

commit v2 on v1

--- a/solution.py
+++ b/solution.py
@@ -200,7 +200,7 @@
         density = jnp.exp(pre * pre * -0.5) * 0.3989422804014327
         slope_ref[rows] = (cdf + pre * density).astype(B16)
 
-    loop(in_ref.shape[0], step)
+    loop(in_ref.shape[0], step, unroll=2)
 
 
 def up(me, in_low, own, other, vectors, bias, pieces):
@@ -320,7 +320,8 @@
                         out_ref[k, :, there] = product[first : first + rows]
                         first += rows
 
-            loop(right_ref.shape[1], step, tile, unroll=4 if wide or keep else 1)
+            count_tiles = right_ref.shape[1] // tile
+            loop(right_ref.shape[1], step, tile, unroll=count_tiles if wide or keep else 1)
             at += right_ref.shape[1]
 
     shapes = [((len(offsets), rows, total), B16) for offsets in groups]

time: 184 us -> 183 us (level)
    pallas_call x24, Pallas kernels: 59.3 us -> 57.5 us  [call(): pl.pallas_call(body, in_specs=[SMEM_SPEC if member.dtype == jnp.int32 and...]
  transfers between devices with their start and end apart: 48 -> 48, of which waited for: 22 -> 24; matrix products, arithmetic and copies ran while one was open for 3% -> 3% of each run, Pallas kernels for 29% -> 28%
where the time goes in v2:
time: 183 us
  waiting for transfers between devices  59.9 us (33%)
  starting transfers between devices  57.8 us (32%)
  Pallas kernels  57.5 us (31%)
  other arithmetic  6.19 us (3%)
    ppermute x42, waiting for transfers between devices, swap(): return lax.ppermute(values, 'dp', [(i, i ^ bit) for i in range(BLOCKS)])  58.4 us
    pallas_call x24, Pallas kernels, call(): pl.pallas_call(body, in_specs=[SMEM_SPEC if member.dtype == jnp.int32 and...  57.5 us
    ppermute x42, starting transfers between devices, swap(): return lax.ppermute(values, 'dp', [(i, i ^ bit) for i in range(BLOCKS)])  57.1 us
  transfers between devices with their start and end apart: 48, of which 24 were waited for; matrix products, arithmetic and copies ran while one was open for 3% of the time, Pallas kernels for 28%

profile of v2, /device:TPU:0, one launch (start us, length us, event | category | flops | bytes accessed | tf_op | source)
XLA Modules:
  0.0 183.1 jit_solution(5444362913763693726)
XLA Ops:
  1.5 5.1 %collective-permute-start = (bf16[48,1536]{1,0:T(8,128)(2,1)S(1)}, bf16[48,1536]{1,0:T(8,128)(2,1)S(1)}, u32[]{:S(2)}, u32[]{:S(2)}) collective-permute-start(bf16[48,1536]{1,0:T(8,128)(2,1)S(1)} %get-tuple-element.347), channel_id=1, source_target_pairs={{0,24},{2,26},{4,28},{6,30},{8,16},{10,18},{12,20},{14,22},{16,8},... | collective-permute-start | bytes 442376 | tf_op jit(solution)/shard_map/ppermute | solution.py:22
  11.0 2.7 %collective-permute-start.3 = (bf16[2,48,1536]{2,1,0:T(8,128)(2,1)S(1)}, bf16[2,48,1536]{2,1,0:T(8,128)(2,1)S(1)}, u32[]{:S(2)}, u32[]{:S(2)}) collective-permute-start(bf16[2,48,1536]{2,1,0:T(8,128)(2,1)S(1)} %pad_maximum_fusion.rest_0_), channel_id=1, source_target_pairs={{0,8},{2,10},{4,12},{6,14},{8,0},{10,2},{12,4},{14,6},{16,24},{18,... | collective-permute-start | bytes 884744 | tf_op jit(solution)/shard_map/ppermute | solution.py:22
  16.7 3.3 %collective-permute-done.3.rest_1_ = bf16[2,48,1536]{2,1,0:T(8,128)(2,1)S(1)} collective-permute-done((bf16[2,48,1536]{2,1,0:T(8,128)(2,1)S(1)}, bf16[2,48,1536]{2,1,0:T(8,128)(2,1)S(1)}, u32[]{:S(2)}, u32[]{:S(2)}) %collective-permute-start.3) | collective-permute-done | bytes 294944 | tf_op jit(solution)/shard_map/ppermute | solution.py:22
  26.4 6.1 %collective-permute-done.6 = bf16[48,1536]{1,0:T(8,128)(2,1)S(1)} collective-permute-done((bf16[48,1536]{1,0:T(8,128)(2,1)S(1)}, bf16[48,1536]{1,0:T(8,128)(2,1)S(1)}, u32[]{:S(2)}, u32[]{:S(2)}) %collective-permute-start.6) | collective-permute-done | bytes 147488 | tf_op jit(solution)/shard_map/ppermute | solution.py:22
  36.7 4.2 %collective-permute-done.9.rest_1_ = bf16[2,48,1536]{2,1,0:T(8,128)(2,1)S(1)} collective-permute-done((bf16[2,48,1536]{2,1,0:T(8,128)(2,1)S(1)}, bf16[2,48,1536]{2,1,0:T(8,128)(2,1)S(1)}, u32[]{:S(2)}, u32[]{:S(2)}) %collective-permute-start.9) | collective-permute-done | bytes 294944 | tf_op jit(solution)/shard_map/ppermute | solution.py:22
  41.8 6.0 %collective-permute-done.7.rest_7_ = bf16[2,48,1536]{2,1,0:T(8,128)(2,1)S(1)} collective-permute-done((bf16[2,48,1536]{2,1,0:T(8,128)(2,1)S(1)}, bf16[2,48,1536]{2,1,0:T(8,128)(2,1)S(1)}, u32[]{:S(2)}, u32[]{:S(2)}) %collective-permute-start.7) | collective-permute-done | bytes 294944 | tf_op jit(solution)/shard_map/ppermute | solution.py:22
  54.0 5.7 %attend.1 = (bf16[768,1536]{1,0:T(8,128)(2,1)S(1)}, bf16[1024,1152]{1,0:T(8,128)(2,1)S(1)}, bf16[1024,768]{1,0:T(8,128)(2,1)S(1)}, bf16[1024,384]{1,0:T(8,128)(2,1)S(1)}, bf16[1024,768]{1,0:T(8,128)(2,1)S(1)}) custom-call(s32[1]{0:T(128)} %bitcast.1.me_ref, s32[8]{0:T(128)S(1)} %copy-done.1, bf16[1024,768]{1,0:T(8,128)(2,1)S(1)} %broadcast_select_fusion.in_ref.refs_0_, ...), custom_call_target="tpu_custom_call" | custom-call | flops 1 | bytes 1 | tf_op jit(solution)/shard_map/attend/pallas_call | solution.py:55
  62.1 7.1 %collective-permute-done.18.rest_5_ = bf16[2,48,1536]{2,1,0:T(8,128)(2,1)S(1)} collective-permute-done((bf16[2,48,1536]{2,1,0:T(8,128)(2,1)S(1)}, bf16[2,48,1536]{2,1,0:T(8,128)(2,1)S(1)}, u32[]{:S(2)}, u32[]{:S(2)}) %collective-permute-start.18) | collective-permute-done | bytes 294944 | tf_op jit(solution)/shard_map/ppermute | solution.py:22
  73.6 5.8 %up.1 = (bf16[768,1536]{1,0:T(8,128)(2,1)S(1)}, f32[1024,768]{1,0:T(8,128)S(1)}, f32[1024,128]{1,0:T(8,128)S(1)}, bf16[1024,768]{1,0:T(8,128)(2,1)S(1)}, bf16[10...) custom-call(s32[1]{0:T(128)} %bitcast.1.me_ref, bf16[1024,768]{1,0:T(8,128)(2,1)S(1)} %broadcast_select_fusion.in_ref.refs_0_, ...), custom_call_target="tpu_custom_call" | custom-call | flops 1 | bytes 1 | tf_op jit(solution)/shard_map/up/pallas_call | solution.py:55
  90.9 2.4 %weight_grad.6 = (bf16[2,48,1536]{2,1,0:T(8,128)(2,1)S(1)}, bf16[2,48,1536]{2,1,0:T(8,128)(2,1)S(1)}, bf16[4,48,1536]{2,1,0:T(8,128)(2,1)S(1)}) custom-call(s32[1]{0:T(128)} %bitcast.1.me_ref, bf16[768,1024]{1,0:T(8,128)(2,1)S(1)} %get-tuple-element.245.refs_0_, bf16[1024,1536]{1,0:T(8,128)(2,1)S(1)} %get-tuple-element.220.act_ref.refs_2_.refs_1_), custom_call_target="tpu_custom_call" | custom-call | flops 1 | bytes 1 | tf_op jit(solution)/shard_map/weight_grad/pallas_call | solution.py:55
  93.3 6.3 %hidden_back.1 = (bf16[1024,1536]{1,0:T(8,128)(2,1)S(1)}, bf16[1024,768]{1,0:T(8,128)(2,1)S(1)}, f32[8,1536]{1,0:T(8,128)S(1)}) custom-call(bf16[512,768]{1,0:T(8,128)(2,1)S(1)} %get-tuple-element.233.refs_0_.low_a_ref, bf16[512,768]{1,0:T(8,128)(2,1)S(1)} %get-tuple-element.234.refs_1_.low_b_ref, bf16[1024,1536]{1,0:T(8,128)(2,1)S(1)} %get-tuple-element.235.slope_ref, ...), custom_call_target="tpu_custom_call" | custom-call | flops 1 | bytes 1 | tf_op jit(solution)/shard_map/hidden_back/pallas_call | solution.py:55
  99.6 4.5 %weight_grad.5 = (bf16[4,48,1536]{2,1,0:T(8,128)(2,1)S(1)}, bf16[4,48,1536]{2,1,0:T(8,128)(2,1)S(1)}, bf16[2,48,1536]{2,1,0:T(8,128)(2,1)S(1)}, bf16[2,48,1536]{2,1,0:T(8,128)(2,1)S(1)}, bf16[4,48,1536]{2,1,0:T(8,128)(2,1)S(1)}) custom-call(s32[1]{0:T(128)} %bitcast.1.me_ref, bf16[1024,768]{1,0:T(8,128)(2,1)S(1)} %get-tuple-element.215.refs_0_, ...), custom_call_target="tpu_custom_call" | custom-call | flops 1 | bytes 1 | tf_op jit(solution)/shard_map/weight_grad/pallas_call | solution.py:55
  110.2 15.4 %attend_back.1 = (f32[1024,768]{1,0:T(8,128)S(1)}, bf16[1024,768]{1,0:T(8,128)(2,1)S(1)}, bf16[1024,1152]{1,0:T(8,128)(2,1)S(1)}, bf16[1024,768]{1,0:T(8,128)(2,...) custom-call(f32[512,768]{1,0:T(8,128)S(1)} %get-tuple-element.257.dz_a_ref, ...), custom_call_target="tpu_custom_call" | custom-call | flops 1 | bytes 1 | tf_op jit(solution)/shard_map/attend_back/pallas_call | solution.py:55
  125.6 2.4 %collective-permute-done.31.late_x_ref = bf16[2,48,1536]{2,1,0:T(8,128)(2,1)S(1)} collective-permute-done((bf16[2,48,1536]{2,1,0:T(8,128)(2,1)S(1)}, bf16[2,48,1536]{2,1,0:T(8,128)(2,1)S(1)}, u32[]{:S(2)}, u32[]{:S(2)}) %collective-permute-start.31) | collective-permute-done | bytes 294944 | tf_op jit(solution)/shard_map/ppermute | solution.py:22
  132.8 3.9 %weight_grad.7 = (bf16[4,48,1664]{2,1,0:T(8,128)(2,1)S(1)}, bf16[4,48,1536]{2,1,0:T(8,128)(2,1)S(1)}, bf16[2,48,1536]{2,1,0:T(8,128)(2,1)S(1)}, bf16[2,48,1536]{2,1,0:T(8,128)(2,1)S(1)}, bf16[4,48,1536]{2,1,0:T(8,128)(2,1)S(1)}) custom-call(s32[1]{0:T(128)} %bitcast.1.me_ref, bf16[1024,768]{1,0:T(8,128)(2,1)S(1)} %broadcast_select_fusion.in_ref.refs_0_, ...), custom_call_target="tpu_custom_call" | custom-call | flops 1 | bytes 1 | tf_op jit(solution)/shard_map/weight_grad/pallas_call | solution.py:55
  142.1 3.5 %collective-permute-start.41 = (bf16[48,1536]{1,0:T(8,128)(2,1)S(1)}, bf16[48,1536]{1,0:T(8,128)(2,1)S(1)}, u32[]{:S(2)}, u32[]{:S(2)}) collective-permute-start(bf16[48,1536]{1,0:T(8,128)(2,1)S(1)} %get-tuple-element.296), channel_id=1, source_target_pairs={{0,24},{2,26},{4,28},{6,30},{8,16},{10,18},{12,20},{14,22},{16,8},... | collective-permute-start | bytes 442376 | tf_op jit(solution)/shard_map/ppermute | solution.py:22
  145.5 2.8 %last.1 = (f32[1024,768]{1,0:T(8,128)}, bf16[1024,768]{1,0:T(8,128)(2,1)}) custom-call(f32[1024,768]{1,0:T(8,128)S(1)} %get-tuple-element.297.dz_ref, bf16[1024,768]{1,0:T(8,128)(2,1)S(1)} %get-tuple-element.298.own_ref, bf16[1024,768]{1,0:T(8,128)(2,1)S(1)} %collective-permute-done.42.other_ref, f32[1024,128]{1,0:T(8,128)S(1)} %broadcast_in_dim.36.flag_ref, ...), custom_call_target="tpu_custom_call" | custom-call | flops 1 | bytes 1 | tf_op jit(solution)/shard_map/last/pallas_call | solution.py:55
  148.4 7.0 %collective-permute-done.41 = bf16[48,1536]{1,0:T(8,128)(2,1)S(1)} collective-permute-done((bf16[48,1536]{1,0:T(8,128)(2,1)S(1)}, bf16[48,1536]{1,0:T(8,128)(2,1)S(1)}, u32[]{:S(2)}, u32[]{:S(2)}) %collective-permute-start.41) | collective-permute-done | bytes 147488 | tf_op jit(solution)/shard_map/ppermute | solution.py:22
  158.0 3.5 %collective-permute-start.45 = (bf16[48,1536]{1,0:T(8,128)(2,1)S(1)}, bf16[48,1536]{1,0:T(8,128)(2,1)S(1)}, u32[]{:S(2)}, u32[]{:S(2)}) collective-permute-start(bf16[48,1536]{1,0:T(8,128)(2,1)S(1)} %get-tuple-element.314), channel_id=1, source_target_pairs={{0,24},{2,26},{4,28},{6,30},{8,16},{10,18},{12,20},{14,22},{16,8},... | collective-permute-start | bytes 442376 | tf_op jit(solution)/shard_map/ppermute | solution.py:22
  161.5 3.6 %collective-permute-done.45 = bf16[48,1536]{1,0:T(8,128)(2,1)S(1)} collective-permute-done((bf16[48,1536]{1,0:T(8,128)(2,1)S(1)}, bf16[48,1536]{1,0:T(8,128)(2,1)S(1)}, u32[]{:S(2)}, u32[]{:S(2)}) %collective-permute-start.45) | collective-permute-done | bytes 147488 | tf_op jit(solution)/shard_map/ppermute | solution.py:22
  165.6 2.3 %collective-permute-start.46 = (bf16[2,48,1664]{2,1,0:T(8,128)(2,1)S(1)}, bf16[2,48,1664]{2,1,0:T(8,128)(2,1)S(1)}, u32[]{:S(2)}, u32[]{:S(2)}) collective-permute-start(bf16[2,48,1664]{2,1,0:T(8,128)(2,1)S(1)} %get-tuple-element.319), channel_id=1, source_target_pairs={{0,8},{2,10},{4,12},{6,14},{8,0},{10,2},{12,4},{14,6},{16,24},{18,... | collective-permute-start | bytes 958472 | tf_op jit(solution)/shard_map/ppermute | solution.py:22
  168.7 6.0 %collective-permute-done.46.mid_ref = bf16[2,48,1664]{2,1,0:T(8,128)(2,1)S(1)} collective-permute-done((bf16[2,48,1664]{2,1,0:T(8,128)(2,1)S(1)}, bf16[2,48,1664]{2,1,0:T(8,128)(2,1)S(1)}, u32[]{:S(2)}, u32[]{:S(2)}) %collective-permute-start.46) | collective-permute-done | bytes 319520 | tf_op jit(solution)/shard_map/ppermute | solution.py:22
  174.8 2.4 %collective-permute-start.47 = (bf16[48,1792]{1,0:T(8,128)(2,1)S(1)}, bf16[48,1792]{1,0:T(8,128)(2,1)S(1)}, u32[]{:S(2)}, u32[]{:S(2)}) collective-permute-start(bf16[48,1792]{1,0:T(8,128)(2,1)S(1)} %get-tuple-element.325), channel_id=1, source_target_pairs={{0,24},{2,26},{4,28},{6,30},{8,16},{10,18},{12,20},{14,22},{16,8},... | collective-permute-start | bytes 516104 | tf_op jit(solution)/shard_map/ppermute | solution.py:22
  177.9 4.2 %collective-permute-done.47.far_ref = bf16[48,1792]{1,0:T(8,128)(2,1)S(1)} collective-permute-done((bf16[48,1792]{1,0:T(8,128)(2,1)S(1)}, bf16[48,1792]{1,0:T(8,128)(2,1)S(1)}, u32[]{:S(2)}, u32[]{:S(2)}) %collective-permute-start.47) | collective-permute-done | bytes 172064 | tf_op jit(solution)/shard_map/ppermute | solution.py:22
  (142 shorter events, 65.5 us)
Async XLA Ops:
  1.5 9.2 %collective-permute-start = (bf16[48,1536]{1,0:T(8,128)(2,1)S(1)}, bf16[48,1536]{1,0:T(8,128)(2,1)S(1)}, u32[]{:S(2)}, u32[]{:S(2)}) collective-permute-start(bf16[48,1536]{1,0:T(8,128)(2,1)S(1)} %get-tuple-element.347), channel_id=1, source_target_pairs={{0,24},{2,26},{4,28},{6,30},{8,16},{10,18},{12,20},{14,22},{16,8},... | collective-permute-start | bytes 442376 | tf_op jit(solution)/shard_map/ppermute | solution.py:22
  22.7 9.8 %collective-permute-start.5 = (bf16[2,48,1536]{2,1,0:T(8,128)(2,1)S(1)}, bf16[2,48,1536]{2,1,0:T(8,128)(2,1)S(1)}, u32[]{:S(2)}, u32[]{:S(2)}) collective-permute-start(bf16[2,48,1536]{2,1,0:T(8,128)(2,1)S(1)} %collective-permute-done.3.rest_1_), channel_id=1, source_target_pairs={{0,4},{2,6},{4,0},{6,2},{8,12},{10,14},{12,8},{14,10},{16,20},{18,... | collective-permute-start | bytes 884744 | tf_op jit(solution)/shard_map/ppermute | solution.py:22
  23.2 9.3 %collective-permute-start.4 = (bf16[2,48,1536]{2,1,0:T(8,128)(2,1)S(1)}, bf16[2,48,1536]{2,1,0:T(8,128)(2,1)S(1)}, u32[]{:S(2)}, u32[]{:S(2)}) collective-permute-start(bf16[2,48,1536]{2,1,0:T(8,128)(2,1)S(1)} %collective-permute-done.3.rest_1_), channel_id=1, source_target_pairs={{0,2},{2,0},{4,6},{6,4},{8,10},{10,8},{12,14},{14,12},{16,18},{18,... | collective-permute-start | bytes 884744 | tf_op jit(solution)/shard_map/ppermute | solution.py:22
  32.6 9.2 %collective-permute-start.11 = (bf16[2,48,1536]{2,1,0:T(8,128)(2,1)S(1)}, bf16[2,48,1536]{2,1,0:T(8,128)(2,1)S(1)}, u32[]{:S(2)}, u32[]{:S(2)}) collective-permute-start(bf16[2,48,1536]{2,1,0:T(8,128)(2,1)S(1)} %pad_maximum_fusion.1.rest_0_), channel_id=1, source_target_pairs={{0,4},{2,6},{4,0},{6,2},{8,12},{10,14},{12,8},{14,10},{16,20},{18,... | collective-permute-start | bytes 884744 | tf_op jit(solution)/shard_map/ppermute | solution.py:22
  34.8 13.0 %collective-permute-start.7 = (bf16[2,48,1536]{2,1,0:T(8,128)(2,1)S(1)}, bf16[2,48,1536]{2,1,0:T(8,128)(2,1)S(1)}, u32[]{:S(2)}, u32[]{:S(2)}) collective-permute-start(bf16[2,48,1536]{2,1,0:T(8,128)(2,1)S(1)} %collective-permute-done.5.rest_5_), channel_id=1, source_target_pairs={{0,2},{2,0},{4,6},{6,4},{8,10},{10,8},{12,14},{14,12},{16,18},{18,... | collective-permute-start | bytes 884744 | tf_op jit(solution)/shard_map/ppermute | solution.py:22
  36.3 11.5 %collective-permute-start.8 = (bf16[2,48,1536]{2,1,0:T(8,128)(2,1)S(1)}, bf16[2,48,1536]{2,1,0:T(8,128)(2,1)S(1)}, u32[]{:S(2)}, u32[]{:S(2)}) collective-permute-start(bf16[2,48,1536]{2,1,0:T(8,128)(2,1)S(1)} %collective-permute-done.1.rest_2_), channel_id=1, source_target_pairs={{0,4},{2,6},{4,0},{6,2},{8,12},{10,14},{12,8},{14,10},{16,20},{18,... | collective-permute-start | bytes 884744 | tf_op jit(solution)/shard_map/ppermute | solution.py:22
  47.8 11.9 %collective-permute-start.12 = (bf16[2,48,1536]{2,1,0:T(8,128)(2,1)S(1)}, bf16[2,48,1536]{2,1,0:T(8,128)(2,1)S(1)}, u32[]{:S(2)}, u32[]{:S(2)}) collective-permute-start(bf16[2,48,1536]{2,1,0:T(8,128)(2,1)S(1)} %collective-permute-done.9.rest_1_), channel_id=1, source_target_pairs={{0,2},{2,0},{4,6},{6,4},{8,10},{10,8},{12,14},{14,12},{16,18},{18,... | collective-permute-start | bytes 884744 | tf_op jit(solution)/shard_map/ppermute | solution.py:22
  48.3 11.4 %collective-permute-start.13 = (bf16[2,48,1536]{2,1,0:T(8,128)(2,1)S(1)}, bf16[2,48,1536]{2,1,0:T(8,128)(2,1)S(1)}, u32[]{:S(2)}, u32[]{:S(2)}) collective-permute-start(bf16[2,48,1536]{2,1,0:T(8,128)(2,1)S(1)} %collective-permute-done.10.rest_2_), channel_id=1, source_target_pairs={{0,4},{2,6},{4,0},{6,2},{8,12},{10,14},{12,8},{14,10},{16,20},{18,... | collective-permute-start | bytes 884744 | tf_op jit(solution)/shard_map/ppermute | solution.py:22
  49.5 10.2 %collective-permute-start.17 = (bf16[2,48,1536]{2,1,0:T(8,128)(2,1)S(1)}, bf16[2,48,1536]{2,1,0:T(8,128)(2,1)S(1)}, u32[]{:S(2)}, u32[]{:S(2)}) collective-permute-start(bf16[2,48,1536]{2,1,0:T(8,128)(2,1)S(1)} %pad_maximum_fusion.2.rest_0_), channel_id=1, source_target_pairs={{0,4},{2,6},{4,0},{6,2},{8,12},{10,14},{12,8},{14,10},{16,20},{18,... | collective-permute-start | bytes 884744 | tf_op jit(solution)/shard_map/ppermute | solution.py:22
  50.4 9.3 %collective-permute-start.16 = (bf16[2,48,1536]{2,1,0:T(8,128)(2,1)S(1)}, bf16[2,48,1536]{2,1,0:T(8,128)(2,1)S(1)}, u32[]{:S(2)}, u32[]{:S(2)}) collective-permute-start(bf16[2,48,1536]{2,1,0:T(8,128)(2,1)S(1)} %pad_maximum_fusion.2.rest_0_), channel_id=1, source_target_pairs={{0,2},{2,0},{4,6},{6,4},{8,10},{10,8},{12,14},{14,12},{16,18},{18,... | collective-permute-start | bytes 884744 | tf_op jit(solution)/shard_map/ppermute | solution.py:22
  59.7 9.8 %collective-permute-start.21 = (bf16[1024,768]{1,0:T(8,128)(2,1)S(1)}, bf16[1024,768]{1,0:T(8,128)(2,1)S(1)}, u32[]{:S(2)}, u32[]{:S(2)}) collective-permute-start(bf16[1024,768]{1,0:T(8,128)(2,1)S(1)} %get-tuple-element.207.own_ref), channel_id=1, source_target_pairs={{0,1},{1,0},{2,3},{3,2},{4,5},{5,4},{6,7},{7,6},{8,9},{9,8},{10,11... | collective-permute-start | bytes 4718600 | tf_op jit(solution)/shard_map/ppermute | solution.py:34
  59.8 9.4 %collective-permute-start.18 = (bf16[2,48,1536]{2,1,0:T(8,128)(2,1)S(1)}, bf16[2,48,1536]{2,1,0:T(8,128)(2,1)S(1)}, u32[]{:S(2)}, u32[]{:S(2)}) collective-permute-start(bf16[2,48,1536]{2,1,0:T(8,128)(2,1)S(1)} %collective-permute-done.9.rest_1_), channel_id=1, source_target_pairs={{0,4},{2,6},{4,0},{6,2},{8,12},{10,14},{12,8},{14,10},{16,20},{18,... | collective-permute-start | bytes 884744 | tf_op jit(solution)/shard_map/ppermute | solution.py:22
  69.5 10.0 %collective-permute-start.24 = (bf16[2,48,1536]{2,1,0:T(8,128)(2,1)S(1)}, bf16[2,48,1536]{2,1,0:T(8,128)(2,1)S(1)}, u32[]{:S(2)}, u32[]{:S(2)}) collective-permute-start(bf16[2,48,1536]{2,1,0:T(8,128)(2,1)S(1)} %collective-permute-done.19.rest_6_), channel_id=1, source_target_pairs={{0,8},{2,10},{4,12},{6,14},{8,0},{10,2},{12,4},{14,6},{16,24},{18,... | collective-permute-start | bytes 884744 | tf_op jit(solution)/shard_map/ppermute | solution.py:22
  89.5 15.6 %collective-permute-start.27 = (bf16[4,48,1536]{2,1,0:T(8,128)(2,1)S(1)}, bf16[4,48,1536]{2,1,0:T(8,128)(2,1)S(1)}, u32[]{:S(2)}, u32[]{:S(2)}) collective-permute-start(bf16[4,48,1536]{2,1,0:T(8,128)(2,1)S(1)} %get-tuple-element.240), channel_id=1, source_target_pairs={{0,2},{2,0},{4,6},{6,4},{8,10},{10,8},{12,14},{14,12},{16,18},{18,... | collective-permute-start | bytes 1769480 | tf_op jit(solution)/shard_map/ppermute | solution.py:22
  90.6 15.3 %collective-permute-start.28 = (bf16[4,48,1536]{2,1,0:T(8,128)(2,1)S(1)}, bf16[4,48,1536]{2,1,0:T(8,128)(2,1)S(1)}, u32[]{:S(2)}, u32[]{:S(2)}) collective-permute-start(bf16[4,48,1536]{2,1,0:T(8,128)(2,1)S(1)} %get-tuple-element.241), channel_id=1, source_target_pairs={{0,4},{2,6},{4,0},{6,2},{8,12},{10,14},{12,8},{14,10},{16,20},{18,... | collective-permute-start | bytes 1769480 | tf_op jit(solution)/shard_map/ppermute | solution.py:22
  105.9 22.7 %collective-permute-start.29 = (bf16[4,48,1536]{2,1,0:T(8,128)(2,1)S(1)}, bf16[4,48,1536]{2,1,0:T(8,128)(2,1)S(1)}, u32[]{:S(2)}, u32[]{:S(2)}) collective-permute-start(bf16[4,48,1536]{2,1,0:T(8,128)(2,1)S(1)} %get-tuple-element.249), channel_id=1, source_target_pairs={{0,2},{2,0},{4,6},{6,4},{8,10},{10,8},{12,14},{14,12},{16,18},{18,... | collective-permute-start | bytes 1769480 | tf_op jit(solution)/shard_map/ppermute | solution.py:22
  106.9 21.8 %collective-permute-start.30 = (bf16[4,48,1536]{2,1,0:T(8,128)(2,1)S(1)}, bf16[4,48,1536]{2,1,0:T(8,128)(2,1)S(1)}, u32[]{:S(2)}, u32[]{:S(2)}) collective-permute-start(bf16[4,48,1536]{2,1,0:T(8,128)(2,1)S(1)} %get-tuple-element.250), channel_id=1, source_target_pairs={{0,4},{2,6},{4,0},{6,2},{8,12},{10,14},{12,8},{14,10},{16,20},{18,... | collective-permute-start | bytes 1769480 | tf_op jit(solution)/shard_map/ppermute | solution.py:22
  107.3 20.7 %collective-permute-start.31 = (bf16[2,48,1536]{2,1,0:T(8,128)(2,1)S(1)}, bf16[2,48,1536]{2,1,0:T(8,128)(2,1)S(1)}, u32[]{:S(2)}, u32[]{:S(2)}) collective-permute-start(bf16[2,48,1536]{2,1,0:T(8,128)(2,1)S(1)} %get-tuple-element.255), channel_id=1, source_target_pairs={{0,2},{2,0},{4,6},{6,4},{8,10},{10,8},{12,14},{14,12},{16,18},{18,... | collective-permute-start | bytes 884744 | tf_op jit(solution)/shard_map/ppermute | solution.py:22
  108.5 20.2 %collective-permute-start.32 = (bf16[2,48,1536]{2,1,0:T(8,128)(2,1)S(1)}, bf16[2,48,1536]{2,1,0:T(8,128)(2,1)S(1)}, u32[]{:S(2)}, u32[]{:S(2)}) collective-permute-start(bf16[2,48,1536]{2,1,0:T(8,128)(2,1)S(1)} %get-tuple-element.256), channel_id=1, source_target_pairs={{0,4},{2,6},{4,0},{6,2},{8,12},{10,14},{12,8},{14,10},{16,20},{18,... | collective-permute-start | bytes 884744 | tf_op jit(solution)/shard_map/ppermute | solution.py:22
  138.3 17.1 %collective-permute-start.38 = (bf16[4,48,1664]{2,1,0:T(8,128)(2,1)S(1)}, bf16[4,48,1664]{2,1,0:T(8,128)(2,1)S(1)}, u32[]{:S(2)}, u32[]{:S(2)}) collective-permute-start(bf16[4,48,1664]{2,1,0:T(8,128)(2,1)S(1)} %get-tuple-element.288), channel_id=1, source_target_pairs={{0,2},{2,0},{4,6},{6,4},{8,10},{10,8},{12,14},{14,12},{16,18},{18,... | collective-permute-start | bytes 1916936 | tf_op jit(solution)/shard_map/ppermute | solution.py:22
  139.3 16.1 %collective-permute-start.39 = (bf16[4,48,1536]{2,1,0:T(8,128)(2,1)S(1)}, bf16[4,48,1536]{2,1,0:T(8,128)(2,1)S(1)}, u32[]{:S(2)}, u32[]{:S(2)}) collective-permute-start(bf16[4,48,1536]{2,1,0:T(8,128)(2,1)S(1)} %get-tuple-element.289), channel_id=1, source_target_pairs={{0,4},{2,6},{4,0},{6,2},{8,12},{10,14},{12,8},{14,10},{16,20},{18,... | collective-permute-start | bytes 1769480 | tf_op jit(solution)/shard_map/ppermute | solution.py:22
  141.2 14.2 %collective-permute-start.40 = (bf16[2,48,1536]{2,1,0:T(8,128)(2,1)S(1)}, bf16[2,48,1536]{2,1,0:T(8,128)(2,1)S(1)}, u32[]{:S(2)}, u32[]{:S(2)}) collective-permute-start(bf16[2,48,1536]{2,1,0:T(8,128)(2,1)S(1)} %get-tuple-element.293), channel_id=1, source_target_pairs={{0,8},{2,10},{4,12},{6,14},{8,0},{10,2},{12,4},{14,6},{16,24},{18,... | collective-permute-start | bytes 884744 | tf_op jit(solution)/shard_map/ppermute | solution.py:22
  142.1 13.3 %collective-permute-start.41 = (bf16[48,1536]{1,0:T(8,128)(2,1)S(1)}, bf16[48,1536]{1,0:T(8,128)(2,1)S(1)}, u32[]{:S(2)}, u32[]{:S(2)}) collective-permute-start(bf16[48,1536]{1,0:T(8,128)(2,1)S(1)} %get-tuple-element.296), channel_id=1, source_target_pairs={{0,24},{2,26},{4,28},{6,30},{8,16},{10,18},{12,20},{14,22},{16,8},... | collective-permute-start | bytes 442376 | tf_op jit(solution)/shard_map/ppermute | solution.py:22
  155.5 9.8 %collective-permute-start.44 = (bf16[2,48,1664]{2,1,0:T(8,128)(2,1)S(1)}, bf16[2,48,1664]{2,1,0:T(8,128)(2,1)S(1)}, u32[]{:S(2)}, u32[]{:S(2)}) collective-permute-start(bf16[2,48,1664]{2,1,0:T(8,128)(2,1)S(1)} %get-tuple-element.311), channel_id=1, source_target_pairs={{0,4},{2,6},{4,0},{6,2},{8,12},{10,14},{12,8},{14,10},{16,20},{18,... | collective-permute-start | bytes 958472 | tf_op jit(solution)/shard_map/ppermute | solution.py:22
  (35 other events, 277.2 us)

commit v3 on v2

--- a/solution.py
+++ b/solution.py
@@ -509,34 +509,26 @@
         + from_x_ref[2:, :, :cols].astype(F32)
         + late_y_ref[:, :, :cols].astype(F32)
     )
-    mid_ref[:, :, :cols] = (
+    mid_ref[...] = (
         own_ref[2:].astype(F32) + late_x_ref[...].astype(F32) + from_y_ref[2:].astype(F32)
     ).astype(B16)
-    vector = (v_ref[...].astype(F32) + late_y_ref[:, :, cols:].astype(F32)).astype(B16)
-    mid_ref[:, :, cols:] = vector
-    vector_ref[...] = vector
-
-
-def mid_vector_body(near_ref, mid_ref, v_ref, own_ref, far_ref, vector_ref):
-    cols = own_ref.shape[1]
-    own_ref[...] = near_ref[0] + mid_ref[0, :, :cols].astype(F32)
-    far_ref[:, :cols] = (near_ref[1] + mid_ref[1, :, :cols].astype(F32)).astype(B16)
-    vector = (v_ref[...].astype(F32) + mid_ref[:, :, cols:].astype(F32)).astype(B16)
-    for k in range(2):
-        far_ref[:, cols + 128 * k : cols + 128 * (k + 1)] = vector[k]
-    vector_ref[...] = vector
-
-
-def far_vector_body(own_ref, far_ref, v_ref, *outs):
+    vector_ref[...] = (v_ref[...].astype(F32) + late_y_ref[:, :, cols:].astype(F32)).astype(B16)
+
+
+def mid_vector_body(near_ref, mid_ref, v_ref, from_ref, own_ref, far_ref, vector_ref):
+    own_ref[...] = near_ref[0] + mid_ref[0].astype(F32)
+    far_ref[...] = (near_ref[1] + mid_ref[1].astype(F32)).astype(B16)
+    vector_ref[...] = (v_ref[...].astype(F32) + from_ref[...].astype(F32)).astype(B16)
+
+
+def far_vector_body(own_ref, far_ref, v_ref, from_ref, *outs):
     rows, cols = own_ref.shape
     part = cols // 4
     for k in range(4):
         lanes = slice(k * part, (k + 1) * part)
         outs[k][...] = own_ref[:, lanes] + far_ref[:, lanes].astype(F32)
     place = 0
-    joined = [
-        v_ref[k].astype(F32) + far_ref[:, cols + 128 * k : cols + 128 * (k + 1)].astype(F32) for k in range(2)
-    ]
+    joined = [v_ref[k].astype(F32) + from_ref[k].astype(F32) for k in range(2)]
     for out_ref in outs[4:]:
         for k in range(out_ref.shape[0]):
             out_ref[k : k + 1] = joined[place // rows][place % rows : place % rows + 1]
@@ -551,22 +543,20 @@
 
 
 def own_vector(own, from_x, from_y, late_x, late_y, vector):
-    rows, cols = own.shape[1:]
-    shapes = [((2, rows, cols), F32), ((2, rows, cols + 128), B16), (vector.shape, B16)]
+    shapes = [(late_x.shape, F32), (late_x.shape, B16), (vector.shape, B16)]
     operands = [own, from_x, from_y, late_x, late_y, vector]
     return call(own_vector_body, "own_vector", shapes, operands, limit=8)
 
 
-def mid_vector(near, mid, vector):
-    rows, cols = near.shape[1:]
-    shapes = [((rows, cols), F32), ((rows, cols + 256), B16), (vector.shape, B16)]
-    return call(mid_vector_body, "mid_vector", shapes, [near, mid, vector], limit=8)
-
-
-def far_vector(own, far, vector, sizes):
+def mid_vector(near, mid, vector, other):
+    shapes = [(near.shape[1:], F32), (near.shape[1:], B16), (vector.shape, B16)]
+    return call(mid_vector_body, "mid_vector", shapes, [near, mid, vector, other], limit=8)
+
+
+def far_vector(own, far, vector, other, sizes):
     rows, cols = own.shape
     shapes = [((rows, cols // 4), F32)] * 4 + [((size // 128, 128), F32) for size in sizes]
-    outs = call(far_vector_body, "far_vector", shapes, [own, far, vector], limit=8)
+    outs = call(far_vector_body, "far_vector", shapes, [own, far, vector, other], limit=8)
     return outs[:4], [member.reshape(-1) for member in outs[4:]]
 
 
@@ -695,13 +685,13 @@
         c_farr = swap(c_far, 12)
         axlr, aylr, c_farr = tie(axlr, aylr, c_farr)
         a_near, a_mid, vector = own_vector(ao, axr, ayr, axlr, aylr, vector)
-        a_midr = swap(a_mid, 4)
+        a_midr, other = swap(a_mid, 4), swap(vector, 4)
         d_w_down_t = d_near + d_farr.astype(F32)
-        a_midr, d_w_down_t = tie(a_midr, d_w_down_t)
-        a_near, a_far, vector = mid_vector(a_near, a_midr, vector)
-        a_farr = swap(a_far, 12)
+        a_midr, other, d_w_down_t = tie(a_midr, other, d_w_down_t)
+        a_near, a_far, vector = mid_vector(a_near, a_midr, vector, other)
+        a_farr, other = swap(a_far, 12), swap(vector, 12)
         d_w_up = c_near + c_farr.astype(F32)
-        d_wa, summed = far_vector(a_near, a_farr, vector, sizes)
+        d_wa, summed = far_vector(a_near, a_farr, vector, other, sizes)
     else:
         full = []
         for parts in ((ax, ay, axl, ayl, ao), (cx, cy, cxl, cyl, co), (dx, dy, dxl, dyl, do)):

time: 183 us -> 186 us (1.016)
    ppermute x42 -> x44, starting transfers between devices: 57.1 us -> 58.7 us  [swap(): return lax.ppermute(values, 'dp', [(i, i ^ bit) for i in range(BLOCKS)])]
    ppermute x42 -> x44, waiting for transfers between devices: 58.4 us -> 59.3 us  [swap(): return lax.ppermute(values, 'dp', [(i, i ^ bit) for i in range(BLOCKS)])]
  transfers between devices with their start and end apart: 48 -> 50, of which waited for: 24 -> 26; matrix products, arithmetic and copies ran while one was open for 3% -> 3% of each run, Pallas kernels for 28% -> 27%
where the time goes in v3:
time: 186 us
  waiting for transfers between devices  60.8 us (33%)
  starting transfers between devices  59.4 us (32%)
  Pallas kernels  57.5 us (31%)
  other arithmetic  6.19 us (3%)
    ppermute x44, waiting for transfers between devices, swap(): return lax.ppermute(values, 'dp', [(i, i ^ bit) for i in range(BLOCKS)])  59.3 us
    ppermute x44, starting transfers between devices, swap(): return lax.ppermute(values, 'dp', [(i, i ^ bit) for i in range(BLOCKS)])  58.7 us
    pallas_call x24, Pallas kernels, call(): pl.pallas_call(body, in_specs=[SMEM_SPEC if member.dtype == jnp.int32 and...  57.5 us
  transfers between devices with their start and end apart: 50, of which 26 were waited for; matrix products, arithmetic and copies ran while one was open for 3% of the time, Pallas kernels for 27%

profile of v3, /device:TPU:0, one launch (start us, length us, event | category | flops | bytes accessed | tf_op | source)
XLA Modules:
  0.0 185.6 jit_solution(2934452431893736488)
XLA Ops:
  1.5 5.1 %collective-permute-start = (bf16[48,1536]{1,0:T(8,128)(2,1)S(1)}, bf16[48,1536]{1,0:T(8,128)(2,1)S(1)}, u32[]{:S(2)}, u32[]{:S(2)}) collective-permute-start(bf16[48,1536]{1,0:T(8,128)(2,1)S(1)} %get-tuple-element.349), channel_id=1, source_target_pairs={{0,24},{2,26},{4,28},{6,30},{8,16},{10,18},{12,20},{14,22},{16,8},... | collective-permute-start | bytes 442376 | tf_op jit(solution)/shard_map/ppermute | solution.py:22
  11.0 2.7 %collective-permute-start.3 = (bf16[2,48,1536]{2,1,0:T(8,128)(2,1)S(1)}, bf16[2,48,1536]{2,1,0:T(8,128)(2,1)S(1)}, u32[]{:S(2)}, u32[]{:S(2)}) collective-permute-start(bf16[2,48,1536]{2,1,0:T(8,128)(2,1)S(1)} %pad_maximum_fusion.rest_0_), channel_id=1, source_target_pairs={{0,8},{2,10},{4,12},{6,14},{8,0},{10,2},{12,4},{14,6},{16,24},{18,... | collective-permute-start | bytes 884744 | tf_op jit(solution)/shard_map/ppermute | solution.py:22
  16.7 3.3 %collective-permute-done.3.rest_1_ = bf16[2,48,1536]{2,1,0:T(8,128)(2,1)S(1)} collective-permute-done((bf16[2,48,1536]{2,1,0:T(8,128)(2,1)S(1)}, bf16[2,48,1536]{2,1,0:T(8,128)(2,1)S(1)}, u32[]{:S(2)}, u32[]{:S(2)}) %collective-permute-start.3) | collective-permute-done | bytes 294944 | tf_op jit(solution)/shard_map/ppermute | solution.py:22
  26.4 6.1 %collective-permute-done.6 = bf16[48,1536]{1,0:T(8,128)(2,1)S(1)} collective-permute-done((bf16[48,1536]{1,0:T(8,128)(2,1)S(1)}, bf16[48,1536]{1,0:T(8,128)(2,1)S(1)}, u32[]{:S(2)}, u32[]{:S(2)}) %collective-permute-start.6) | collective-permute-done | bytes 147488 | tf_op jit(solution)/shard_map/ppermute | solution.py:22
  36.7 4.2 %collective-permute-done.9.rest_1_ = bf16[2,48,1536]{2,1,0:T(8,128)(2,1)S(1)} collective-permute-done((bf16[2,48,1536]{2,1,0:T(8,128)(2,1)S(1)}, bf16[2,48,1536]{2,1,0:T(8,128)(2,1)S(1)}, u32[]{:S(2)}, u32[]{:S(2)}) %collective-permute-start.9) | collective-permute-done | bytes 294944 | tf_op jit(solution)/shard_map/ppermute | solution.py:22
  41.8 6.0 %collective-permute-done.7.rest_7_ = bf16[2,48,1536]{2,1,0:T(8,128)(2,1)S(1)} collective-permute-done((bf16[2,48,1536]{2,1,0:T(8,128)(2,1)S(1)}, bf16[2,48,1536]{2,1,0:T(8,128)(2,1)S(1)}, u32[]{:S(2)}, u32[]{:S(2)}) %collective-permute-start.7) | collective-permute-done | bytes 294944 | tf_op jit(solution)/shard_map/ppermute | solution.py:22
  54.0 5.7 %attend.1 = (bf16[768,1536]{1,0:T(8,128)(2,1)S(1)}, bf16[1024,1152]{1,0:T(8,128)(2,1)S(1)}, bf16[1024,768]{1,0:T(8,128)(2,1)S(1)}, bf16[1024,384]{1,0:T(8,128)(2,1)S(1)}, bf16[1024,768]{1,0:T(8,128)(2,1)S(1)}) custom-call(s32[1]{0:T(128)} %bitcast.1.me_ref, s32[8]{0:T(128)S(1)} %copy-done.1, bf16[1024,768]{1,0:T(8,128)(2,1)S(1)} %broadcast_select_fusion.in_ref.refs_0_, ...), custom_call_target="tpu_custom_call" | custom-call | flops 1 | bytes 1 | tf_op jit(solution)/shard_map/attend/pallas_call | solution.py:55
  62.1 7.1 %collective-permute-done.18.rest_5_ = bf16[2,48,1536]{2,1,0:T(8,128)(2,1)S(1)} collective-permute-done((bf16[2,48,1536]{2,1,0:T(8,128)(2,1)S(1)}, bf16[2,48,1536]{2,1,0:T(8,128)(2,1)S(1)}, u32[]{:S(2)}, u32[]{:S(2)}) %collective-permute-start.18) | collective-permute-done | bytes 294944 | tf_op jit(solution)/shard_map/ppermute | solution.py:22
  73.6 5.8 %up.1 = (bf16[768,1536]{1,0:T(8,128)(2,1)S(1)}, f32[1024,768]{1,0:T(8,128)S(1)}, f32[1024,128]{1,0:T(8,128)S(1)}, bf16[1024,768]{1,0:T(8,128)(2,1)S(1)}, bf16[10...) custom-call(s32[1]{0:T(128)} %bitcast.1.me_ref, bf16[1024,768]{1,0:T(8,128)(2,1)S(1)} %broadcast_select_fusion.in_ref.refs_0_, ...), custom_call_target="tpu_custom_call" | custom-call | flops 1 | bytes 1 | tf_op jit(solution)/shard_map/up/pallas_call | solution.py:55
  87.2 2.3 %weight_grad.4 = (bf16[4,48,1536]{2,1,0:T(8,128)(2,1)S(1)}, bf16[4,48,1536]{2,1,0:T(8,128)(2,1)S(1)}, bf16[768,1024]{1,0:T(8,128)(2,1)S(1)}) custom-call(s32[1]{0:T(128)} %bitcast.1.me_ref, bf16[512,768]{1,0:T(8,128)(2,1)S(1)} %get-tuple-element.234.refs_0_.low_a_ref, bf16[512,768]{1,0:T(8,128)(2,1)S(1)} %get-tuple-element.235.refs_1_.low_b_ref, ...), custom_call_target="tpu_custom_call" | custom-call | flops 1 | bytes 1 | tf_op jit(solution)/shard_map/weight_grad/pallas_call | solution.py:55
  90.9 2.4 %weight_grad.6 = (bf16[2,48,1536]{2,1,0:T(8,128)(2,1)S(1)}, bf16[2,48,1536]{2,1,0:T(8,128)(2,1)S(1)}, bf16[4,48,1536]{2,1,0:T(8,128)(2,1)S(1)}) custom-call(s32[1]{0:T(128)} %bitcast.1.me_ref, bf16[768,1024]{1,0:T(8,128)(2,1)S(1)} %get-tuple-element.246.refs_0_, bf16[1024,1536]{1,0:T(8,128)(2,1)S(1)} %get-tuple-element.221.act_ref.refs_2_.refs_1_), custom_call_target="tpu_custom_call" | custom-call | flops 1 | bytes 1 | tf_op jit(solution)/shard_map/weight_grad/pallas_call | solution.py:55
  93.3 6.3 %hidden_back.1 = (bf16[1024,1536]{1,0:T(8,128)(2,1)S(1)}, bf16[1024,768]{1,0:T(8,128)(2,1)S(1)}, f32[8,1536]{1,0:T(8,128)S(1)}) custom-call(bf16[512,768]{1,0:T(8,128)(2,1)S(1)} %get-tuple-element.234.refs_0_.low_a_ref, bf16[512,768]{1,0:T(8,128)(2,1)S(1)} %get-tuple-element.235.refs_1_.low_b_ref, bf16[1024,1536]{1,0:T(8,128)(2,1)S(1)} %get-tuple-element.236.slope_ref, ...), custom_call_target="tpu_custom_call" | custom-call | flops 1 | bytes 1 | tf_op jit(solution)/shard_map/hidden_back/pallas_call | solution.py:55
  99.6 4.5 %weight_grad.5 = (bf16[4,48,1536]{2,1,0:T(8,128)(2,1)S(1)}, bf16[4,48,1536]{2,1,0:T(8,128)(2,1)S(1)}, bf16[2,48,1536]{2,1,0:T(8,128)(2,1)S(1)}, bf16[2,48,1536]{2,1,0:T(8,128)(2,1)S(1)}, bf16[4,48,1536]{2,1,0:T(8,128)(2,1)S(1)}) custom-call(s32[1]{0:T(128)} %bitcast.1.me_ref, bf16[1024,768]{1,0:T(8,128)(2,1)S(1)} %get-tuple-element.216.refs_0_, ...), custom_call_target="tpu_custom_call" | custom-call | flops 1 | bytes 1 | tf_op jit(solution)/shard_map/weight_grad/pallas_call | solution.py:55
  110.2 15.4 %attend_back.1 = (f32[1024,768]{1,0:T(8,128)S(1)}, bf16[1024,768]{1,0:T(8,128)(2,1)S(1)}, bf16[1024,1152]{1,0:T(8,128)(2,1)S(1)}, bf16[1024,768]{1,0:T(8,128)(2,...) custom-call(f32[512,768]{1,0:T(8,128)S(1)} %get-tuple-element.258.dz_a_ref, ...), custom_call_target="tpu_custom_call" | custom-call | flops 1 | bytes 1 | tf_op jit(solution)/shard_map/attend_back/pallas_call | solution.py:55
  125.6 2.4 %collective-permute-done.31.late_x_ref = bf16[2,48,1536]{2,1,0:T(8,128)(2,1)S(1)} collective-permute-done((bf16[2,48,1536]{2,1,0:T(8,128)(2,1)S(1)}, bf16[2,48,1536]{2,1,0:T(8,128)(2,1)S(1)}, u32[]{:S(2)}, u32[]{:S(2)}) %collective-permute-start.31) | collective-permute-done | bytes 294944 | tf_op jit(solution)/shard_map/ppermute | solution.py:22
  132.8 3.9 %weight_grad.7 = (bf16[4,48,1664]{2,1,0:T(8,128)(2,1)S(1)}, bf16[4,48,1536]{2,1,0:T(8,128)(2,1)S(1)}, bf16[2,48,1536]{2,1,0:T(8,128)(2,1)S(1)}, bf16[2,48,1536]{2,1,0:T(8,128)(2,1)S(1)}, bf16[4,48,1536]{2,1,0:T(8,128)(2,1)S(1)}) custom-call(s32[1]{0:T(128)} %bitcast.1.me_ref, bf16[1024,768]{1,0:T(8,128)(2,1)S(1)} %broadcast_select_fusion.in_ref.refs_0_, ...), custom_call_target="tpu_custom_call" | custom-call | flops 1 | bytes 1 | tf_op jit(solution)/shard_map/weight_grad/pallas_call | solution.py:55
  142.1 3.5 %collective-permute-start.41 = (bf16[48,1536]{1,0:T(8,128)(2,1)S(1)}, bf16[48,1536]{1,0:T(8,128)(2,1)S(1)}, u32[]{:S(2)}, u32[]{:S(2)}) collective-permute-start(bf16[48,1536]{1,0:T(8,128)(2,1)S(1)} %get-tuple-element.297), channel_id=1, source_target_pairs={{0,24},{2,26},{4,28},{6,30},{8,16},{10,18},{12,20},{14,22},{16,8},... | collective-permute-start | bytes 442376 | tf_op jit(solution)/shard_map/ppermute | solution.py:22
  145.5 2.8 %last.1 = (f32[1024,768]{1,0:T(8,128)}, bf16[1024,768]{1,0:T(8,128)(2,1)}) custom-call(f32[1024,768]{1,0:T(8,128)S(1)} %get-tuple-element.298.dz_ref, bf16[1024,768]{1,0:T(8,128)(2,1)S(1)} %get-tuple-element.299.own_ref, bf16[1024,768]{1,0:T(8,128)(2,1)S(1)} %collective-permute-done.42.other_ref, f32[1024,128]{1,0:T(8,128)S(1)} %broadcast_in_dim.36.flag_ref, ...), custom_call_target="tpu_custom_call" | custom-call | flops 1 | bytes 1 | tf_op jit(solution)/shard_map/last/pallas_call | solution.py:55
  148.4 7.0 %collective-permute-done.41 = bf16[48,1536]{1,0:T(8,128)(2,1)S(1)} collective-permute-done((bf16[48,1536]{1,0:T(8,128)(2,1)S(1)}, bf16[48,1536]{1,0:T(8,128)(2,1)S(1)}, u32[]{:S(2)}, u32[]{:S(2)}) %collective-permute-start.41) | collective-permute-done | bytes 147488 | tf_op jit(solution)/shard_map/ppermute | solution.py:22
  158.0 3.5 %collective-permute-start.45 = (bf16[48,1536]{1,0:T(8,128)(2,1)S(1)}, bf16[48,1536]{1,0:T(8,128)(2,1)S(1)}, u32[]{:S(2)}, u32[]{:S(2)}) collective-permute-start(bf16[48,1536]{1,0:T(8,128)(2,1)S(1)} %get-tuple-element.315), channel_id=1, source_target_pairs={{0,24},{2,26},{4,28},{6,30},{8,16},{10,18},{12,20},{14,22},{16,8},... | collective-permute-start | bytes 442376 | tf_op jit(solution)/shard_map/ppermute | solution.py:22
  161.5 3.6 %collective-permute-done.45 = bf16[48,1536]{1,0:T(8,128)(2,1)S(1)} collective-permute-done((bf16[48,1536]{1,0:T(8,128)(2,1)S(1)}, bf16[48,1536]{1,0:T(8,128)(2,1)S(1)}, u32[]{:S(2)}, u32[]{:S(2)}) %collective-permute-start.45) | collective-permute-done | bytes 147488 | tf_op jit(solution)/shard_map/ppermute | solution.py:22
  165.6 2.3 %collective-permute-start.47 = (bf16[2,48,128]{2,1,0:T(8,128)(2,1)S(1)}, bf16[2,48,128]{2,1,0:T(8,128)(2,1)S(1)}, u32[]{:S(2)}, u32[]{:S(2)}) collective-permute-start(bf16[2,48,128]{2,1,0:T(8,128)(2,1)S(1)} %get-tuple-element.321.v_ref), channel_id=1, source_target_pairs={{0,8},{2,10},{4,12},{6,14},{8,0},{10,2},{12,4},{14,6},{16,24},{18,... | collective-permute-start | bytes 73736 | tf_op jit(solution)/shard_map/ppermute | solution.py:22
  170.0 5.9 %collective-permute-done.46.mid_ref = bf16[2,48,1536]{2,1,0:T(8,128)(2,1)S(1)} collective-permute-done((bf16[2,48,1536]{2,1,0:T(8,128)(2,1)S(1)}, bf16[2,48,1536]{2,1,0:T(8,128)(2,1)S(1)}, u32[]{:S(2)}, u32[]{:S(2)}) %collective-permute-start.46) | collective-permute-done | bytes 294944 | tf_op jit(solution)/shard_map/ppermute | solution.py:22
  181.8 2.9 %collective-permute-done.48.far_ref = bf16[48,1536]{1,0:T(8,128)(2,1)S(1)} collective-permute-done((bf16[48,1536]{1,0:T(8,128)(2,1)S(1)}, bf16[48,1536]{1,0:T(8,128)(2,1)S(1)}, u32[]{:S(2)}, u32[]{:S(2)}) %collective-permute-start.48) | collective-permute-done | bytes 147488 | tf_op jit(solution)/shard_map/ppermute | solution.py:22
  (146 shorter events, 69.6 us)
Async XLA Ops:
  1.5 9.2 %collective-permute-start = (bf16[48,1536]{1,0:T(8,128)(2,1)S(1)}, bf16[48,1536]{1,0:T(8,128)(2,1)S(1)}, u32[]{:S(2)}, u32[]{:S(2)}) collective-permute-start(bf16[48,1536]{1,0:T(8,128)(2,1)S(1)} %get-tuple-element.349), channel_id=1, source_target_pairs={{0,24},{2,26},{4,28},{6,30},{8,16},{10,18},{12,20},{14,22},{16,8},... | collective-permute-start | bytes 442376 | tf_op jit(solution)/shard_map/ppermute | solution.py:22
  22.7 9.8 %collective-permute-start.5 = (bf16[2,48,1536]{2,1,0:T(8,128)(2,1)S(1)}, bf16[2,48,1536]{2,1,0:T(8,128)(2,1)S(1)}, u32[]{:S(2)}, u32[]{:S(2)}) collective-permute-start(bf16[2,48,1536]{2,1,0:T(8,128)(2,1)S(1)} %collective-permute-done.3.rest_1_), channel_id=1, source_target_pairs={{0,4},{2,6},{4,0},{6,2},{8,12},{10,14},{12,8},{14,10},{16,20},{18,... | collective-permute-start | bytes 884744 | tf_op jit(solution)/shard_map/ppermute | solution.py:22
  23.2 9.3 %collective-permute-start.4 = (bf16[2,48,1536]{2,1,0:T(8,128)(2,1)S(1)}, bf16[2,48,1536]{2,1,0:T(8,128)(2,1)S(1)}, u32[]{:S(2)}, u32[]{:S(2)}) collective-permute-start(bf16[2,48,1536]{2,1,0:T(8,128)(2,1)S(1)} %collective-permute-done.3.rest_1_), channel_id=1, source_target_pairs={{0,2},{2,0},{4,6},{6,4},{8,10},{10,8},{12,14},{14,12},{16,18},{18,... | collective-permute-start | bytes 884744 | tf_op jit(solution)/shard_map/ppermute | solution.py:22
  32.6 9.2 %collective-permute-start.11 = (bf16[2,48,1536]{2,1,0:T(8,128)(2,1)S(1)}, bf16[2,48,1536]{2,1,0:T(8,128)(2,1)S(1)}, u32[]{:S(2)}, u32[]{:S(2)}) collective-permute-start(bf16[2,48,1536]{2,1,0:T(8,128)(2,1)S(1)} %pad_maximum_fusion.1.rest_0_), channel_id=1, source_target_pairs={{0,4},{2,6},{4,0},{6,2},{8,12},{10,14},{12,8},{14,10},{16,20},{18,... | collective-permute-start | bytes 884744 | tf_op jit(solution)/shard_map/ppermute | solution.py:22
  34.8 13.0 %collective-permute-start.7 = (bf16[2,48,1536]{2,1,0:T(8,128)(2,1)S(1)}, bf16[2,48,1536]{2,1,0:T(8,128)(2,1)S(1)}, u32[]{:S(2)}, u32[]{:S(2)}) collective-permute-start(bf16[2,48,1536]{2,1,0:T(8,128)(2,1)S(1)} %collective-permute-done.5.rest_5_), channel_id=1, source_target_pairs={{0,2},{2,0},{4,6},{6,4},{8,10},{10,8},{12,14},{14,12},{16,18},{18,... | collective-permute-start | bytes 884744 | tf_op jit(solution)/shard_map/ppermute | solution.py:22
  36.3 11.5 %collective-permute-start.8 = (bf16[2,48,1536]{2,1,0:T(8,128)(2,1)S(1)}, bf16[2,48,1536]{2,1,0:T(8,128)(2,1)S(1)}, u32[]{:S(2)}, u32[]{:S(2)}) collective-permute-start(bf16[2,48,1536]{2,1,0:T(8,128)(2,1)S(1)} %collective-permute-done.1.rest_2_), channel_id=1, source_target_pairs={{0,4},{2,6},{4,0},{6,2},{8,12},{10,14},{12,8},{14,10},{16,20},{18,... | collective-permute-start | bytes 884744 | tf_op jit(solution)/shard_map/ppermute | solution.py:22
  47.8 11.9 %collective-permute-start.12 = (bf16[2,48,1536]{2,1,0:T(8,128)(2,1)S(1)}, bf16[2,48,1536]{2,1,0:T(8,128)(2,1)S(1)}, u32[]{:S(2)}, u32[]{:S(2)}) collective-permute-start(bf16[2,48,1536]{2,1,0:T(8,128)(2,1)S(1)} %collective-permute-done.9.rest_1_), channel_id=1, source_target_pairs={{0,2},{2,0},{4,6},{6,4},{8,10},{10,8},{12,14},{14,12},{16,18},{18,... | collective-permute-start | bytes 884744 | tf_op jit(solution)/shard_map/ppermute | solution.py:22
  48.3 11.4 %collective-permute-start.13 = (bf16[2,48,1536]{2,1,0:T(8,128)(2,1)S(1)}, bf16[2,48,1536]{2,1,0:T(8,128)(2,1)S(1)}, u32[]{:S(2)}, u32[]{:S(2)}) collective-permute-start(bf16[2,48,1536]{2,1,0:T(8,128)(2,1)S(1)} %collective-permute-done.10.rest_2_), channel_id=1, source_target_pairs={{0,4},{2,6},{4,0},{6,2},{8,12},{10,14},{12,8},{14,10},{16,20},{18,... | collective-permute-start | bytes 884744 | tf_op jit(solution)/shard_map/ppermute | solution.py:22
  49.5 10.2 %collective-permute-start.17 = (bf16[2,48,1536]{2,1,0:T(8,128)(2,1)S(1)}, bf16[2,48,1536]{2,1,0:T(8,128)(2,1)S(1)}, u32[]{:S(2)}, u32[]{:S(2)}) collective-permute-start(bf16[2,48,1536]{2,1,0:T(8,128)(2,1)S(1)} %pad_maximum_fusion.2.rest_0_), channel_id=1, source_target_pairs={{0,4},{2,6},{4,0},{6,2},{8,12},{10,14},{12,8},{14,10},{16,20},{18,... | collective-permute-start | bytes 884744 | tf_op jit(solution)/shard_map/ppermute | solution.py:22
  50.4 9.3 %collective-permute-start.16 = (bf16[2,48,1536]{2,1,0:T(8,128)(2,1)S(1)}, bf16[2,48,1536]{2,1,0:T(8,128)(2,1)S(1)}, u32[]{:S(2)}, u32[]{:S(2)}) collective-permute-start(bf16[2,48,1536]{2,1,0:T(8,128)(2,1)S(1)} %pad_maximum_fusion.2.rest_0_), channel_id=1, source_target_pairs={{0,2},{2,0},{4,6},{6,4},{8,10},{10,8},{12,14},{14,12},{16,18},{18,... | collective-permute-start | bytes 884744 | tf_op jit(solution)/shard_map/ppermute | solution.py:22
  59.7 9.8 %collective-permute-start.21 = (bf16[1024,768]{1,0:T(8,128)(2,1)S(1)}, bf16[1024,768]{1,0:T(8,128)(2,1)S(1)}, u32[]{:S(2)}, u32[]{:S(2)}) collective-permute-start(bf16[1024,768]{1,0:T(8,128)(2,1)S(1)} %get-tuple-element.208.own_ref), channel_id=1, source_target_pairs={{0,1},{1,0},{2,3},{3,2},{4,5},{5,4},{6,7},{7,6},{8,9},{9,8},{10,11... | collective-permute-start | bytes 4718600 | tf_op jit(solution)/shard_map/ppermute | solution.py:34
  59.8 9.4 %collective-permute-start.18 = (bf16[2,48,1536]{2,1,0:T(8,128)(2,1)S(1)}, bf16[2,48,1536]{2,1,0:T(8,128)(2,1)S(1)}, u32[]{:S(2)}, u32[]{:S(2)}) collective-permute-start(bf16[2,48,1536]{2,1,0:T(8,128)(2,1)S(1)} %collective-permute-done.9.rest_1_), channel_id=1, source_target_pairs={{0,4},{2,6},{4,0},{6,2},{8,12},{10,14},{12,8},{14,10},{16,20},{18,... | collective-permute-start | bytes 884744 | tf_op jit(solution)/shard_map/ppermute | solution.py:22
  69.5 10.0 %collective-permute-start.24 = (bf16[2,48,1536]{2,1,0:T(8,128)(2,1)S(1)}, bf16[2,48,1536]{2,1,0:T(8,128)(2,1)S(1)}, u32[]{:S(2)}, u32[]{:S(2)}) collective-permute-start(bf16[2,48,1536]{2,1,0:T(8,128)(2,1)S(1)} %collective-permute-done.19.rest_6_), channel_id=1, source_target_pairs={{0,8},{2,10},{4,12},{6,14},{8,0},{10,2},{12,4},{14,6},{16,24},{18,... | collective-permute-start | bytes 884744 | tf_op jit(solution)/shard_map/ppermute | solution.py:22
  89.5 15.6 %collective-permute-start.27 = (bf16[4,48,1536]{2,1,0:T(8,128)(2,1)S(1)}, bf16[4,48,1536]{2,1,0:T(8,128)(2,1)S(1)}, u32[]{:S(2)}, u32[]{:S(2)}) collective-permute-start(bf16[4,48,1536]{2,1,0:T(8,128)(2,1)S(1)} %get-tuple-element.241), channel_id=1, source_target_pairs={{0,2},{2,0},{4,6},{6,4},{8,10},{10,8},{12,14},{14,12},{16,18},{18,... | collective-permute-start | bytes 1769480 | tf_op jit(solution)/shard_map/ppermute | solution.py:22
  90.6 15.3 %collective-permute-start.28 = (bf16[4,48,1536]{2,1,0:T(8,128)(2,1)S(1)}, bf16[4,48,1536]{2,1,0:T(8,128)(2,1)S(1)}, u32[]{:S(2)}, u32[]{:S(2)}) collective-permute-start(bf16[4,48,1536]{2,1,0:T(8,128)(2,1)S(1)} %get-tuple-element.242), channel_id=1, source_target_pairs={{0,4},{2,6},{4,0},{6,2},{8,12},{10,14},{12,8},{14,10},{16,20},{18,... | collective-permute-start | bytes 1769480 | tf_op jit(solution)/shard_map/ppermute | solution.py:22
  105.9 22.7 %collective-permute-start.29 = (bf16[4,48,1536]{2,1,0:T(8,128)(2,1)S(1)}, bf16[4,48,1536]{2,1,0:T(8,128)(2,1)S(1)}, u32[]{:S(2)}, u32[]{:S(2)}) collective-permute-start(bf16[4,48,1536]{2,1,0:T(8,128)(2,1)S(1)} %get-tuple-element.250), channel_id=1, source_target_pairs={{0,2},{2,0},{4,6},{6,4},{8,10},{10,8},{12,14},{14,12},{16,18},{18,... | collective-permute-start | bytes 1769480 | tf_op jit(solution)/shard_map/ppermute | solution.py:22
  106.9 21.8 %collective-permute-start.30 = (bf16[4,48,1536]{2,1,0:T(8,128)(2,1)S(1)}, bf16[4,48,1536]{2,1,0:T(8,128)(2,1)S(1)}, u32[]{:S(2)}, u32[]{:S(2)}) collective-permute-start(bf16[4,48,1536]{2,1,0:T(8,128)(2,1)S(1)} %get-tuple-element.251), channel_id=1, source_target_pairs={{0,4},{2,6},{4,0},{6,2},{8,12},{10,14},{12,8},{14,10},{16,20},{18,... | collective-permute-start | bytes 1769480 | tf_op jit(solution)/shard_map/ppermute | solution.py:22
  107.3 20.7 %collective-permute-start.31 = (bf16[2,48,1536]{2,1,0:T(8,128)(2,1)S(1)}, bf16[2,48,1536]{2,1,0:T(8,128)(2,1)S(1)}, u32[]{:S(2)}, u32[]{:S(2)}) collective-permute-start(bf16[2,48,1536]{2,1,0:T(8,128)(2,1)S(1)} %get-tuple-element.256), channel_id=1, source_target_pairs={{0,2},{2,0},{4,6},{6,4},{8,10},{10,8},{12,14},{14,12},{16,18},{18,... | collective-permute-start | bytes 884744 | tf_op jit(solution)/shard_map/ppermute | solution.py:22
  108.5 20.2 %collective-permute-start.32 = (bf16[2,48,1536]{2,1,0:T(8,128)(2,1)S(1)}, bf16[2,48,1536]{2,1,0:T(8,128)(2,1)S(1)}, u32[]{:S(2)}, u32[]{:S(2)}) collective-permute-start(bf16[2,48,1536]{2,1,0:T(8,128)(2,1)S(1)} %get-tuple-element.257), channel_id=1, source_target_pairs={{0,4},{2,6},{4,0},{6,2},{8,12},{10,14},{12,8},{14,10},{16,20},{18,... | collective-permute-start | bytes 884744 | tf_op jit(solution)/shard_map/ppermute | solution.py:22
  138.3 17.1 %collective-permute-start.38 = (bf16[4,48,1664]{2,1,0:T(8,128)(2,1)S(1)}, bf16[4,48,1664]{2,1,0:T(8,128)(2,1)S(1)}, u32[]{:S(2)}, u32[]{:S(2)}) collective-permute-start(bf16[4,48,1664]{2,1,0:T(8,128)(2,1)S(1)} %get-tuple-element.289), channel_id=1, source_target_pairs={{0,2},{2,0},{4,6},{6,4},{8,10},{10,8},{12,14},{14,12},{16,18},{18,... | collective-permute-start | bytes 1916936 | tf_op jit(solution)/shard_map/ppermute | solution.py:22
  139.3 16.1 %collective-permute-start.39 = (bf16[4,48,1536]{2,1,0:T(8,128)(2,1)S(1)}, bf16[4,48,1536]{2,1,0:T(8,128)(2,1)S(1)}, u32[]{:S(2)}, u32[]{:S(2)}) collective-permute-start(bf16[4,48,1536]{2,1,0:T(8,128)(2,1)S(1)} %get-tuple-element.290), channel_id=1, source_target_pairs={{0,4},{2,6},{4,0},{6,2},{8,12},{10,14},{12,8},{14,10},{16,20},{18,... | collective-permute-start | bytes 1769480 | tf_op jit(solution)/shard_map/ppermute | solution.py:22
  141.2 14.2 %collective-permute-start.40 = (bf16[2,48,1536]{2,1,0:T(8,128)(2,1)S(1)}, bf16[2,48,1536]{2,1,0:T(8,128)(2,1)S(1)}, u32[]{:S(2)}, u32[]{:S(2)}) collective-permute-start(bf16[2,48,1536]{2,1,0:T(8,128)(2,1)S(1)} %get-tuple-element.294), channel_id=1, source_target_pairs={{0,8},{2,10},{4,12},{6,14},{8,0},{10,2},{12,4},{14,6},{16,24},{18,... | collective-permute-start | bytes 884744 | tf_op jit(solution)/shard_map/ppermute | solution.py:22
  142.1 13.3 %collective-permute-start.41 = (bf16[48,1536]{1,0:T(8,128)(2,1)S(1)}, bf16[48,1536]{1,0:T(8,128)(2,1)S(1)}, u32[]{:S(2)}, u32[]{:S(2)}) collective-permute-start(bf16[48,1536]{1,0:T(8,128)(2,1)S(1)} %get-tuple-element.297), channel_id=1, source_target_pairs={{0,24},{2,26},{4,28},{6,30},{8,16},{10,18},{12,20},{14,22},{16,8},... | collective-permute-start | bytes 442376 | tf_op jit(solution)/shard_map/ppermute | solution.py:22
  155.5 9.8 %collective-permute-start.44 = (bf16[2,48,1664]{2,1,0:T(8,128)(2,1)S(1)}, bf16[2,48,1664]{2,1,0:T(8,128)(2,1)S(1)}, u32[]{:S(2)}, u32[]{:S(2)}) collective-permute-start(bf16[2,48,1664]{2,1,0:T(8,128)(2,1)S(1)} %get-tuple-element.312), channel_id=1, source_target_pairs={{0,4},{2,6},{4,0},{6,2},{8,12},{10,14},{12,8},{14,10},{16,20},{18,... | collective-permute-start | bytes 958472 | tf_op jit(solution)/shard_map/ppermute | solution.py:22
  (37 other events, 285.8 us)

commit v4 on v2

--- a/solution.py
+++ b/solution.py
@@ -679,9 +679,9 @@
     vector = joined.astype(B16) if fast else None
     ax, ay, axl, ayl, ao = weight_grad(me, [[in_low], [dz_one_low]], [d_qkv, attended], vector=vector)
     if fast:
-        cxlr, cylr, d_midr, ax, ay, part = tie(cxlr, cylr, d_midr, ax, ay, part)
+        c_near, c_mid = add_own(co, cxr, cyr, cxlr, cylr)
+        c_near, c_mid, d_midr, ax, ay, part = tie(c_near, c_mid, d_midr, ax, ay, part)
         axr, ayr = swap(ax, 1), swap(ay, 2)
-        c_near, c_mid = add_own(co, cxr, cyr, cxlr, cylr)
         d_near, d_far = add_mid(d_near, d_midr)
         c_midr, d_farr = swap(c_mid, 4), swap(d_far, 12)
     other = pair_swap(part)

time: 183 us -> 184 us (level)
  no operation moved by 1% of the time
where the time goes in v4:
time: 184 us; the launch traced here: 183 us
  waiting for transfers between devices  59.7 us (32%)
  starting transfers between devices  58.1 us (32%)
  Pallas kernels  57.5 us (31%)
  other arithmetic  6.2 us (3%)
    ppermute x42, waiting for transfers between devices, swap(): return lax.ppermute(values, 'dp', [(i, i ^ bit) for i in range(BLOCKS)])  58.2 us
    pallas_call x24, Pallas kernels, call(): pl.pallas_call(body, in_specs=[SMEM_SPEC if member.dtype == jnp.int32 and...  57.5 us
    ppermute x42, starting transfers between devices, swap(): return lax.ppermute(values, 'dp', [(i, i ^ bit) for i in range(BLOCKS)])  57.4 us
  transfers between devices with their start and end apart: 48, of which 24 were waited for; matrix products, arithmetic and copies ran while one was open for 3% of the time, Pallas kernels for 28%

profile of v4, /device:TPU:0, one launch (start us, length us, event | category | flops | bytes accessed | tf_op | source)
XLA Modules:
  0.0 183.1 jit_solution(5385855523662545303)
XLA Ops:
  1.5 5.1 %collective-permute-start = (bf16[48,1536]{1,0:T(8,128)(2,1)S(1)}, bf16[48,1536]{1,0:T(8,128)(2,1)S(1)}, u32[]{:S(2)}, u32[]{:S(2)}) collective-permute-start(bf16[48,1536]{1,0:T(8,128)(2,1)S(1)} %get-tuple-element.347), channel_id=1, source_target_pairs={{0,24},{2,26},{4,28},{6,30},{8,16},{10,18},{12,20},{14,22},{16,8},... | collective-permute-start | bytes 442376 | tf_op jit(solution)/shard_map/ppermute | solution.py:22
  11.0 2.7 %collective-permute-start.3 = (bf16[2,48,1536]{2,1,0:T(8,128)(2,1)S(1)}, bf16[2,48,1536]{2,1,0:T(8,128)(2,1)S(1)}, u32[]{:S(2)}, u32[]{:S(2)}) collective-permute-start(bf16[2,48,1536]{2,1,0:T(8,128)(2,1)S(1)} %pad_maximum_fusion.rest_0_), channel_id=1, source_target_pairs={{0,8},{2,10},{4,12},{6,14},{8,0},{10,2},{12,4},{14,6},{16,24},{18,... | collective-permute-start | bytes 884744 | tf_op jit(solution)/shard_map/ppermute | solution.py:22
  16.7 3.3 %collective-permute-done.3.rest_1_ = bf16[2,48,1536]{2,1,0:T(8,128)(2,1)S(1)} collective-permute-done((bf16[2,48,1536]{2,1,0:T(8,128)(2,1)S(1)}, bf16[2,48,1536]{2,1,0:T(8,128)(2,1)S(1)}, u32[]{:S(2)}, u32[]{:S(2)}) %collective-permute-start.3) | collective-permute-done | bytes 294944 | tf_op jit(solution)/shard_map/ppermute | solution.py:22
  26.4 6.1 %collective-permute-done.6 = bf16[48,1536]{1,0:T(8,128)(2,1)S(1)} collective-permute-done((bf16[48,1536]{1,0:T(8,128)(2,1)S(1)}, bf16[48,1536]{1,0:T(8,128)(2,1)S(1)}, u32[]{:S(2)}, u32[]{:S(2)}) %collective-permute-start.6) | collective-permute-done | bytes 147488 | tf_op jit(solution)/shard_map/ppermute | solution.py:22
  36.7 4.2 %collective-permute-done.9.rest_1_ = bf16[2,48,1536]{2,1,0:T(8,128)(2,1)S(1)} collective-permute-done((bf16[2,48,1536]{2,1,0:T(8,128)(2,1)S(1)}, bf16[2,48,1536]{2,1,0:T(8,128)(2,1)S(1)}, u32[]{:S(2)}, u32[]{:S(2)}) %collective-permute-start.9) | collective-permute-done | bytes 294944 | tf_op jit(solution)/shard_map/ppermute | solution.py:22
  41.8 6.0 %collective-permute-done.7.rest_7_ = bf16[2,48,1536]{2,1,0:T(8,128)(2,1)S(1)} collective-permute-done((bf16[2,48,1536]{2,1,0:T(8,128)(2,1)S(1)}, bf16[2,48,1536]{2,1,0:T(8,128)(2,1)S(1)}, u32[]{:S(2)}, u32[]{:S(2)}) %collective-permute-start.7) | collective-permute-done | bytes 294944 | tf_op jit(solution)/shard_map/ppermute | solution.py:22
  54.0 5.7 %attend.1 = (bf16[768,1536]{1,0:T(8,128)(2,1)S(1)}, bf16[1024,1152]{1,0:T(8,128)(2,1)S(1)}, bf16[1024,768]{1,0:T(8,128)(2,1)S(1)}, bf16[1024,384]{1,0:T(8,128)(2,1)S(1)}, bf16[1024,768]{1,0:T(8,128)(2,1)S(1)}) custom-call(s32[1]{0:T(128)} %bitcast.1.me_ref, s32[8]{0:T(128)S(1)} %copy-done.1, bf16[1024,768]{1,0:T(8,128)(2,1)S(1)} %broadcast_select_fusion.in_ref.refs_0_, ...), custom_call_target="tpu_custom_call" | custom-call | flops 1 | bytes 1 | tf_op jit(solution)/shard_map/attend/pallas_call | solution.py:55
  62.1 7.1 %collective-permute-done.18.rest_5_ = bf16[2,48,1536]{2,1,0:T(8,128)(2,1)S(1)} collective-permute-done((bf16[2,48,1536]{2,1,0:T(8,128)(2,1)S(1)}, bf16[2,48,1536]{2,1,0:T(8,128)(2,1)S(1)}, u32[]{:S(2)}, u32[]{:S(2)}) %collective-permute-start.18) | collective-permute-done | bytes 294944 | tf_op jit(solution)/shard_map/ppermute | solution.py:22
  73.6 5.8 %up.1 = (bf16[768,1536]{1,0:T(8,128)(2,1)S(1)}, f32[1024,768]{1,0:T(8,128)S(1)}, f32[1024,128]{1,0:T(8,128)S(1)}, bf16[1024,768]{1,0:T(8,128)(2,1)S(1)}, bf16[10...) custom-call(s32[1]{0:T(128)} %bitcast.1.me_ref, bf16[1024,768]{1,0:T(8,128)(2,1)S(1)} %broadcast_select_fusion.in_ref.refs_0_, ...), custom_call_target="tpu_custom_call" | custom-call | flops 1 | bytes 1 | tf_op jit(solution)/shard_map/up/pallas_call | solution.py:55
  90.9 2.4 %weight_grad.6 = (bf16[2,48,1536]{2,1,0:T(8,128)(2,1)S(1)}, bf16[2,48,1536]{2,1,0:T(8,128)(2,1)S(1)}, bf16[4,48,1536]{2,1,0:T(8,128)(2,1)S(1)}) custom-call(s32[1]{0:T(128)} %bitcast.1.me_ref, bf16[768,1024]{1,0:T(8,128)(2,1)S(1)} %get-tuple-element.244.refs_0_, bf16[1024,1536]{1,0:T(8,128)(2,1)S(1)} %get-tuple-element.220.act_ref.refs_2_.refs_1_), custom_call_target="tpu_custom_call" | custom-call | flops 1 | bytes 1 | tf_op jit(solution)/shard_map/weight_grad/pallas_call | solution.py:55
  93.3 6.3 %hidden_back.1 = (bf16[1024,1536]{1,0:T(8,128)(2,1)S(1)}, bf16[1024,768]{1,0:T(8,128)(2,1)S(1)}, f32[8,1536]{1,0:T(8,128)S(1)}) custom-call(bf16[512,768]{1,0:T(8,128)(2,1)S(1)} %get-tuple-element.233.refs_0_.low_a_ref, bf16[512,768]{1,0:T(8,128)(2,1)S(1)} %get-tuple-element.234.refs_1_.low_b_ref, bf16[1024,1536]{1,0:T(8,128)(2,1)S(1)} %get-tuple-element.235.slope_ref, ...), custom_call_target="tpu_custom_call" | custom-call | flops 1 | bytes 1 | tf_op jit(solution)/shard_map/hidden_back/pallas_call | solution.py:55
  99.6 4.5 %weight_grad.5 = (bf16[4,48,1536]{2,1,0:T(8,128)(2,1)S(1)}, bf16[4,48,1536]{2,1,0:T(8,128)(2,1)S(1)}, bf16[2,48,1536]{2,1,0:T(8,128)(2,1)S(1)}, bf16[2,48,1536]{2,1,0:T(8,128)(2,1)S(1)}, bf16[4,48,1536]{2,1,0:T(8,128)(2,1)S(1)}) custom-call(s32[1]{0:T(128)} %bitcast.1.me_ref, bf16[1024,768]{1,0:T(8,128)(2,1)S(1)} %get-tuple-element.215.refs_0_, ...), custom_call_target="tpu_custom_call" | custom-call | flops 1 | bytes 1 | tf_op jit(solution)/shard_map/weight_grad/pallas_call | solution.py:55
  110.2 15.5 %attend_back.1 = (f32[1024,768]{1,0:T(8,128)S(1)}, bf16[1024,768]{1,0:T(8,128)(2,1)S(1)}, bf16[1024,1152]{1,0:T(8,128)(2,1)S(1)}, bf16[1024,768]{1,0:T(8,128)(2,...) custom-call(f32[512,768]{1,0:T(8,128)S(1)} %get-tuple-element.256.dz_a_ref, ...), custom_call_target="tpu_custom_call" | custom-call | flops 1 | bytes 1 | tf_op jit(solution)/shard_map/attend_back/pallas_call | solution.py:55
  125.7 2.3 %collective-permute-done.31.late_x_ref = bf16[2,48,1536]{2,1,0:T(8,128)(2,1)S(1)} collective-permute-done((bf16[2,48,1536]{2,1,0:T(8,128)(2,1)S(1)}, bf16[2,48,1536]{2,1,0:T(8,128)(2,1)S(1)}, u32[]{:S(2)}, u32[]{:S(2)}) %collective-permute-start.31) | collective-permute-done | bytes 294944 | tf_op jit(solution)/shard_map/ppermute | solution.py:22
  132.8 3.9 %weight_grad.7 = (bf16[4,48,1664]{2,1,0:T(8,128)(2,1)S(1)}, bf16[4,48,1536]{2,1,0:T(8,128)(2,1)S(1)}, bf16[2,48,1536]{2,1,0:T(8,128)(2,1)S(1)}, bf16[2,48,1536]{2,1,0:T(8,128)(2,1)S(1)}, bf16[4,48,1536]{2,1,0:T(8,128)(2,1)S(1)}) custom-call(s32[1]{0:T(128)} %bitcast.1.me_ref, bf16[1024,768]{1,0:T(8,128)(2,1)S(1)} %broadcast_select_fusion.in_ref.refs_0_, ...), custom_call_target="tpu_custom_call" | custom-call | flops 1 | bytes 1 | tf_op jit(solution)/shard_map/weight_grad/pallas_call | solution.py:55
  141.7 3.5 %collective-permute-start.41 = (bf16[48,1536]{1,0:T(8,128)(2,1)S(1)}, bf16[48,1536]{1,0:T(8,128)(2,1)S(1)}, u32[]{:S(2)}, u32[]{:S(2)}) collective-permute-start(bf16[48,1536]{1,0:T(8,128)(2,1)S(1)} %get-tuple-element.296), channel_id=1, source_target_pairs={{0,24},{2,26},{4,28},{6,30},{8,16},{10,18},{12,20},{14,22},{16,8},... | collective-permute-start | bytes 442376 | tf_op jit(solution)/shard_map/ppermute | solution.py:22
  145.2 2.8 %last.1 = (f32[1024,768]{1,0:T(8,128)}, bf16[1024,768]{1,0:T(8,128)(2,1)}) custom-call(f32[1024,768]{1,0:T(8,128)S(1)} %get-tuple-element.297.dz_ref, bf16[1024,768]{1,0:T(8,128)(2,1)S(1)} %get-tuple-element.298.own_ref, bf16[1024,768]{1,0:T(8,128)(2,1)S(1)} %collective-permute-done.42.other_ref, f32[1024,128]{1,0:T(8,128)S(1)} %broadcast_in_dim.36.flag_ref, ...), custom_call_target="tpu_custom_call" | custom-call | flops 1 | bytes 1 | tf_op jit(solution)/shard_map/last/pallas_call | solution.py:55
  148.0 7.0 %collective-permute-done.41 = bf16[48,1536]{1,0:T(8,128)(2,1)S(1)} collective-permute-done((bf16[48,1536]{1,0:T(8,128)(2,1)S(1)}, bf16[48,1536]{1,0:T(8,128)(2,1)S(1)}, u32[]{:S(2)}, u32[]{:S(2)}) %collective-permute-start.41) | collective-permute-done | bytes 147488 | tf_op jit(solution)/shard_map/ppermute | solution.py:22
  158.1 3.5 %collective-permute-start.45 = (bf16[48,1536]{1,0:T(8,128)(2,1)S(1)}, bf16[48,1536]{1,0:T(8,128)(2,1)S(1)}, u32[]{:S(2)}, u32[]{:S(2)}) collective-permute-start(bf16[48,1536]{1,0:T(8,128)(2,1)S(1)} %get-tuple-element.314), channel_id=1, source_target_pairs={{0,24},{2,26},{4,28},{6,30},{8,16},{10,18},{12,20},{14,22},{16,8},... | collective-permute-start | bytes 442376 | tf_op jit(solution)/shard_map/ppermute | solution.py:22
  161.5 3.6 %collective-permute-done.45 = bf16[48,1536]{1,0:T(8,128)(2,1)S(1)} collective-permute-done((bf16[48,1536]{1,0:T(8,128)(2,1)S(1)}, bf16[48,1536]{1,0:T(8,128)(2,1)S(1)}, u32[]{:S(2)}, u32[]{:S(2)}) %collective-permute-start.45) | collective-permute-done | bytes 147488 | tf_op jit(solution)/shard_map/ppermute | solution.py:22
  165.6 2.3 %collective-permute-start.46 = (bf16[2,48,1664]{2,1,0:T(8,128)(2,1)S(1)}, bf16[2,48,1664]{2,1,0:T(8,128)(2,1)S(1)}, u32[]{:S(2)}, u32[]{:S(2)}) collective-permute-start(bf16[2,48,1664]{2,1,0:T(8,128)(2,1)S(1)} %get-tuple-element.319), channel_id=1, source_target_pairs={{0,8},{2,10},{4,12},{6,14},{8,0},{10,2},{12,4},{14,6},{16,24},{18,... | collective-permute-start | bytes 958472 | tf_op jit(solution)/shard_map/ppermute | solution.py:22
  168.7 6.0 %collective-permute-done.46.mid_ref = bf16[2,48,1664]{2,1,0:T(8,128)(2,1)S(1)} collective-permute-done((bf16[2,48,1664]{2,1,0:T(8,128)(2,1)S(1)}, bf16[2,48,1664]{2,1,0:T(8,128)(2,1)S(1)}, u32[]{:S(2)}, u32[]{:S(2)}) %collective-permute-start.46) | collective-permute-done | bytes 319520 | tf_op jit(solution)/shard_map/ppermute | solution.py:22
  174.8 2.4 %collective-permute-start.47 = (bf16[48,1792]{1,0:T(8,128)(2,1)S(1)}, bf16[48,1792]{1,0:T(8,128)(2,1)S(1)}, u32[]{:S(2)}, u32[]{:S(2)}) collective-permute-start(bf16[48,1792]{1,0:T(8,128)(2,1)S(1)} %get-tuple-element.325), channel_id=1, source_target_pairs={{0,24},{2,26},{4,28},{6,30},{8,16},{10,18},{12,20},{14,22},{16,8},... | collective-permute-start | bytes 516104 | tf_op jit(solution)/shard_map/ppermute | solution.py:22
  178.0 4.2 %collective-permute-done.47.far_ref = bf16[48,1792]{1,0:T(8,128)(2,1)S(1)} collective-permute-done((bf16[48,1792]{1,0:T(8,128)(2,1)S(1)}, bf16[48,1792]{1,0:T(8,128)(2,1)S(1)}, u32[]{:S(2)}, u32[]{:S(2)}) %collective-permute-start.47) | collective-permute-done | bytes 172064 | tf_op jit(solution)/shard_map/ppermute | solution.py:22
  (142 shorter events, 65.5 us)
Async XLA Ops:
  1.5 9.2 %collective-permute-start = (bf16[48,1536]{1,0:T(8,128)(2,1)S(1)}, bf16[48,1536]{1,0:T(8,128)(2,1)S(1)}, u32[]{:S(2)}, u32[]{:S(2)}) collective-permute-start(bf16[48,1536]{1,0:T(8,128)(2,1)S(1)} %get-tuple-element.347), channel_id=1, source_target_pairs={{0,24},{2,26},{4,28},{6,30},{8,16},{10,18},{12,20},{14,22},{16,8},... | collective-permute-start | bytes 442376 | tf_op jit(solution)/shard_map/ppermute | solution.py:22
  22.7 9.8 %collective-permute-start.5 = (bf16[2,48,1536]{2,1,0:T(8,128)(2,1)S(1)}, bf16[2,48,1536]{2,1,0:T(8,128)(2,1)S(1)}, u32[]{:S(2)}, u32[]{:S(2)}) collective-permute-start(bf16[2,48,1536]{2,1,0:T(8,128)(2,1)S(1)} %collective-permute-done.3.rest_1_), channel_id=1, source_target_pairs={{0,4},{2,6},{4,0},{6,2},{8,12},{10,14},{12,8},{14,10},{16,20},{18,... | collective-permute-start | bytes 884744 | tf_op jit(solution)/shard_map/ppermute | solution.py:22
  23.2 9.3 %collective-permute-start.4 = (bf16[2,48,1536]{2,1,0:T(8,128)(2,1)S(1)}, bf16[2,48,1536]{2,1,0:T(8,128)(2,1)S(1)}, u32[]{:S(2)}, u32[]{:S(2)}) collective-permute-start(bf16[2,48,1536]{2,1,0:T(8,128)(2,1)S(1)} %collective-permute-done.3.rest_1_), channel_id=1, source_target_pairs={{0,2},{2,0},{4,6},{6,4},{8,10},{10,8},{12,14},{14,12},{16,18},{18,... | collective-permute-start | bytes 884744 | tf_op jit(solution)/shard_map/ppermute | solution.py:22
  32.6 9.2 %collective-permute-start.11 = (bf16[2,48,1536]{2,1,0:T(8,128)(2,1)S(1)}, bf16[2,48,1536]{2,1,0:T(8,128)(2,1)S(1)}, u32[]{:S(2)}, u32[]{:S(2)}) collective-permute-start(bf16[2,48,1536]{2,1,0:T(8,128)(2,1)S(1)} %pad_maximum_fusion.1.rest_0_), channel_id=1, source_target_pairs={{0,4},{2,6},{4,0},{6,2},{8,12},{10,14},{12,8},{14,10},{16,20},{18,... | collective-permute-start | bytes 884744 | tf_op jit(solution)/shard_map/ppermute | solution.py:22
  34.8 13.0 %collective-permute-start.7 = (bf16[2,48,1536]{2,1,0:T(8,128)(2,1)S(1)}, bf16[2,48,1536]{2,1,0:T(8,128)(2,1)S(1)}, u32[]{:S(2)}, u32[]{:S(2)}) collective-permute-start(bf16[2,48,1536]{2,1,0:T(8,128)(2,1)S(1)} %collective-permute-done.5.rest_5_), channel_id=1, source_target_pairs={{0,2},{2,0},{4,6},{6,4},{8,10},{10,8},{12,14},{14,12},{16,18},{18,... | collective-permute-start | bytes 884744 | tf_op jit(solution)/shard_map/ppermute | solution.py:22
  36.3 11.5 %collective-permute-start.8 = (bf16[2,48,1536]{2,1,0:T(8,128)(2,1)S(1)}, bf16[2,48,1536]{2,1,0:T(8,128)(2,1)S(1)}, u32[]{:S(2)}, u32[]{:S(2)}) collective-permute-start(bf16[2,48,1536]{2,1,0:T(8,128)(2,1)S(1)} %collective-permute-done.1.rest_2_), channel_id=1, source_target_pairs={{0,4},{2,6},{4,0},{6,2},{8,12},{10,14},{12,8},{14,10},{16,20},{18,... | collective-permute-start | bytes 884744 | tf_op jit(solution)/shard_map/ppermute | solution.py:22
  47.8 11.9 %collective-permute-start.12 = (bf16[2,48,1536]{2,1,0:T(8,128)(2,1)S(1)}, bf16[2,48,1536]{2,1,0:T(8,128)(2,1)S(1)}, u32[]{:S(2)}, u32[]{:S(2)}) collective-permute-start(bf16[2,48,1536]{2,1,0:T(8,128)(2,1)S(1)} %collective-permute-done.9.rest_1_), channel_id=1, source_target_pairs={{0,2},{2,0},{4,6},{6,4},{8,10},{10,8},{12,14},{14,12},{16,18},{18,... | collective-permute-start | bytes 884744 | tf_op jit(solution)/shard_map/ppermute | solution.py:22
  48.3 11.4 %collective-permute-start.13 = (bf16[2,48,1536]{2,1,0:T(8,128)(2,1)S(1)}, bf16[2,48,1536]{2,1,0:T(8,128)(2,1)S(1)}, u32[]{:S(2)}, u32[]{:S(2)}) collective-permute-start(bf16[2,48,1536]{2,1,0:T(8,128)(2,1)S(1)} %collective-permute-done.10.rest_2_), channel_id=1, source_target_pairs={{0,4},{2,6},{4,0},{6,2},{8,12},{10,14},{12,8},{14,10},{16,20},{18,... | collective-permute-start | bytes 884744 | tf_op jit(solution)/shard_map/ppermute | solution.py:22
  49.5 10.2 %collective-permute-start.17 = (bf16[2,48,1536]{2,1,0:T(8,128)(2,1)S(1)}, bf16[2,48,1536]{2,1,0:T(8,128)(2,1)S(1)}, u32[]{:S(2)}, u32[]{:S(2)}) collective-permute-start(bf16[2,48,1536]{2,1,0:T(8,128)(2,1)S(1)} %pad_maximum_fusion.2.rest_0_), channel_id=1, source_target_pairs={{0,4},{2,6},{4,0},{6,2},{8,12},{10,14},{12,8},{14,10},{16,20},{18,... | collective-permute-start | bytes 884744 | tf_op jit(solution)/shard_map/ppermute | solution.py:22
  50.4 9.3 %collective-permute-start.16 = (bf16[2,48,1536]{2,1,0:T(8,128)(2,1)S(1)}, bf16[2,48,1536]{2,1,0:T(8,128)(2,1)S(1)}, u32[]{:S(2)}, u32[]{:S(2)}) collective-permute-start(bf16[2,48,1536]{2,1,0:T(8,128)(2,1)S(1)} %pad_maximum_fusion.2.rest_0_), channel_id=1, source_target_pairs={{0,2},{2,0},{4,6},{6,4},{8,10},{10,8},{12,14},{14,12},{16,18},{18,... | collective-permute-start | bytes 884744 | tf_op jit(solution)/shard_map/ppermute | solution.py:22
  59.7 9.8 %collective-permute-start.21 = (bf16[1024,768]{1,0:T(8,128)(2,1)S(1)}, bf16[1024,768]{1,0:T(8,128)(2,1)S(1)}, u32[]{:S(2)}, u32[]{:S(2)}) collective-permute-start(bf16[1024,768]{1,0:T(8,128)(2,1)S(1)} %get-tuple-element.207.own_ref), channel_id=1, source_target_pairs={{0,1},{1,0},{2,3},{3,2},{4,5},{5,4},{6,7},{7,6},{8,9},{9,8},{10,11... | collective-permute-start | bytes 4718600 | tf_op jit(solution)/shard_map/ppermute | solution.py:34
  59.8 9.4 %collective-permute-start.18 = (bf16[2,48,1536]{2,1,0:T(8,128)(2,1)S(1)}, bf16[2,48,1536]{2,1,0:T(8,128)(2,1)S(1)}, u32[]{:S(2)}, u32[]{:S(2)}) collective-permute-start(bf16[2,48,1536]{2,1,0:T(8,128)(2,1)S(1)} %collective-permute-done.9.rest_1_), channel_id=1, source_target_pairs={{0,4},{2,6},{4,0},{6,2},{8,12},{10,14},{12,8},{14,10},{16,20},{18,... | collective-permute-start | bytes 884744 | tf_op jit(solution)/shard_map/ppermute | solution.py:22
  69.5 10.0 %collective-permute-start.24 = (bf16[2,48,1536]{2,1,0:T(8,128)(2,1)S(1)}, bf16[2,48,1536]{2,1,0:T(8,128)(2,1)S(1)}, u32[]{:S(2)}, u32[]{:S(2)}) collective-permute-start(bf16[2,48,1536]{2,1,0:T(8,128)(2,1)S(1)} %collective-permute-done.19.rest_6_), channel_id=1, source_target_pairs={{0,8},{2,10},{4,12},{6,14},{8,0},{10,2},{12,4},{14,6},{16,24},{18,... | collective-permute-start | bytes 884744 | tf_op jit(solution)/shard_map/ppermute | solution.py:22
  89.5 15.6 %collective-permute-start.27 = (bf16[4,48,1536]{2,1,0:T(8,128)(2,1)S(1)}, bf16[4,48,1536]{2,1,0:T(8,128)(2,1)S(1)}, u32[]{:S(2)}, u32[]{:S(2)}) collective-permute-start(bf16[4,48,1536]{2,1,0:T(8,128)(2,1)S(1)} %get-tuple-element.239), channel_id=1, source_target_pairs={{0,2},{2,0},{4,6},{6,4},{8,10},{10,8},{12,14},{14,12},{16,18},{18,... | collective-permute-start | bytes 1769480 | tf_op jit(solution)/shard_map/ppermute | solution.py:22
  90.6 15.3 %collective-permute-start.28 = (bf16[4,48,1536]{2,1,0:T(8,128)(2,1)S(1)}, bf16[4,48,1536]{2,1,0:T(8,128)(2,1)S(1)}, u32[]{:S(2)}, u32[]{:S(2)}) collective-permute-start(bf16[4,48,1536]{2,1,0:T(8,128)(2,1)S(1)} %get-tuple-element.240), channel_id=1, source_target_pairs={{0,4},{2,6},{4,0},{6,2},{8,12},{10,14},{12,8},{14,10},{16,20},{18,... | collective-permute-start | bytes 1769480 | tf_op jit(solution)/shard_map/ppermute | solution.py:22
  105.9 22.7 %collective-permute-start.29 = (bf16[4,48,1536]{2,1,0:T(8,128)(2,1)S(1)}, bf16[4,48,1536]{2,1,0:T(8,128)(2,1)S(1)}, u32[]{:S(2)}, u32[]{:S(2)}) collective-permute-start(bf16[4,48,1536]{2,1,0:T(8,128)(2,1)S(1)} %get-tuple-element.248), channel_id=1, source_target_pairs={{0,2},{2,0},{4,6},{6,4},{8,10},{10,8},{12,14},{14,12},{16,18},{18,... | collective-permute-start | bytes 1769480 | tf_op jit(solution)/shard_map/ppermute | solution.py:22
  106.9 21.8 %collective-permute-start.30 = (bf16[4,48,1536]{2,1,0:T(8,128)(2,1)S(1)}, bf16[4,48,1536]{2,1,0:T(8,128)(2,1)S(1)}, u32[]{:S(2)}, u32[]{:S(2)}) collective-permute-start(bf16[4,48,1536]{2,1,0:T(8,128)(2,1)S(1)} %get-tuple-element.249), channel_id=1, source_target_pairs={{0,4},{2,6},{4,0},{6,2},{8,12},{10,14},{12,8},{14,10},{16,20},{18,... | collective-permute-start | bytes 1769480 | tf_op jit(solution)/shard_map/ppermute | solution.py:22
  107.3 20.7 %collective-permute-start.31 = (bf16[2,48,1536]{2,1,0:T(8,128)(2,1)S(1)}, bf16[2,48,1536]{2,1,0:T(8,128)(2,1)S(1)}, u32[]{:S(2)}, u32[]{:S(2)}) collective-permute-start(bf16[2,48,1536]{2,1,0:T(8,128)(2,1)S(1)} %get-tuple-element.254), channel_id=1, source_target_pairs={{0,2},{2,0},{4,6},{6,4},{8,10},{10,8},{12,14},{14,12},{16,18},{18,... | collective-permute-start | bytes 884744 | tf_op jit(solution)/shard_map/ppermute | solution.py:22
  108.5 20.2 %collective-permute-start.32 = (bf16[2,48,1536]{2,1,0:T(8,128)(2,1)S(1)}, bf16[2,48,1536]{2,1,0:T(8,128)(2,1)S(1)}, u32[]{:S(2)}, u32[]{:S(2)}) collective-permute-start(bf16[2,48,1536]{2,1,0:T(8,128)(2,1)S(1)} %get-tuple-element.255), channel_id=1, source_target_pairs={{0,4},{2,6},{4,0},{6,2},{8,12},{10,14},{12,8},{14,10},{16,20},{18,... | collective-permute-start | bytes 884744 | tf_op jit(solution)/shard_map/ppermute | solution.py:22
  138.3 16.8 %collective-permute-start.38 = (bf16[4,48,1664]{2,1,0:T(8,128)(2,1)S(1)}, bf16[4,48,1664]{2,1,0:T(8,128)(2,1)S(1)}, u32[]{:S(2)}, u32[]{:S(2)}) collective-permute-start(bf16[4,48,1664]{2,1,0:T(8,128)(2,1)S(1)} %get-tuple-element.291), channel_id=1, source_target_pairs={{0,2},{2,0},{4,6},{6,4},{8,10},{10,8},{12,14},{14,12},{16,18},{18,... | collective-permute-start | bytes 1916936 | tf_op jit(solution)/shard_map/ppermute | solution.py:22
  139.3 15.8 %collective-permute-start.39 = (bf16[4,48,1536]{2,1,0:T(8,128)(2,1)S(1)}, bf16[4,48,1536]{2,1,0:T(8,128)(2,1)S(1)}, u32[]{:S(2)}, u32[]{:S(2)}) collective-permute-start(bf16[4,48,1536]{2,1,0:T(8,128)(2,1)S(1)} %get-tuple-element.292), channel_id=1, source_target_pairs={{0,4},{2,6},{4,0},{6,2},{8,12},{10,14},{12,8},{14,10},{16,20},{18,... | collective-permute-start | bytes 1769480 | tf_op jit(solution)/shard_map/ppermute | solution.py:22
  141.0 14.1 %collective-permute-start.40 = (bf16[2,48,1536]{2,1,0:T(8,128)(2,1)S(1)}, bf16[2,48,1536]{2,1,0:T(8,128)(2,1)S(1)}, u32[]{:S(2)}, u32[]{:S(2)}) collective-permute-start(bf16[2,48,1536]{2,1,0:T(8,128)(2,1)S(1)} %get-tuple-element.293), channel_id=1, source_target_pairs={{0,8},{2,10},{4,12},{6,14},{8,0},{10,2},{12,4},{14,6},{16,24},{18,... | collective-permute-start | bytes 884744 | tf_op jit(solution)/shard_map/ppermute | solution.py:22
  141.7 13.3 %collective-permute-start.41 = (bf16[48,1536]{1,0:T(8,128)(2,1)S(1)}, bf16[48,1536]{1,0:T(8,128)(2,1)S(1)}, u32[]{:S(2)}, u32[]{:S(2)}) collective-permute-start(bf16[48,1536]{1,0:T(8,128)(2,1)S(1)} %get-tuple-element.296), channel_id=1, source_target_pairs={{0,24},{2,26},{4,28},{6,30},{8,16},{10,18},{12,20},{14,22},{16,8},... | collective-permute-start | bytes 442376 | tf_op jit(solution)/shard_map/ppermute | solution.py:22
  155.2 10.1 %collective-permute-start.44 = (bf16[2,48,1664]{2,1,0:T(8,128)(2,1)S(1)}, bf16[2,48,1664]{2,1,0:T(8,128)(2,1)S(1)}, u32[]{:S(2)}, u32[]{:S(2)}) collective-permute-start(bf16[2,48,1664]{2,1,0:T(8,128)(2,1)S(1)} %get-tuple-element.311), channel_id=1, source_target_pairs={{0,4},{2,6},{4,0},{6,2},{8,12},{10,14},{12,8},{14,10},{16,20},{18,... | collective-permute-start | bytes 958472 | tf_op jit(solution)/shard_map/ppermute | solution.py:22
  (35 other events, 276.9 us)

commit v5 on v4

--- a/solution.py
+++ b/solution.py
@@ -220,14 +220,12 @@
 def down_body(me_ref, act_ref, *rest):
     pieces, (w_ref, part_ref) = rest[:-2], rest[-2:]
     fill(me_ref[0], pieces, w_ref)
-    for rows in chunks(part_ref.shape[0]):
-        part_ref[rows] = dot_t(act_ref[rows], w_ref[...]).astype(B16)
+    part_ref[...] = dot_t(act_ref[: part_ref.shape[0]], w_ref[...]).astype(B16)
 
 
 def down_rest_body(act_ref, w_ref, part_ref):
     half = part_ref.shape[0]
-    for rows in chunks(half):
-        part_ref[rows] = dot_t(act_ref[half + rows.start : half + rows.stop], w_ref[...]).astype(B16)
+    part_ref[...] = dot_t(act_ref[half:], w_ref[...]).astype(B16)
 
 
 def down(me, act, pieces):
@@ -290,6 +288,8 @@
     wide = [] if vector is None else [vector]
     keep = turned is None and len(groups) < len(ORDER)
     wanted = [offset for offsets in groups for offset in offsets]
+    if keep and total % (2 * tile) == 0:
+        tile *= 2
 
     def body(me_ref, *refs):
         left_refs, right_refs = list(refs[: len(flat)]), refs[len(flat) : len(flat) + n]

time: 184 us -> 183 us (level)
  no operation moved by 1% of the time
where the time goes in v5:
time: 183 us
  waiting for transfers between devices  59.7 us (33%)
  starting transfers between devices  58.1 us (32%)
  Pallas kernels  57.1 us (31%)
  other arithmetic  6.2 us (3%)
    ppermute x42, waiting for transfers between devices, swap(): return lax.ppermute(values, 'dp', [(i, i ^ bit) for i in range(BLOCKS)])  58.2 us
    ppermute x42, starting transfers between devices, swap(): return lax.ppermute(values, 'dp', [(i, i ^ bit) for i in range(BLOCKS)])  57.4 us
    pallas_call x24, Pallas kernels, call(): pl.pallas_call(body, in_specs=[SMEM_SPEC if member.dtype == jnp.int32 and...  57.1 us
  transfers between devices with their start and end apart: 48, of which 24 were waited for; matrix products, arithmetic and copies ran while one was open for 3% of the time, Pallas kernels for 28%

profile of v5, /device:TPU:0, one launch (start us, length us, event | category | flops | bytes accessed | tf_op | source)
XLA Modules:
  0.0 182.7 jit_solution(3372063574054830328)
XLA Ops:
  1.5 5.1 %collective-permute-start = (bf16[48,1536]{1,0:T(8,128)(2,1)S(1)}, bf16[48,1536]{1,0:T(8,128)(2,1)S(1)}, u32[]{:S(2)}, u32[]{:S(2)}) collective-permute-start(bf16[48,1536]{1,0:T(8,128)(2,1)S(1)} %get-tuple-element.347), channel_id=1, source_target_pairs={{0,24},{2,26},{4,28},{6,30},{8,16},{10,18},{12,20},{14,22},{16,8},... | collective-permute-start | bytes 442376 | tf_op jit(solution)/shard_map/ppermute | solution.py:22
  11.0 2.7 %collective-permute-start.3 = (bf16[2,48,1536]{2,1,0:T(8,128)(2,1)S(1)}, bf16[2,48,1536]{2,1,0:T(8,128)(2,1)S(1)}, u32[]{:S(2)}, u32[]{:S(2)}) collective-permute-start(bf16[2,48,1536]{2,1,0:T(8,128)(2,1)S(1)} %pad_maximum_fusion.rest_0_), channel_id=1, source_target_pairs={{0,8},{2,10},{4,12},{6,14},{8,0},{10,2},{12,4},{14,6},{16,24},{18,... | collective-permute-start | bytes 884744 | tf_op jit(solution)/shard_map/ppermute | solution.py:22
  16.7 3.3 %collective-permute-done.3.rest_1_ = bf16[2,48,1536]{2,1,0:T(8,128)(2,1)S(1)} collective-permute-done((bf16[2,48,1536]{2,1,0:T(8,128)(2,1)S(1)}, bf16[2,48,1536]{2,1,0:T(8,128)(2,1)S(1)}, u32[]{:S(2)}, u32[]{:S(2)}) %collective-permute-start.3) | collective-permute-done | bytes 294944 | tf_op jit(solution)/shard_map/ppermute | solution.py:22
  26.4 6.1 %collective-permute-done.6 = bf16[48,1536]{1,0:T(8,128)(2,1)S(1)} collective-permute-done((bf16[48,1536]{1,0:T(8,128)(2,1)S(1)}, bf16[48,1536]{1,0:T(8,128)(2,1)S(1)}, u32[]{:S(2)}, u32[]{:S(2)}) %collective-permute-start.6) | collective-permute-done | bytes 147488 | tf_op jit(solution)/shard_map/ppermute | solution.py:22
  36.7 4.2 %collective-permute-done.9.rest_1_ = bf16[2,48,1536]{2,1,0:T(8,128)(2,1)S(1)} collective-permute-done((bf16[2,48,1536]{2,1,0:T(8,128)(2,1)S(1)}, bf16[2,48,1536]{2,1,0:T(8,128)(2,1)S(1)}, u32[]{:S(2)}, u32[]{:S(2)}) %collective-permute-start.9) | collective-permute-done | bytes 294944 | tf_op jit(solution)/shard_map/ppermute | solution.py:22
  41.8 6.0 %collective-permute-done.7.rest_7_ = bf16[2,48,1536]{2,1,0:T(8,128)(2,1)S(1)} collective-permute-done((bf16[2,48,1536]{2,1,0:T(8,128)(2,1)S(1)}, bf16[2,48,1536]{2,1,0:T(8,128)(2,1)S(1)}, u32[]{:S(2)}, u32[]{:S(2)}) %collective-permute-start.7) | collective-permute-done | bytes 294944 | tf_op jit(solution)/shard_map/ppermute | solution.py:22
  54.0 5.7 %attend.1 = (bf16[768,1536]{1,0:T(8,128)(2,1)S(1)}, bf16[1024,1152]{1,0:T(8,128)(2,1)S(1)}, bf16[1024,768]{1,0:T(8,128)(2,1)S(1)}, bf16[1024,384]{1,0:T(8,128)(2,1)S(1)}, bf16[1024,768]{1,0:T(8,128)(2,1)S(1)}) custom-call(s32[1]{0:T(128)} %bitcast.1.me_ref, s32[8]{0:T(128)S(1)} %copy-done.1, bf16[1024,768]{1,0:T(8,128)(2,1)S(1)} %broadcast_select_fusion.in_ref.refs_0_, ...), custom_call_target="tpu_custom_call" | custom-call | flops 1 | bytes 1 | tf_op jit(solution)/shard_map/attend/pallas_call | solution.py:55
  62.1 7.1 %collective-permute-done.18.rest_5_ = bf16[2,48,1536]{2,1,0:T(8,128)(2,1)S(1)} collective-permute-done((bf16[2,48,1536]{2,1,0:T(8,128)(2,1)S(1)}, bf16[2,48,1536]{2,1,0:T(8,128)(2,1)S(1)}, u32[]{:S(2)}, u32[]{:S(2)}) %collective-permute-start.18) | collective-permute-done | bytes 294944 | tf_op jit(solution)/shard_map/ppermute | solution.py:22
  73.6 5.8 %up.1 = (bf16[768,1536]{1,0:T(8,128)(2,1)S(1)}, f32[1024,768]{1,0:T(8,128)S(1)}, f32[1024,128]{1,0:T(8,128)S(1)}, bf16[1024,768]{1,0:T(8,128)(2,1)S(1)}, bf16[10...) custom-call(s32[1]{0:T(128)} %bitcast.1.me_ref, bf16[1024,768]{1,0:T(8,128)(2,1)S(1)} %broadcast_select_fusion.in_ref.refs_0_, ...), custom_call_target="tpu_custom_call" | custom-call | flops 1 | bytes 1 | tf_op jit(solution)/shard_map/up/pallas_call | solution.py:55
  90.5 2.4 %weight_grad.6 = (bf16[2,48,1536]{2,1,0:T(8,128)(2,1)S(1)}, bf16[2,48,1536]{2,1,0:T(8,128)(2,1)S(1)}, bf16[4,48,1536]{2,1,0:T(8,128)(2,1)S(1)}) custom-call(s32[1]{0:T(128)} %bitcast.1.me_ref, bf16[768,1024]{1,0:T(8,128)(2,1)S(1)} %get-tuple-element.244.refs_0_, bf16[1024,1536]{1,0:T(8,128)(2,1)S(1)} %get-tuple-element.220.act_ref.refs_2_.refs_1_), custom_call_target="tpu_custom_call" | custom-call | flops 1 | bytes 1 | tf_op jit(solution)/shard_map/weight_grad/pallas_call | solution.py:55
  92.9 6.3 %hidden_back.1 = (bf16[1024,1536]{1,0:T(8,128)(2,1)S(1)}, bf16[1024,768]{1,0:T(8,128)(2,1)S(1)}, f32[8,1536]{1,0:T(8,128)S(1)}) custom-call(bf16[512,768]{1,0:T(8,128)(2,1)S(1)} %get-tuple-element.233.refs_0_.low_a_ref, bf16[512,768]{1,0:T(8,128)(2,1)S(1)} %get-tuple-element.234.refs_1_.low_b_ref, bf16[1024,1536]{1,0:T(8,128)(2,1)S(1)} %get-tuple-element.235.slope_ref, ...), custom_call_target="tpu_custom_call" | custom-call | flops 1 | bytes 1 | tf_op jit(solution)/shard_map/hidden_back/pallas_call | solution.py:55
  99.2 4.5 %weight_grad.5 = (bf16[4,48,1536]{2,1,0:T(8,128)(2,1)S(1)}, bf16[4,48,1536]{2,1,0:T(8,128)(2,1)S(1)}, bf16[2,48,1536]{2,1,0:T(8,128)(2,1)S(1)}, bf16[2,48,1536]{2,1,0:T(8,128)(2,1)S(1)}, bf16[4,48,1536]{2,1,0:T(8,128)(2,1)S(1)}) custom-call(s32[1]{0:T(128)} %bitcast.1.me_ref, bf16[1024,768]{1,0:T(8,128)(2,1)S(1)} %get-tuple-element.215.refs_0_, ...), custom_call_target="tpu_custom_call" | custom-call | flops 1 | bytes 1 | tf_op jit(solution)/shard_map/weight_grad/pallas_call | solution.py:55
  109.8 15.4 %attend_back.1 = (f32[1024,768]{1,0:T(8,128)S(1)}, bf16[1024,768]{1,0:T(8,128)(2,1)S(1)}, bf16[1024,1152]{1,0:T(8,128)(2,1)S(1)}, bf16[1024,768]{1,0:T(8,128)(2,...) custom-call(f32[512,768]{1,0:T(8,128)S(1)} %get-tuple-element.256.dz_a_ref, ...), custom_call_target="tpu_custom_call" | custom-call | flops 1 | bytes 1 | tf_op jit(solution)/shard_map/attend_back/pallas_call | solution.py:55
  125.2 2.3 %collective-permute-done.31.late_x_ref = bf16[2,48,1536]{2,1,0:T(8,128)(2,1)S(1)} collective-permute-done((bf16[2,48,1536]{2,1,0:T(8,128)(2,1)S(1)}, bf16[2,48,1536]{2,1,0:T(8,128)(2,1)S(1)}, u32[]{:S(2)}, u32[]{:S(2)}) %collective-permute-start.31) | collective-permute-done | bytes 294944 | tf_op jit(solution)/shard_map/ppermute | solution.py:22
  132.4 3.9 %weight_grad.7 = (bf16[4,48,1664]{2,1,0:T(8,128)(2,1)S(1)}, bf16[4,48,1536]{2,1,0:T(8,128)(2,1)S(1)}, bf16[2,48,1536]{2,1,0:T(8,128)(2,1)S(1)}, bf16[2,48,1536]{2,1,0:T(8,128)(2,1)S(1)}, bf16[4,48,1536]{2,1,0:T(8,128)(2,1)S(1)}) custom-call(s32[1]{0:T(128)} %bitcast.1.me_ref, bf16[1024,768]{1,0:T(8,128)(2,1)S(1)} %broadcast_select_fusion.in_ref.refs_0_, ...), custom_call_target="tpu_custom_call" | custom-call | flops 1 | bytes 1 | tf_op jit(solution)/shard_map/weight_grad/pallas_call | solution.py:55
  141.3 3.5 %collective-permute-start.41 = (bf16[48,1536]{1,0:T(8,128)(2,1)S(1)}, bf16[48,1536]{1,0:T(8,128)(2,1)S(1)}, u32[]{:S(2)}, u32[]{:S(2)}) collective-permute-start(bf16[48,1536]{1,0:T(8,128)(2,1)S(1)} %get-tuple-element.296), channel_id=1, source_target_pairs={{0,24},{2,26},{4,28},{6,30},{8,16},{10,18},{12,20},{14,22},{16,8},... | collective-permute-start | bytes 442376 | tf_op jit(solution)/shard_map/ppermute | solution.py:22
  144.8 2.8 %last.1 = (f32[1024,768]{1,0:T(8,128)}, bf16[1024,768]{1,0:T(8,128)(2,1)}) custom-call(f32[1024,768]{1,0:T(8,128)S(1)} %get-tuple-element.297.dz_ref, bf16[1024,768]{1,0:T(8,128)(2,1)S(1)} %get-tuple-element.298.own_ref, bf16[1024,768]{1,0:T(8,128)(2,1)S(1)} %collective-permute-done.42.other_ref, f32[1024,128]{1,0:T(8,128)S(1)} %broadcast_in_dim.36.flag_ref, ...), custom_call_target="tpu_custom_call" | custom-call | flops 1 | bytes 1 | tf_op jit(solution)/shard_map/last/pallas_call | solution.py:55
  147.6 7.0 %collective-permute-done.41 = bf16[48,1536]{1,0:T(8,128)(2,1)S(1)} collective-permute-done((bf16[48,1536]{1,0:T(8,128)(2,1)S(1)}, bf16[48,1536]{1,0:T(8,128)(2,1)S(1)}, u32[]{:S(2)}, u32[]{:S(2)}) %collective-permute-start.41) | collective-permute-done | bytes 147488 | tf_op jit(solution)/shard_map/ppermute | solution.py:22
  157.6 3.5 %collective-permute-start.45 = (bf16[48,1536]{1,0:T(8,128)(2,1)S(1)}, bf16[48,1536]{1,0:T(8,128)(2,1)S(1)}, u32[]{:S(2)}, u32[]{:S(2)}) collective-permute-start(bf16[48,1536]{1,0:T(8,128)(2,1)S(1)} %get-tuple-element.314), channel_id=1, source_target_pairs={{0,24},{2,26},{4,28},{6,30},{8,16},{10,18},{12,20},{14,22},{16,8},... | collective-permute-start | bytes 442376 | tf_op jit(solution)/shard_map/ppermute | solution.py:22
  161.1 3.6 %collective-permute-done.45 = bf16[48,1536]{1,0:T(8,128)(2,1)S(1)} collective-permute-done((bf16[48,1536]{1,0:T(8,128)(2,1)S(1)}, bf16[48,1536]{1,0:T(8,128)(2,1)S(1)}, u32[]{:S(2)}, u32[]{:S(2)}) %collective-permute-start.45) | collective-permute-done | bytes 147488 | tf_op jit(solution)/shard_map/ppermute | solution.py:22
  165.2 2.3 %collective-permute-start.46 = (bf16[2,48,1664]{2,1,0:T(8,128)(2,1)S(1)}, bf16[2,48,1664]{2,1,0:T(8,128)(2,1)S(1)}, u32[]{:S(2)}, u32[]{:S(2)}) collective-permute-start(bf16[2,48,1664]{2,1,0:T(8,128)(2,1)S(1)} %get-tuple-element.319), channel_id=1, source_target_pairs={{0,8},{2,10},{4,12},{6,14},{8,0},{10,2},{12,4},{14,6},{16,24},{18,... | collective-permute-start | bytes 958472 | tf_op jit(solution)/shard_map/ppermute | solution.py:22
  168.3 6.0 %collective-permute-done.46.mid_ref = bf16[2,48,1664]{2,1,0:T(8,128)(2,1)S(1)} collective-permute-done((bf16[2,48,1664]{2,1,0:T(8,128)(2,1)S(1)}, bf16[2,48,1664]{2,1,0:T(8,128)(2,1)S(1)}, u32[]{:S(2)}, u32[]{:S(2)}) %collective-permute-start.46) | collective-permute-done | bytes 319520 | tf_op jit(solution)/shard_map/ppermute | solution.py:22
  174.4 2.4 %collective-permute-start.47 = (bf16[48,1792]{1,0:T(8,128)(2,1)S(1)}, bf16[48,1792]{1,0:T(8,128)(2,1)S(1)}, u32[]{:S(2)}, u32[]{:S(2)}) collective-permute-start(bf16[48,1792]{1,0:T(8,128)(2,1)S(1)} %get-tuple-element.325), channel_id=1, source_target_pairs={{0,24},{2,26},{4,28},{6,30},{8,16},{10,18},{12,20},{14,22},{16,8},... | collective-permute-start | bytes 516104 | tf_op jit(solution)/shard_map/ppermute | solution.py:22
  177.5 4.2 %collective-permute-done.47.far_ref = bf16[48,1792]{1,0:T(8,128)(2,1)S(1)} collective-permute-done((bf16[48,1792]{1,0:T(8,128)(2,1)S(1)}, bf16[48,1792]{1,0:T(8,128)(2,1)S(1)}, u32[]{:S(2)}, u32[]{:S(2)}) %collective-permute-start.47) | collective-permute-done | bytes 172064 | tf_op jit(solution)/shard_map/ppermute | solution.py:22
  (142 shorter events, 65.1 us)
Async XLA Ops:
  1.5 9.2 %collective-permute-start = (bf16[48,1536]{1,0:T(8,128)(2,1)S(1)}, bf16[48,1536]{1,0:T(8,128)(2,1)S(1)}, u32[]{:S(2)}, u32[]{:S(2)}) collective-permute-start(bf16[48,1536]{1,0:T(8,128)(2,1)S(1)} %get-tuple-element.347), channel_id=1, source_target_pairs={{0,24},{2,26},{4,28},{6,30},{8,16},{10,18},{12,20},{14,22},{16,8},... | collective-permute-start | bytes 442376 | tf_op jit(solution)/shard_map/ppermute | solution.py:22
  22.7 9.8 %collective-permute-start.5 = (bf16[2,48,1536]{2,1,0:T(8,128)(2,1)S(1)}, bf16[2,48,1536]{2,1,0:T(8,128)(2,1)S(1)}, u32[]{:S(2)}, u32[]{:S(2)}) collective-permute-start(bf16[2,48,1536]{2,1,0:T(8,128)(2,1)S(1)} %collective-permute-done.3.rest_1_), channel_id=1, source_target_pairs={{0,4},{2,6},{4,0},{6,2},{8,12},{10,14},{12,8},{14,10},{16,20},{18,... | collective-permute-start | bytes 884744 | tf_op jit(solution)/shard_map/ppermute | solution.py:22
  23.2 9.3 %collective-permute-start.4 = (bf16[2,48,1536]{2,1,0:T(8,128)(2,1)S(1)}, bf16[2,48,1536]{2,1,0:T(8,128)(2,1)S(1)}, u32[]{:S(2)}, u32[]{:S(2)}) collective-permute-start(bf16[2,48,1536]{2,1,0:T(8,128)(2,1)S(1)} %collective-permute-done.3.rest_1_), channel_id=1, source_target_pairs={{0,2},{2,0},{4,6},{6,4},{8,10},{10,8},{12,14},{14,12},{16,18},{18,... | collective-permute-start | bytes 884744 | tf_op jit(solution)/shard_map/ppermute | solution.py:22
  32.6 9.2 %collective-permute-start.11 = (bf16[2,48,1536]{2,1,0:T(8,128)(2,1)S(1)}, bf16[2,48,1536]{2,1,0:T(8,128)(2,1)S(1)}, u32[]{:S(2)}, u32[]{:S(2)}) collective-permute-start(bf16[2,48,1536]{2,1,0:T(8,128)(2,1)S(1)} %pad_maximum_fusion.1.rest_0_), channel_id=1, source_target_pairs={{0,4},{2,6},{4,0},{6,2},{8,12},{10,14},{12,8},{14,10},{16,20},{18,... | collective-permute-start | bytes 884744 | tf_op jit(solution)/shard_map/ppermute | solution.py:22
  34.8 13.0 %collective-permute-start.7 = (bf16[2,48,1536]{2,1,0:T(8,128)(2,1)S(1)}, bf16[2,48,1536]{2,1,0:T(8,128)(2,1)S(1)}, u32[]{:S(2)}, u32[]{:S(2)}) collective-permute-start(bf16[2,48,1536]{2,1,0:T(8,128)(2,1)S(1)} %collective-permute-done.5.rest_5_), channel_id=1, source_target_pairs={{0,2},{2,0},{4,6},{6,4},{8,10},{10,8},{12,14},{14,12},{16,18},{18,... | collective-permute-start | bytes 884744 | tf_op jit(solution)/shard_map/ppermute | solution.py:22
  36.3 11.5 %collective-permute-start.8 = (bf16[2,48,1536]{2,1,0:T(8,128)(2,1)S(1)}, bf16[2,48,1536]{2,1,0:T(8,128)(2,1)S(1)}, u32[]{:S(2)}, u32[]{:S(2)}) collective-permute-start(bf16[2,48,1536]{2,1,0:T(8,128)(2,1)S(1)} %collective-permute-done.1.rest_2_), channel_id=1, source_target_pairs={{0,4},{2,6},{4,0},{6,2},{8,12},{10,14},{12,8},{14,10},{16,20},{18,... | collective-permute-start | bytes 884744 | tf_op jit(solution)/shard_map/ppermute | solution.py:22
  47.8 11.9 %collective-permute-start.12 = (bf16[2,48,1536]{2,1,0:T(8,128)(2,1)S(1)}, bf16[2,48,1536]{2,1,0:T(8,128)(2,1)S(1)}, u32[]{:S(2)}, u32[]{:S(2)}) collective-permute-start(bf16[2,48,1536]{2,1,0:T(8,128)(2,1)S(1)} %collective-permute-done.9.rest_1_), channel_id=1, source_target_pairs={{0,2},{2,0},{4,6},{6,4},{8,10},{10,8},{12,14},{14,12},{16,18},{18,... | collective-permute-start | bytes 884744 | tf_op jit(solution)/shard_map/ppermute | solution.py:22
  48.3 11.4 %collective-permute-start.13 = (bf16[2,48,1536]{2,1,0:T(8,128)(2,1)S(1)}, bf16[2,48,1536]{2,1,0:T(8,128)(2,1)S(1)}, u32[]{:S(2)}, u32[]{:S(2)}) collective-permute-start(bf16[2,48,1536]{2,1,0:T(8,128)(2,1)S(1)} %collective-permute-done.10.rest_2_), channel_id=1, source_target_pairs={{0,4},{2,6},{4,0},{6,2},{8,12},{10,14},{12,8},{14,10},{16,20},{18,... | collective-permute-start | bytes 884744 | tf_op jit(solution)/shard_map/ppermute | solution.py:22
  49.5 10.2 %collective-permute-start.17 = (bf16[2,48,1536]{2,1,0:T(8,128)(2,1)S(1)}, bf16[2,48,1536]{2,1,0:T(8,128)(2,1)S(1)}, u32[]{:S(2)}, u32[]{:S(2)}) collective-permute-start(bf16[2,48,1536]{2,1,0:T(8,128)(2,1)S(1)} %pad_maximum_fusion.2.rest_0_), channel_id=1, source_target_pairs={{0,4},{2,6},{4,0},{6,2},{8,12},{10,14},{12,8},{14,10},{16,20},{18,... | collective-permute-start | bytes 884744 | tf_op jit(solution)/shard_map/ppermute | solution.py:22
  50.4 9.3 %collective-permute-start.16 = (bf16[2,48,1536]{2,1,0:T(8,128)(2,1)S(1)}, bf16[2,48,1536]{2,1,0:T(8,128)(2,1)S(1)}, u32[]{:S(2)}, u32[]{:S(2)}) collective-permute-start(bf16[2,48,1536]{2,1,0:T(8,128)(2,1)S(1)} %pad_maximum_fusion.2.rest_0_), channel_id=1, source_target_pairs={{0,2},{2,0},{4,6},{6,4},{8,10},{10,8},{12,14},{14,12},{16,18},{18,... | collective-permute-start | bytes 884744 | tf_op jit(solution)/shard_map/ppermute | solution.py:22
  59.7 9.8 %collective-permute-start.21 = (bf16[1024,768]{1,0:T(8,128)(2,1)S(1)}, bf16[1024,768]{1,0:T(8,128)(2,1)S(1)}, u32[]{:S(2)}, u32[]{:S(2)}) collective-permute-start(bf16[1024,768]{1,0:T(8,128)(2,1)S(1)} %get-tuple-element.207.own_ref), channel_id=1, source_target_pairs={{0,1},{1,0},{2,3},{3,2},{4,5},{5,4},{6,7},{7,6},{8,9},{9,8},{10,11... | collective-permute-start | bytes 4718600 | tf_op jit(solution)/shard_map/ppermute | solution.py:34
  59.8 9.4 %collective-permute-start.18 = (bf16[2,48,1536]{2,1,0:T(8,128)(2,1)S(1)}, bf16[2,48,1536]{2,1,0:T(8,128)(2,1)S(1)}, u32[]{:S(2)}, u32[]{:S(2)}) collective-permute-start(bf16[2,48,1536]{2,1,0:T(8,128)(2,1)S(1)} %collective-permute-done.9.rest_1_), channel_id=1, source_target_pairs={{0,4},{2,6},{4,0},{6,2},{8,12},{10,14},{12,8},{14,10},{16,20},{18,... | collective-permute-start | bytes 884744 | tf_op jit(solution)/shard_map/ppermute | solution.py:22
  69.5 10.0 %collective-permute-start.24 = (bf16[2,48,1536]{2,1,0:T(8,128)(2,1)S(1)}, bf16[2,48,1536]{2,1,0:T(8,128)(2,1)S(1)}, u32[]{:S(2)}, u32[]{:S(2)}) collective-permute-start(bf16[2,48,1536]{2,1,0:T(8,128)(2,1)S(1)} %collective-permute-done.19.rest_6_), channel_id=1, source_target_pairs={{0,8},{2,10},{4,12},{6,14},{8,0},{10,2},{12,4},{14,6},{16,24},{18,... | collective-permute-start | bytes 884744 | tf_op jit(solution)/shard_map/ppermute | solution.py:22
  89.1 15.6 %collective-permute-start.27 = (bf16[4,48,1536]{2,1,0:T(8,128)(2,1)S(1)}, bf16[4,48,1536]{2,1,0:T(8,128)(2,1)S(1)}, u32[]{:S(2)}, u32[]{:S(2)}) collective-permute-start(bf16[4,48,1536]{2,1,0:T(8,128)(2,1)S(1)} %get-tuple-element.239), channel_id=1, source_target_pairs={{0,2},{2,0},{4,6},{6,4},{8,10},{10,8},{12,14},{14,12},{16,18},{18,... | collective-permute-start | bytes 1769480 | tf_op jit(solution)/shard_map/ppermute | solution.py:22
  90.2 15.3 %collective-permute-start.28 = (bf16[4,48,1536]{2,1,0:T(8,128)(2,1)S(1)}, bf16[4,48,1536]{2,1,0:T(8,128)(2,1)S(1)}, u32[]{:S(2)}, u32[]{:S(2)}) collective-permute-start(bf16[4,48,1536]{2,1,0:T(8,128)(2,1)S(1)} %get-tuple-element.240), channel_id=1, source_target_pairs={{0,4},{2,6},{4,0},{6,2},{8,12},{10,14},{12,8},{14,10},{16,20},{18,... | collective-permute-start | bytes 1769480 | tf_op jit(solution)/shard_map/ppermute | solution.py:22
  105.5 22.7 %collective-permute-start.29 = (bf16[4,48,1536]{2,1,0:T(8,128)(2,1)S(1)}, bf16[4,48,1536]{2,1,0:T(8,128)(2,1)S(1)}, u32[]{:S(2)}, u32[]{:S(2)}) collective-permute-start(bf16[4,48,1536]{2,1,0:T(8,128)(2,1)S(1)} %get-tuple-element.248), channel_id=1, source_target_pairs={{0,2},{2,0},{4,6},{6,4},{8,10},{10,8},{12,14},{14,12},{16,18},{18,... | collective-permute-start | bytes 1769480 | tf_op jit(solution)/shard_map/ppermute | solution.py:22
  106.5 21.8 %collective-permute-start.30 = (bf16[4,48,1536]{2,1,0:T(8,128)(2,1)S(1)}, bf16[4,48,1536]{2,1,0:T(8,128)(2,1)S(1)}, u32[]{:S(2)}, u32[]{:S(2)}) collective-permute-start(bf16[4,48,1536]{2,1,0:T(8,128)(2,1)S(1)} %get-tuple-element.249), channel_id=1, source_target_pairs={{0,4},{2,6},{4,0},{6,2},{8,12},{10,14},{12,8},{14,10},{16,20},{18,... | collective-permute-start | bytes 1769480 | tf_op jit(solution)/shard_map/ppermute | solution.py:22
  106.9 20.7 %collective-permute-start.31 = (bf16[2,48,1536]{2,1,0:T(8,128)(2,1)S(1)}, bf16[2,48,1536]{2,1,0:T(8,128)(2,1)S(1)}, u32[]{:S(2)}, u32[]{:S(2)}) collective-permute-start(bf16[2,48,1536]{2,1,0:T(8,128)(2,1)S(1)} %get-tuple-element.254), channel_id=1, source_target_pairs={{0,2},{2,0},{4,6},{6,4},{8,10},{10,8},{12,14},{14,12},{16,18},{18,... | collective-permute-start | bytes 884744 | tf_op jit(solution)/shard_map/ppermute | solution.py:22
  108.1 20.2 %collective-permute-start.32 = (bf16[2,48,1536]{2,1,0:T(8,128)(2,1)S(1)}, bf16[2,48,1536]{2,1,0:T(8,128)(2,1)S(1)}, u32[]{:S(2)}, u32[]{:S(2)}) collective-permute-start(bf16[2,48,1536]{2,1,0:T(8,128)(2,1)S(1)} %get-tuple-element.255), channel_id=1, source_target_pairs={{0,4},{2,6},{4,0},{6,2},{8,12},{10,14},{12,8},{14,10},{16,20},{18,... | collective-permute-start | bytes 884744 | tf_op jit(solution)/shard_map/ppermute | solution.py:22
  137.9 16.8 %collective-permute-start.38 = (bf16[4,48,1664]{2,1,0:T(8,128)(2,1)S(1)}, bf16[4,48,1664]{2,1,0:T(8,128)(2,1)S(1)}, u32[]{:S(2)}, u32[]{:S(2)}) collective-permute-start(bf16[4,48,1664]{2,1,0:T(8,128)(2,1)S(1)} %get-tuple-element.291), channel_id=1, source_target_pairs={{0,2},{2,0},{4,6},{6,4},{8,10},{10,8},{12,14},{14,12},{16,18},{18,... | collective-permute-start | bytes 1916936 | tf_op jit(solution)/shard_map/ppermute | solution.py:22
  138.9 15.8 %collective-permute-start.39 = (bf16[4,48,1536]{2,1,0:T(8,128)(2,1)S(1)}, bf16[4,48,1536]{2,1,0:T(8,128)(2,1)S(1)}, u32[]{:S(2)}, u32[]{:S(2)}) collective-permute-start(bf16[4,48,1536]{2,1,0:T(8,128)(2,1)S(1)} %get-tuple-element.292), channel_id=1, source_target_pairs={{0,4},{2,6},{4,0},{6,2},{8,12},{10,14},{12,8},{14,10},{16,20},{18,... | collective-permute-start | bytes 1769480 | tf_op jit(solution)/shard_map/ppermute | solution.py:22
  140.6 14.1 %collective-permute-start.40 = (bf16[2,48,1536]{2,1,0:T(8,128)(2,1)S(1)}, bf16[2,48,1536]{2,1,0:T(8,128)(2,1)S(1)}, u32[]{:S(2)}, u32[]{:S(2)}) collective-permute-start(bf16[2,48,1536]{2,1,0:T(8,128)(2,1)S(1)} %get-tuple-element.293), channel_id=1, source_target_pairs={{0,8},{2,10},{4,12},{6,14},{8,0},{10,2},{12,4},{14,6},{16,24},{18,... | collective-permute-start | bytes 884744 | tf_op jit(solution)/shard_map/ppermute | solution.py:22
  141.3 13.3 %collective-permute-start.41 = (bf16[48,1536]{1,0:T(8,128)(2,1)S(1)}, bf16[48,1536]{1,0:T(8,128)(2,1)S(1)}, u32[]{:S(2)}, u32[]{:S(2)}) collective-permute-start(bf16[48,1536]{1,0:T(8,128)(2,1)S(1)} %get-tuple-element.296), channel_id=1, source_target_pairs={{0,24},{2,26},{4,28},{6,30},{8,16},{10,18},{12,20},{14,22},{16,8},... | collective-permute-start | bytes 442376 | tf_op jit(solution)/shard_map/ppermute | solution.py:22
  154.8 10.1 %collective-permute-start.44 = (bf16[2,48,1664]{2,1,0:T(8,128)(2,1)S(1)}, bf16[2,48,1664]{2,1,0:T(8,128)(2,1)S(1)}, u32[]{:S(2)}, u32[]{:S(2)}) collective-permute-start(bf16[2,48,1664]{2,1,0:T(8,128)(2,1)S(1)} %get-tuple-element.311), channel_id=1, source_target_pairs={{0,4},{2,6},{4,0},{6,2},{8,12},{10,14},{12,8},{14,10},{16,20},{18,... | collective-permute-start | bytes 958472 | tf_op jit(solution)/shard_map/ppermute | solution.py:22
  (35 other events, 276.9 us)
